TPU v7x, 32 devices: a whole 2x2x4 slice. The times are simulated.
32 devices in a mesh: len: 8 (over y, x, core), wid: 4 (over z).
Axes of the slice: x: 2, y: 2, z: 4, core: 2. Of those that a mesh axis runs over, the one named last changes fastest.
Arguments:
- prior_heat_level: float32 [32, 1024, 1024], P(None, 'wid', 'len'), may hold values from -6 to 6
- spanwise_diffusivity_number: float32 [32, 1024], P(None, 'len'), may hold values from 30 to 8000
- planar_speed_vector: float32 [2, 32, 1024, 1024], P(None, None, 'wid', 'len'), may hold values from -4 to 4
- driving_load_vector: float32 [2, 32, 1024, 1024], P(None, None, 'wid', 'len'), may hold values from -6 to 6
- pinned_indicator: int32 [32, 1024, 1024], P(None, 'wid', 'len'), may hold values 0 or 1
Outputs:
- heated: float32 [32, 1024, 1024], P(None, 'wid', 'len')
- flow: float32 [2, 32, 1024, 1024], P(None, None, 'wid', 'len')
All inputs are finite; a program needn't handle non-finite values. No bound on the sum of `pinned_indicator` on one device may be relied on, other than what follows from the above.
Results may differ from a plain program's by a relative error of at most 0.0008.
Values sent between devices are 32-bit elements; how exact they have to be, the bound alone decides.
No kernel may reach another device: no remote copies, remote signals or barrier semaphores. Data moves between devices by JAX's collectives and lax.ppermute only.
A program may use at most 192 MiB of HBM per device.

v0:
```python
import functools

import jax
import jax.numpy as jnp
from jax import lax
from jax.experimental import pallas as pl
from jax.experimental.pallas import tpu as pltpu
from jax.sharding import PartitionSpec as P

DRAG_COEFF = 0.5
RELAX_FACTOR = 0.8
F32 = jnp.float32
MIB = 1 << 20


def decay(d):
    x = 1.0 / d
    one_less = jnp.sqrt(x + 0.25 * x * x) - 0.5 * x
    r = 1.0 - one_less
    return r, (1.0 - r) / (1.0 + r)


def power(r, n):
    out = None
    while n:
        if n & 1:
            out = r if out is None else out * r
        n >>= 1
        if n:
            r = r * r
    return out


def sublane_powers(r, shape):
    s = lax.broadcasted_iota(jnp.int32, shape, 0)
    r2 = r * r
    r4 = r2 * r2
    one = jnp.ones(shape, F32)
    return (
        jnp.where((s & 1) != 0, r, one)
        * jnp.where((s & 2) != 0, r2, one)
        * jnp.where((s & 4) != 0, r4, one)
    )


def iotas():
    lane = lax.broadcasted_iota(jnp.int32, (8, 128), 1)
    sub = lax.broadcasted_iota(jnp.int32, (8, 128), 0)
    return lane, sub


def moments_kernel(tb, n, d_ref, f_ref, seg_ref, pq_ref):
    S = n // 8
    base = pl.program_id(0) * tb
    G = 4
    for g in range(tb // G):
        rs = []
        for u in range(G):
            r, _ = decay(d_ref[pl.ds(base + g * G + u, 1), :])
            rs.append(jnp.broadcast_to(r, (8, 128)))
        fwd = [None] * G
        bwd = [None] * G
        for i in range(S):
            for u in range(G):
                a = f_ref[g * G + u, pl.ds(i, 8, stride=S), :]
                b = f_ref[g * G + u, pl.ds(S - 1 - i, 8, stride=S), :]
                fwd[u] = a if i == 0 else fwd[u] * rs[u] + a
                bwd[u] = b if i == 0 else bwd[u] * rs[u] + b
        for u in range(G):
            k = g * G + u
            seg_ref[0, k] = fwd[u]
            seg_ref[1, k] = bwd[u]
            rS = power(rs[u], S)
            up = sublane_powers(rS, (8, 128))
            s = lax.broadcasted_iota(jnp.int32, (8, 128), 0)
            rS2 = rS * rS
            one = jnp.ones((8, 128), F32)
            down = (
                jnp.where((s & 1) == 0, rS, one)
                * jnp.where((s & 2) == 0, rS2, one)
                * jnp.where((s & 4) == 0, rS2 * rS2, one)
            )
            pq_ref[0, k : k + 1, :] = jnp.sum(fwd[u] * down, axis=0, keepdims=True)
            pq_ref[1, k : k + 1, :] = jnp.sum(bwd[u] * up, axis=0, keepdims=True)


def moments(d, prior):
    T, n, _ = prior.shape
    tb = 8
    return pl.pallas_call(
        functools.partial(moments_kernel, tb, n),
        grid=(T // tb,),
        in_specs=[
            pl.BlockSpec((T, 128), lambda t: (0, 0)),
            pl.BlockSpec((tb, n, 128), lambda t: (t, 0, 0)),
        ],
        out_specs=[
            pl.BlockSpec((2, tb, 8, 128), lambda t: (0, t, 0, 0)),
            pl.BlockSpec((2, tb, 128), lambda t: (0, t, 0)),
        ],
        out_shape=[
            jax.ShapeDtypeStruct((2, T, 8, 128), F32),
            jax.ShapeDtypeStruct((2, T, 128), F32),
        ],
        compiler_params=pltpu.CompilerParams(vmem_limit_bytes=16 * MIB),
        cost_estimate=pl.CostEstimate(flops=4 * T * n * 128, bytes_accessed=4 * T * n * 128, transcendentals=0),
        name="moments",
    )(d, prior)


def pack_kernel(tb, n, v_ref, f_ref, p_ref, pk_ref, lo_ref, hi_ref):
    base = pl.program_id(0) * tb
    lane = lax.broadcasted_iota(jnp.int32, (n, 128), 1)
    group = lane >> 2
    for k in range(5):
        acc = pk_ref[k]
        for u in range(tb):
            if k < 2:
                x = v_ref[k, u]
            elif k < 4:
                x = f_ref[k - 2, u]
            else:
                x = 1.0 - p_ref[u].astype(F32)
            t = base + u
            acc = jnp.where(group == t, pltpu.roll(x, (4 * t + 2) & 127, 1), acc)
        pk_ref[k] = acc
    for u in range(tb):
        for ref, a, e in ((lo_ref, 0, 0), (hi_ref, n - 2, n - 1)):
            ref[u, 0:2, :] = v_ref[0, u, a : a + 2, :]
            ref[u, 2:4, :] = v_ref[1, u, a : a + 2, :]
            ref[u, 4:5, :] = f_ref[0, u, e : e + 1, :]
            ref[u, 5:6, :] = f_ref[1, u, e : e + 1, :]
            ref[u, 6:7, :] = 1.0 - p_ref[u, e : e + 1, :].astype(F32)
            ref[u, 7:8, :] = jnp.zeros((1, 128), F32)


def pack(v, f, pinned):
    _, T, n, _ = v.shape
    tb = 4
    row = jax.ShapeDtypeStruct((T, 8, 128), F32)
    return pl.pallas_call(
        functools.partial(pack_kernel, tb, n),
        grid=(T // tb,),
        in_specs=[
            pl.BlockSpec((2, tb, n, 128), lambda t: (0, t, 0, 0)),
            pl.BlockSpec((2, tb, n, 128), lambda t: (0, t, 0, 0)),
            pl.BlockSpec((tb, n, 128), lambda t: (t, 0, 0)),
        ],
        out_specs=[
            pl.BlockSpec((5, n, 128), lambda t: (0, 0, 0)),
            pl.BlockSpec((tb, 8, 128), lambda t: (t, 0, 0)),
            pl.BlockSpec((tb, 8, 128), lambda t: (t, 0, 0)),
        ],
        out_shape=[jax.ShapeDtypeStruct((5, n, 128), F32), row, row],
        compiler_params=pltpu.CompilerParams(vmem_limit_bytes=24 * MIB),
        cost_estimate=pl.CostEstimate(flops=5 * T * n * 128, bytes_accessed=20 * T * n * 128, transcendentals=0),
        name="pack_edges",
    )(v, f, pinned)


def heat_kernel(
    J, tb, n, d_ref, all_ref, seg_ref, f_ref, pk_ref, lo7_ref, hi7_ref,
    out_ref, right_ref, left_ref, lo_ref, hi_ref, sums, pkh, ys,
):
    S = n // 8
    T = d_ref.shape[0]
    step = pl.program_id(0)
    base = step * tb

    @pl.when(step == 0)
    def _():
        j = lax.axis_index("wid")
        r, _ = decay(d_ref[...])
        rn = power(r, n)
        rN = power(rn, J)
        sp = all_ref[0, 0]
        for i in range(1, J):
            sp = sp * rn + all_ref[i, 0]
        sq = all_ref[J - 1, 1]
        for i in range(J - 2, -1, -1):
            sq = sq * rn + all_ref[i, 1]
        inv = 1.0 / (1.0 - rN * rN)
        left = (sq + rN * sp) * inv
        right = (sp + rN * sq) * inv
        for i in range(J - 1):
            left = jnp.where(i < j, rn * left + all_ref[i, 0], left)
        for i in range(J - 1, 0, -1):
            right = jnp.where(i > j, rn * right + all_ref[i, 1], right)
        sums[0] = left
        sums[1] = right

    _, sub = iotas()
    rs, gain, y, z = [], [], [], []
    for u in range(tb):
        t = base + u
        r, a0 = decay(d_ref[pl.ds(t, 1), :])
        r = jnp.broadcast_to(r, (8, 128))
        a0 = jnp.broadcast_to(a0, (8, 128))
        rS = power(r, S)
        rS2 = rS * rS
        rS4 = rS2 * rS2
        c = jnp.where(sub == 0, sums[0, pl.ds(t, 1), :], pltpu.roll(seg_ref[0, u], 1, 0))
        b = jnp.where(sub == 7, sums[1, pl.ds(t, 1), :], pltpu.roll(seg_ref[1, u], 7, 0))
        for s, q in ((1, rS), (2, rS2), (4, rS4)):
            c = c + q * jnp.where(sub >= s, pltpu.roll(c, s, 0), 0.0)
            b = b + q * jnp.where(sub < 8 - s, pltpu.roll(b, 8 - s, 0), 0.0)
        rs.append(r)
        gain.append(a0)
        y.append(c)
        z.append(b)
    for i in range(S):
        for u in range(tb):
            y[u] = y[u] * rs[u] + f_ref[u, pl.ds(i, 8, stride=S), :]
            ys[u, i] = y[u]
    for i in range(S - 1, -1, -1):
        for u in range(tb):
            zr = z[u] * rs[u]
            out_ref[u, pl.ds(i, 8, stride=S), :] = gain[u] * (ys[u, i] + zr)
            z[u] = zr + f_ref[u, pl.ds(i, 8, stride=S), :]

    lane_n = lax.broadcasted_iota(jnp.int32, (n, 128), 1)
    group = lane_n >> 2
    acc = pkh[...]
    for u in range(tb):
        t = base + u
        acc = jnp.where(group == t, pltpu.roll(out_ref[u], (4 * t + 2) & 127, 1), acc)
    pkh[...] = acc
    for u in range(tb):
        lo_ref[u] = jnp.where(sub == 7, out_ref[u, 0:1, :], lo7_ref[u])
        hi_ref[u] = jnp.where(sub == 7, out_ref[u, n - 1 : n, :], hi7_ref[u])

    @pl.when(step == pl.num_programs(0) - 1)
    def _():
        slot = lane_n & 3
        v0, v1, f0, f1, fr, he = pk_ref[0], pk_ref[1], pk_ref[2], pk_ref[3], pk_ref[4], pkh[...]

        def sel(a, b, c, d):
            return jnp.where(slot < 2, jnp.where(slot == 0, a, b), jnp.where(slot == 2, c, d))

        right_ref[0] = jnp.where(slot < 2, v0, pltpu.roll(v1, 2, 1))
        left_ref[0] = jnp.where(slot >= 2, v0, pltpu.roll(v1, 126, 1))
        right_ref[1] = sel(pltpu.roll(f0, 127, 1), f1, pltpu.roll(fr, 1, 1), pltpu.roll(he, 2, 1))
        left_ref[1] = sel(pltpu.roll(f0, 126, 1), pltpu.roll(f1, 127, 1), fr, pltpu.roll(he, 1, 1))


def heat(d, gathered, seg, prior, pk, lo7, hi7):
    T, n, _ = prior.shape
    J = gathered.shape[0]
    tb = 4
    row = jax.ShapeDtypeStruct((T + 1, 8, 128), F32)
    return pl.pallas_call(
        functools.partial(heat_kernel, J, tb, n),
        grid=(T // tb,),
        in_specs=[
            pl.BlockSpec((T, 128), lambda t: (0, 0)),
            pl.BlockSpec((J, 2, T, 128), lambda t: (0, 0, 0, 0)),
            pl.BlockSpec((2, tb, 8, 128), lambda t: (0, t, 0, 0)),
            pl.BlockSpec((tb, n, 128), lambda t: (t, 0, 0)),
            pl.BlockSpec((5, n, 128), lambda t: (0, 0, 0)),
            pl.BlockSpec((tb, 8, 128), lambda t: (t, 0, 0)),
            pl.BlockSpec((tb, 8, 128), lambda t: (t, 0, 0)),
        ],
        out_specs=[
            pl.BlockSpec((tb, n, 128), lambda t: (t, 0, 0)),
            pl.BlockSpec((2, n, 128), lambda t: (0, 0, 0)),
            pl.BlockSpec((2, n, 128), lambda t: (0, 0, 0)),
            pl.BlockSpec((tb, 8, 128), lambda t: (t, 0, 0)),
            pl.BlockSpec((tb, 8, 128), lambda t: (t, 0, 0)),
        ],
        out_shape=[
            jax.ShapeDtypeStruct((T, n, 128), F32),
            jax.ShapeDtypeStruct((2, n, 128), F32),
            jax.ShapeDtypeStruct((2, n, 128), F32),
            row,
            row,
        ],
        scratch_shapes=[
            pltpu.VMEM((2, T, 128), F32),
            pltpu.VMEM((n, 128), F32),
            pltpu.VMEM((tb, n // 8, 8, 128), F32),
        ],
        compiler_params=pltpu.CompilerParams(vmem_limit_bytes=24 * MIB),
        cost_estimate=pl.CostEstimate(flops=10 * T * n * 128, bytes_accessed=8 * T * n * 128, transcendentals=0),
        name="heat",
    )(d, gathered, seg, prior, pk, lo7, hi7)


def corner_kernel(n, fl_ref, fr_ref, lo_in, hi_in, r_ref, lo_ref, hi_ref):
    slot = lax.broadcasted_iota(jnp.int32, (n, 128), 1) & 3
    al, ar, bl, br = fl_ref[0], fr_ref[0], fl_ref[1], fr_ref[1]
    low = slot < 2
    r_ref[0] = jnp.where(low, al, ar)
    r_ref[1] = jnp.where(low, pltpu.roll(al, 126, 1), pltpu.roll(ar, 2, 1))
    for k in range(4):
        a = bl if k == 1 else pltpu.roll(bl, (1 - k) & 127, 1)
        b = br if k == 2 else pltpu.roll(br, (2 - k) & 127, 1)
        r_ref[2 + k] = jnp.where(low, a, b)
    for ref, a, e in ((lo_ref, 0, 0), (hi_ref, n - 2, n - 1)):
        ref[0, 0:2, :] = r_ref[0, a : a + 2, :]
        ref[0, 2:4, :] = r_ref[1, a : a + 2, :]
        for k in range(4):
            ref[0, 4 + k : 5 + k, :] = r_ref[2 + k, e : e + 1, :]


def corners(from_left, from_right, lo, hi):
    _, n, _ = from_left.shape
    T = lo.shape[0] - 1
    row = jax.ShapeDtypeStruct(lo.shape, F32)
    return pl.pallas_call(
        functools.partial(corner_kernel, n),
        grid=(1,),
        in_specs=[
            pl.BlockSpec((2, n, 128), lambda g: (0, 0, 0)),
            pl.BlockSpec((2, n, 128), lambda g: (0, 0, 0)),
            pl.BlockSpec(memory_space=pl.ANY),
            pl.BlockSpec(memory_space=pl.ANY),
        ],
        out_specs=[
            pl.BlockSpec((6, n, 128), lambda g: (0, 0, 0)),
            pl.BlockSpec((1, 8, 128), lambda g: (T, 0, 0)),
            pl.BlockSpec((1, 8, 128), lambda g: (T, 0, 0)),
        ],
        out_shape=[jax.ShapeDtypeStruct((6, n, 128), F32), row, row],
        input_output_aliases={2: 1, 3: 2},
        compiler_params=pltpu.CompilerParams(vmem_limit_bytes=16 * MIB),
        cost_estimate=pl.CostEstimate(flops=0, bytes_accessed=40 * n * 128, transcendentals=0),
        name="corners",
    )(from_left, from_right, lo, hi)


def coefficients(f0, f1, free, heated):
    v = jnp.exp(-0.5 * heated)
    w = RELAX_FACTOR * free
    a = w / (DRAG_COEFF + 4.0 * v)
    return 1.0 - w, a * v, a * f0, a * f1


def sweep_kernel(
    tb, n, v_ref, f_ref, p_ref, h_ref, lo_ref, hi_ref, r_ref, own_ref,
    out_ref, yh1, yh2, v1s, cos, r1s,
):
    S = n // 8
    T = lo_ref.shape[0] - 1
    step = pl.program_id(0)
    lane, sub = iotas()
    slot = lane & 3
    first, last = lane == 0, lane == 127

    def ext(load, lo_row, hi_row, i):
        if i < 0:
            return jnp.where(sub == 0, lo_row(i), pltpu.roll(load(S + i), 1, 0))
        if i >= S:
            return jnp.where(sub == 7, hi_row(i - S), pltpu.roll(load(i - S), 7, 0))
        return load(i)

    @pl.when(step == 0)
    def _():
        own_lo = jnp.zeros((8, 128), F32)
        own_hi = jnp.zeros((8, 128), F32)
        for t in range(T):
            own_lo = jnp.where(lane >> 2 == t, pltpu.roll(lo_ref[t], (4 * t + 2) & 127, 1), own_lo)
            own_hi = jnp.where(lane >> 2 == t, pltpu.roll(hi_ref[t], (4 * t + 2) & 127, 1), own_hi)
        outer = (slot == 0) | (slot == 3)
        sign = jnp.where(slot == 1, -0.25, 0.25)

        def r_at(c, i):
            return ext(
                lambda q: r_ref[c, pl.ds(q, 8, stride=S), :],
                lambda q: lo_ref[T, 2 * c + 2 + q : 2 * c + 3 + q, :],
                lambda q: hi_ref[T, 2 * c + q : 2 * c + 1 + q, :],
                i,
            )

        def o_at(c, i):
            return ext(
                lambda q: own_ref[c, pl.ds(q, 8, stride=S), :],
                lambda q: own_lo[2 * c + 2 + q : 2 * c + 3 + q, :],
                lambda q: own_hi[2 * c + q : 2 * c + 1 + q, :],
                i,
            )

        def e_at(k, i):
            return ext(
                lambda q: r_ref[k, pl.ds(q, 8, stride=S), :],
                lambda q: lo_ref[T, 2 + k : 3 + k, :],
                lambda q: hi_ref[T, 2 + k : 3 + k, :],
                i,
            )

        def both(i):
            r = [r_at(c, i) for c in range(2)]
            w = [jnp.where(outer, r[c], o_at(c, i)) for c in range(2)]
            return r, w

        prev, here = both(-2), both(-1)
        for i in range(-1, S + 1):
            after = both(i + 1)
            k, g, a0, a1 = coefficients(e_at(2, i), e_at(3, i), e_at(4, i), e_at(5, i))
            dr = [after[0][c] - prev[0][c] for c in range(2)]
            qw = [0.25 * (after[1][c] - prev[1][c]) for c in range(2)]
            for c in range(2):
                yh1[c, i + 1] = here[0][c] + sign * dr[1 - c]
                around = (
                    prev[0][c]
                    + after[0][c]
                    + pltpu.roll(here[1][c] + qw[1 - c], 127, 1)
                    + pltpu.roll(here[1][c] - qw[1 - c], 1, 1)
                )
                r1s[c, i + 1] = k * here[0][c] + (a0, a1)[c] + g * around
            prev, here = here, after
        for i in range(S):
            for c in range(2):
                yh2[c, i] = r1s[c, i + 1] + sign * (r1s[1 - c, i + 2] - r1s[1 - c, i])

    def layer(u, _):
        t = step * tb + u
        shift = (126 - 4 * t) & 127

        def update(prev, here, after, k, g, a, yh):
            q = [0.25 * (after[c] - prev[c]) for c in range(2)]
            new = []
            for c in range(2):
                edge = pltpu.roll(yh[c], shift, 1)
                up = jnp.where(first, edge, here[c] + q[1 - c])
                down = jnp.where(last, edge, here[c] - q[1 - c])
                around = prev[c] + after[c] + (pltpu.roll(up, 127, 1) + pltpu.roll(down, 1, 1))
                new.append(k * here[c] + a[c] + g * around)
            return new

        def at(i):
            return [
                ext(
                    lambda q: v_ref[c, u, pl.ds(q, 8, stride=S), :],
                    lambda q: lo_ref[t, 2 * c + 2 + q : 2 * c + 3 + q, :],
                    lambda q: hi_ref[t, 2 * c + q : 2 * c + 1 + q, :],
                    i,
                )
                for c in range(2)
            ]

        def edge_of(k, load, i):
            return ext(load, lambda q: lo_ref[t, k : k + 1, :], lambda q: hi_ref[t, k : k + 1, :], i)

        prev, here = at(-2), at(-1)
        for i in range(-1, S + 1):
            after = at(i + 1)
            co = coefficients(
                edge_of(4, lambda q: f_ref[0, u, pl.ds(q, 8, stride=S), :], i),
                edge_of(5, lambda q: f_ref[1, u, pl.ds(q, 8, stride=S), :], i),
                edge_of(6, lambda q: 1.0 - p_ref[u, pl.ds(q, 8, stride=S), :].astype(F32), i),
                edge_of(7, lambda q: h_ref[u, pl.ds(q, 8, stride=S), :], i),
            )
            if 0 <= i < S:
                for m in range(4):
                    cos[m, i] = co[m]
            new = update(prev, here, after, co[0], co[1], co[2:], [yh1[c, i + 1] for c in range(2)])
            for c in range(2):
                v1s[c, i + 1] = new[c]
            prev, here = here, after
        for i in range(S):
            new = update(
                [v1s[c, i] for c in range(2)],
                [v1s[c, i + 1] for c in range(2)],
                [v1s[c, i + 2] for c in range(2)],
                cos[0, i],
                cos[1, i],
                [cos[2, i], cos[3, i]],
                [yh2[c, i] for c in range(2)],
            )
            for c in range(2):
                out_ref[c, u, pl.ds(i, 8, stride=S), :] = new[c]
        return 0

    lax.fori_loop(0, tb, layer, 0)


def sweeps(v, f, pinned, heated, lo, hi, r, pk):
    _, T, n, _ = v.shape
    S = n // 8
    tb = 2
    return pl.pallas_call(
        functools.partial(sweep_kernel, tb, n),
        grid=(T // tb,),
        in_specs=[
            pl.BlockSpec((2, tb, n, 128), lambda t: (0, t, 0, 0)),
            pl.BlockSpec((2, tb, n, 128), lambda t: (0, t, 0, 0)),
            pl.BlockSpec((tb, n, 128), lambda t: (t, 0, 0)),
            pl.BlockSpec((tb, n, 128), lambda t: (t, 0, 0)),
            pl.BlockSpec((T + 1, 8, 128), lambda t: (0, 0, 0)),
            pl.BlockSpec((T + 1, 8, 128), lambda t: (0, 0, 0)),
            pl.BlockSpec((6, n, 128), lambda t: (0, 0, 0)),
            pl.BlockSpec((2, n, 128), lambda t: (0, 0, 0)),
        ],
        out_specs=pl.BlockSpec((2, tb, n, 128), lambda t: (0, t, 0, 0)),
        out_shape=jax.ShapeDtypeStruct((2, T, n, 128), F32),
        scratch_shapes=[
            pltpu.VMEM((2, S + 2, 8, 128), F32),
            pltpu.VMEM((2, S, 8, 128), F32),
            pltpu.VMEM((2, S + 2, 8, 128), F32),
            pltpu.VMEM((4, S, 8, 128), F32),
            pltpu.VMEM((2, S + 2, 8, 128), F32),
        ],
        compiler_params=pltpu.CompilerParams(vmem_limit_bytes=32 * MIB),
        cost_estimate=pl.CostEstimate(flops=60 * T * n * 128, bytes_accessed=32 * T * n * 128, transcendentals=T * n * 128),
        name="sweeps",
    )(v, f, pinned, heated, lo, hi, r, pk)


def shifted(up_going, down_going, axis):
    count = lax.axis_size(axis)
    up = [(i, i + 1) for i in range(count - 1)]
    down = [(j, i) for i, j in up]
    return lax.ppermute(up_going, axis, up), lax.ppermute(down_going, axis, down)


def local(prior, d, v, f, pinned):
    seg, pq = moments(d, prior)
    gathered = lax.all_gather(pq, "wid")
    pk, lo7, hi7 = pack(v, f, pinned)
    heated, right, left, lo, hi = heat(d, gathered, seg, prior, pk, lo7, hi7)
    from_left, from_right = shifted(right, left, "len")
    r, lo, hi = corners(from_left, from_right, lo, hi)
    from_below, from_above = shifted(hi, lo, "wid")
    flow = sweeps(v, f, pinned, heated, from_below, from_above, r, pk)
    return heated, flow


def solution(mesh):
    in_specs = (
        P(None, "wid", "len"),
        P(None, "len"),
        P(None, None, "wid", "len"),
        P(None, None, "wid", "len"),
        P(None, "wid", "len"),
    )
    out_specs = (P(None, "wid", "len"), P(None, None, "wid", "len"))
    return jax.shard_map(local, mesh=mesh, in_specs=in_specs, out_specs=out_specs, check_vma=False)
```

profile of v0, /device:TPU:4, one launch (start us, length us, event | category | flops | bytes accessed | tf_op | source)
XLA Modules:
  0.0 277.2 jit_solution(1648878459325670855)
XLA Ops:
  0.6 0.0 copy-start.4
  0.6 2.2 copy-done.4
  2.8 0.0 copy-start.7
  2.8 0.7 copy-done.7
  3.5 2.6 moments.1
  6.1 13.6 %all-gather = f32[8,32,128]{2,1,0:T(8,128)S(1)} all-gather(f32[2,32,128]{2,1,0:T(8,128)S(1)} %get-tuple-element.15), channel_id=2, replica_groups=mesh['len'=8,'wid'=4] {'wid'}, dimensions={0}, use_global_device_ids=true | all-gather | bytes 163840 | tf_op jit(solution)/shard_map/all_gather | solution.py:518
  19.7 0.0 copy-start
  19.7 3.4 %copy-done = f32[2,32,256,128]{3,2,1,0:T(8,128)S(1)} copy-done((f32[2,32,256,128]{3,2,1,0:T(8,128)S(1)}, f32[2,32,256,128]{3,2,1,0:T(8,128)}, u32[]{:S(2)}) %copy-start) | copy-done | bytes 8388632
  23.1 0.0 copy-start.2
  23.1 3.4 %copy-done.2 = f32[2,32,256,128]{3,2,1,0:T(8,128)S(1)} copy-done((f32[2,32,256,128]{3,2,1,0:T(8,128)S(1)}, f32[2,32,256,128]{3,2,1,0:T(8,128)}, u32[]{:S(2)}) %copy-start.2) | copy-done | bytes 8388632
  26.5 0.0 copy-start.3
  26.5 2.2 copy-done.3
  28.7 0.0 copy-start.5
  28.7 0.0 copy-start.8
  28.7 0.0 copy-start.1
  28.7 7.3 %pack_edges.1 = (f32[5,256,128]{2,1,0:T(8,128)S(1)}, f32[32,8,128]{2,1,0:T(8,128)S(1)}, f32[32,8,128]{2,1,0:T(8,128)S(1)}) custom-call(f32[2,32,256,128]{3,2,1,0:T(8,128)S(1)} %copy-done, f32[2,32,256,128]{3,2,1,0:T(8,128)S(1)} %copy-done.2, s32[32,256,128]{2,1,0:T(8,128)S(1)} %copy-done.3), custom_call_target="tpu_custom_call" | custom-call | flops 5242880 | bytes 20971520 | tf_op jit(solution)/shard_map/pack_edges/pallas_call | solution.py:141
  36.0 0.0 copy-done.5
  36.0 0.0 copy-done.8
  36.1 9.0 %heat.1 = (f32[32,256,128]{2,1,0:T(8,128)}, f32[2,256,128]{2,1,0:T(8,128)S(1)}, f32[2,256,128]{2,1,0:T(8,128)S(1)}, f32[33,8,128]{2,1,0:T(8,128)S(1)}, f32[33,8,128]{2,1,0:T(8,128)S(1)}) custom-call(f32[32,128]{1,0:T(8,128)S(1)} %copy-done.8, f32[4,2,32,128]{3,2,1,0:T(8,128)S(1)} %bitcast.1, f32[2,32,8,128]{3,2,1,0:T(8,128)S(1)} %get-tuple-element.16.seg_ref, ...), custom_call_target="tpu_custom_call" | custom-call | flops 10485760 | bytes 8388608 | tf_op jit(solution)/shard_map/heat/pallas_call | solution.py:251
  45.0 1.9 collective-permute-start
  47.0 4.5 %collective-permute-start.1 = (f32[2,256,128]{2,1,0:T(8,128)S(1)}, f32[2,256,128]{2,1,0:T(8,128)S(1)}, u32[]{:S(2)}, u32[]{:S(2)}) collective-permute-start(f32[2,256,128]{2,1,0:T(8,128)S(1)} %get-tuple-element.22), channel_id=1, source_target_pairs={{4,0},{8,4},{12,8},{16,12},{20,16},{24,20},{28,24},{5,1},{9,5},{13... | collective-permute-start | bytes 786440 | tf_op jit(solution)/shard_map/ppermute | solution.py:513
  51.5 2.1 collective-permute-done.fl_ref
  53.6 1.8 collective-permute-done.1.fr_ref
  55.4 0.3 corners.1
  55.7 3.8 %collective-permute-start.2 = (f32[33,8,128]{2,1,0:T(8,128)S(1)}, f32[33,8,128]{2,1,0:T(8,128)S(1)}, u32[]{:S(2)}, u32[]{:S(2)}) collective-permute-start(f32[33,8,128]{2,1,0:T(8,128)S(1)} %get-tuple-element.25), channel_id=1, source_target_pairs={{0,1},{1,2},{2,3},{4,5},{5,6},{6,7},{8,9},{9,10},{10,11},{12,13},{... | collective-permute-start | bytes 405512 | tf_op jit(solution)/shard_map/ppermute | solution.py:513
  59.5 1.3 collective-permute-start.3
  60.8 2.6 collective-permute-done.2.lo_ref
  63.4 4.1 %collective-permute-done.3.hi_ref = f32[33,8,128]{2,1,0:T(8,128)S(1)} collective-permute-done((f32[33,8,128]{2,1,0:T(8,128)S(1)}, f32[33,8,128]{2,1,0:T(8,128)S(1)}, u32[]{:S(2)}, u32[]{:S(2)}) %collective-permute-start.3) | collective-permute-done | bytes 135200 | tf_op jit(solution)/shard_map/ppermute | solution.py:513
  67.5 0.0 copy-done.1
  67.5 0.0 copy-start.6
  67.5 2.2 copy-done.6
  69.7 207.5 %sweeps.1 = f32[2,32,256,128]{3,2,1,0:T(8,128)} custom-call(f32[2,32,256,128]{3,2,1,0:T(8,128)S(1)} %copy-done.1, f32[2,32,256,128]{3,2,1,0:T(8,128)} %f_ref.7, s32[32,256,128]{2,1,0:T(8,128)S(1)} %copy-done.3, f32[32,256,128]{2,1,0:T(8,128)S(1)} %copy-done.6, f32[33,8,128]{2,1,0:T(8,128)S(1)} %collective-permute-done.2.lo_ref, ...), custom_call_target="tpu_custom_call" | custom-call | flops 62914560 | bytes 33554432 | tf_op jit(solution)/shard_map/sweeps/pallas_call | solution.py:481
Async XLA Ops:
  0.6 2.2 copy-start.4
  2.8 0.7 copy-start.7
  19.7 3.4 %copy-start = (f32[2,32,256,128]{3,2,1,0:T(8,128)S(1)}, f32[2,32,256,128]{3,2,1,0:T(8,128)}, u32[]{:S(2)}) copy-start(f32[2,32,256,128]{3,2,1,0:T(8,128)} %v_ref.3) | copy-start | bytes 25165828
  23.1 3.4 %copy-start.2 = (f32[2,32,256,128]{3,2,1,0:T(8,128)S(1)}, f32[2,32,256,128]{3,2,1,0:T(8,128)}, u32[]{:S(2)}) copy-start(f32[2,32,256,128]{3,2,1,0:T(8,128)} %f_ref.7) | copy-start | bytes 25165828
  26.5 2.2 copy-start.3
  28.7 7.4 %copy-start.5 = (f32[32,256,128]{2,1,0:T(8,128)S(1)}, f32[32,256,128]{2,1,0:T(8,128)}, u32[]{:S(2)}) copy-start(f32[32,256,128]{2,1,0:T(8,128)} %f_ref.6) | copy-start | bytes 12582916
  28.7 7.4 %copy-start.8 = (f32[32,128]{1,0:T(8,128)S(1)}, f32[32,128]{1,0:T(8,128)}, u32[]{:S(2)}) copy-start(f32[32,128]{1,0:T(8,128)} %d_ref.3) | copy-start | bytes 49156
  28.7 38.8 %copy-start.1 = (f32[2,32,256,128]{3,2,1,0:T(8,128)S(1)}, f32[2,32,256,128]{3,2,1,0:T(8,128)}, u32[]{:S(2)}) copy-start(f32[2,32,256,128]{3,2,1,0:T(8,128)} %v_ref.3) | copy-start | bytes 25165828
  45.0 8.6 %collective-permute-start = (f32[2,256,128]{2,1,0:T(8,128)S(1)}, f32[2,256,128]{2,1,0:T(8,128)S(1)}, u32[]{:S(2)}, u32[]{:S(2)}) collective-permute-start(f32[2,256,128]{2,1,0:T(8,128)S(1)} %get-tuple-element.21), channel_id=1, source_target_pairs={{0,4},{4,8},{8,12},{12,16},{16,20},{20,24},{24,28},{1,5},{5,9},{9,... | collective-permute-start | bytes 786440 | tf_op jit(solution)/shard_map/ppermute | solution.py:513
  47.0 8.4 %collective-permute-start.1 = (f32[2,256,128]{2,1,0:T(8,128)S(1)}, f32[2,256,128]{2,1,0:T(8,128)S(1)}, u32[]{:S(2)}, u32[]{:S(2)}) collective-permute-start(f32[2,256,128]{2,1,0:T(8,128)S(1)} %get-tuple-element.22), channel_id=1, source_target_pairs={{4,0},{8,4},{12,8},{16,12},{20,16},{24,20},{28,24},{5,1},{9,5},{13... | collective-permute-start | bytes 786440 | tf_op jit(solution)/shard_map/ppermute | solution.py:513
  55.7 7.6 %collective-permute-start.2 = (f32[33,8,128]{2,1,0:T(8,128)S(1)}, f32[33,8,128]{2,1,0:T(8,128)S(1)}, u32[]{:S(2)}, u32[]{:S(2)}) collective-permute-start(f32[33,8,128]{2,1,0:T(8,128)S(1)} %get-tuple-element.25), channel_id=1, source_target_pairs={{0,1},{1,2},{2,3},{4,5},{5,6},{6,7},{8,9},{9,10},{10,11},{12,13},{... | collective-permute-start | bytes 405512 | tf_op jit(solution)/shard_map/ppermute | solution.py:513
  59.5 8.0 %collective-permute-start.3 = (f32[33,8,128]{2,1,0:T(8,128)S(1)}, f32[33,8,128]{2,1,0:T(8,128)S(1)}, u32[]{:S(2)}, u32[]{:S(2)}) collective-permute-start(f32[33,8,128]{2,1,0:T(8,128)S(1)} %get-tuple-element.26), channel_id=1, source_target_pairs={{1,0},{2,1},{3,2},{5,4},{6,5},{7,6},{9,8},{10,9},{11,10},{13,12},{... | collective-permute-start | bytes 405512 | tf_op jit(solution)/shard_map/ppermute | solution.py:513
  67.5 2.2 copy-start.6
where the time goes:
time: 278 us; the launch traced here: 277 us
  Pallas kernels  227 us (82%)
  local copies, waits for them, and re-layouts  14 us (5%)
  blocking collectives  13.6 us (5%)
  starting transfers between devices  11.5 us (4%)
  waiting for transfers between devices  10.5 us (4%)
    pallas_call x1, Pallas kernels, sweeps(): pl.pallas_call(functools.partial(sweep_kernel, tb, n), grid=(T // tb,), i...  207 us
    unnamed x18, local copies, waits for them, and re-layouts  14 us
    all_gather x1, blocking collectives, local(): gathered = lax.all_gather(pq, 'wid')  13.6 us
    pallas_call x1, Pallas kernels, heat(): pl.pallas_call(functools.partial(heat_kernel, J, tb, n), grid=(T // tb,),...  8.99 us
    pallas_call x1, Pallas kernels, pack(): pl.pallas_call(functools.partial(pack_kernel, tb, n), grid=(T // tb,), in...  7.35 us
    ppermute x2, waiting for transfers between devices, shifted(): lax.ppermute(down_going, axis, down)  5.88 us
    ppermute x2, starting transfers between devices, shifted(): lax.ppermute(down_going, axis, down)  5.83 us
    ppermute x2, starting transfers between devices, shifted(): lax.ppermute(up_going, axis, up)  5.68 us
  transfers between devices with their start and end apart: 4, of which 4 were waited for; matrix products, arithmetic and copies ran while one was open for 0% of the time, Pallas kernels for 0%

commit v1 on v0

--- a/solution.py
+++ b/solution.py
@@ -41,6 +41,17 @@
         * jnp.where((s & 2) != 0, r2, one)
         * jnp.where((s & 4) != 0, r4, one)
     )
+
+
+def reciprocal(x):
+    y = pl.reciprocal(x, approx=True)
+    return y * (2.0 - x * y)
+
+
+def batches(lo, hi, most=11):
+    parts = -(-(hi - lo) // most)
+    cuts = [lo + (hi - lo) * k // parts for k in range(parts + 1)]
+    return [range(a, b) for a, b in zip(cuts, cuts[1:])]
 
 
 def iotas():
@@ -102,7 +113,7 @@
             jax.ShapeDtypeStruct((2, T, 8, 128), F32),
             jax.ShapeDtypeStruct((2, T, 128), F32),
         ],
-        compiler_params=pltpu.CompilerParams(vmem_limit_bytes=16 * MIB),
+        compiler_params=pltpu.CompilerParams(vmem_limit_bytes=60 * MIB),
         cost_estimate=pl.CostEstimate(flops=4 * T * n * 128, bytes_accessed=4 * T * n * 128, transcendentals=0),
         name="moments",
     )(d, prior)
@@ -124,14 +135,23 @@
             t = base + u
             acc = jnp.where(group == t, pltpu.roll(x, (4 * t + 2) & 127, 1), acc)
         pk_ref[k] = acc
+    _, sub = iotas()
+
+    def stack(v0, v1, f0, f1, fr):
+        out = jnp.where(sub < 2, v0, v1)
+        out = jnp.where(sub >= 4, f0, out)
+        out = jnp.where(sub >= 5, f1, out)
+        return jnp.where(sub >= 6, fr, out)
+
+    tiles = []
     for u in range(tb):
-        for ref, a, e in ((lo_ref, 0, 0), (hi_ref, n - 2, n - 1)):
-            ref[u, 0:2, :] = v_ref[0, u, a : a + 2, :]
-            ref[u, 2:4, :] = v_ref[1, u, a : a + 2, :]
-            ref[u, 4:5, :] = f_ref[0, u, e : e + 1, :]
-            ref[u, 5:6, :] = f_ref[1, u, e : e + 1, :]
-            ref[u, 6:7, :] = 1.0 - p_ref[u, e : e + 1, :].astype(F32)
-            ref[u, 7:8, :] = jnp.zeros((1, 128), F32)
+        for top, at, shifts in ((True, 0, (0, 2, 4, 5, 6)), (False, n - 8, (2, 4, 5, 6, 7))):
+            rows = pl.ds(at, 8)
+            raw = [v_ref[0, u, rows, :], v_ref[1, u, rows, :], f_ref[0, u, rows, :], f_ref[1, u, rows, :]]
+            raw.append(1.0 - p_ref[u, rows, :].astype(F32))
+            tiles.append((u, top, stack(*[pltpu.roll(x, q, 0) if q else x for x, q in zip(raw, shifts)])))
+    for u, top, tile in tiles:
+        (lo_ref if top else hi_ref)[u] = tile
 
 
 def pack(v, f, pinned):
@@ -152,40 +172,43 @@
             pl.BlockSpec((tb, 8, 128), lambda t: (t, 0, 0)),
         ],
         out_shape=[jax.ShapeDtypeStruct((5, n, 128), F32), row, row],
-        compiler_params=pltpu.CompilerParams(vmem_limit_bytes=24 * MIB),
+        compiler_params=pltpu.CompilerParams(vmem_limit_bytes=60 * MIB),
         cost_estimate=pl.CostEstimate(flops=5 * T * n * 128, bytes_accessed=20 * T * n * 128, transcendentals=0),
         name="pack_edges",
     )(v, f, pinned)
 
 
-def heat_kernel(
-    J, tb, n, d_ref, all_ref, seg_ref, f_ref, pk_ref, lo7_ref, hi7_ref,
-    out_ref, right_ref, left_ref, lo_ref, hi_ref, sums, pkh, ys,
-):
+def heat_kernel(J, tb, n, *refs):
+    d_ref, *pq_refs = refs[: J + 1]
+    (
+        seg_ref, f_ref, pk_ref, lo7_ref, hi7_ref,
+        out_ref, right_ref, left_ref, lo_ref, hi_ref, alls, sums, pkh, ys,
+    ) = refs[J + 1 :]
     S = n // 8
-    T = d_ref.shape[0]
     step = pl.program_id(0)
     base = step * tb
 
     @pl.when(step == 0)
     def _():
         j = lax.axis_index("wid")
+        for s in range(J):
+            alls[lax.rem(j - s + J, J)] = pq_refs[s][...]
         r, _ = decay(d_ref[...])
         rn = power(r, n)
         rN = power(rn, J)
-        sp = all_ref[0, 0]
+        sp = alls[0, 0]
         for i in range(1, J):
-            sp = sp * rn + all_ref[i, 0]
-        sq = all_ref[J - 1, 1]
+            sp = sp * rn + alls[i, 0]
+        sq = alls[J - 1, 1]
         for i in range(J - 2, -1, -1):
-            sq = sq * rn + all_ref[i, 1]
+            sq = sq * rn + alls[i, 1]
         inv = 1.0 / (1.0 - rN * rN)
         left = (sq + rN * sp) * inv
         right = (sp + rN * sq) * inv
         for i in range(J - 1):
-            left = jnp.where(i < j, rn * left + all_ref[i, 0], left)
+            left = jnp.where(i < j, rn * left + alls[i, 0], left)
         for i in range(J - 1, 0, -1):
-            right = jnp.where(i > j, rn * right + all_ref[i, 1], right)
+            right = jnp.where(i > j, rn * right + alls[i, 1], right)
         sums[0] = left
         sums[1] = right
 
@@ -208,15 +231,23 @@
         gain.append(a0)
         y.append(c)
         z.append(b)
-    for i in range(S):
-        for u in range(tb):
-            y[u] = y[u] * rs[u] + f_ref[u, pl.ds(i, 8, stride=S), :]
-            ys[u, i] = y[u]
-    for i in range(S - 1, -1, -1):
-        for u in range(tb):
-            zr = z[u] * rs[u]
-            out_ref[u, pl.ds(i, 8, stride=S), :] = gain[u] * (ys[u, i] + zr)
-            z[u] = zr + f_ref[u, pl.ds(i, 8, stride=S), :]
+    for rows in batches(0, S, 8):
+        done = []
+        for i in rows:
+            for u in range(tb):
+                y[u] = y[u] * rs[u] + f_ref[u, pl.ds(i, 8, stride=S), :]
+                done.append((u, i, y[u]))
+        for u, i, value in done:
+            ys[u, i] = value
+    for rows in batches(0, S, 8)[::-1]:
+        done = []
+        for i in rows[::-1]:
+            for u in range(tb):
+                zr = z[u] * rs[u]
+                done.append((u, i, gain[u] * (ys[u, i] + zr)))
+                z[u] = zr + f_ref[u, pl.ds(i, 8, stride=S), :]
+        for u, i, value in done:
+            out_ref[u, pl.ds(i, 8, stride=S), :] = value
 
     lane_n = lax.broadcasted_iota(jnp.int32, (n, 128), 1)
     group = lane_n >> 2
@@ -225,9 +256,11 @@
         t = base + u
         acc = jnp.where(group == t, pltpu.roll(out_ref[u], (4 * t + 2) & 127, 1), acc)
     pkh[...] = acc
+    lows = [jnp.where(sub == 7, out_ref[u, 0:1, :], lo7_ref[u]) for u in range(tb)]
+    highs = [jnp.where(sub == 7, out_ref[u, n - 1 : n, :], hi7_ref[u]) for u in range(tb)]
     for u in range(tb):
-        lo_ref[u] = jnp.where(sub == 7, out_ref[u, 0:1, :], lo7_ref[u])
-        hi_ref[u] = jnp.where(sub == 7, out_ref[u, n - 1 : n, :], hi7_ref[u])
+        lo_ref[u] = lows[u]
+        hi_ref[u] = highs[u]
 
     @pl.when(step == pl.num_programs(0) - 1)
     def _():
@@ -243,9 +276,9 @@
         left_ref[1] = sel(pltpu.roll(f0, 126, 1), pltpu.roll(f1, 127, 1), fr, pltpu.roll(he, 1, 1))
 
 
-def heat(d, gathered, seg, prior, pk, lo7, hi7):
+def heat(d, pqs, seg, prior, pk, lo7, hi7):
     T, n, _ = prior.shape
-    J = gathered.shape[0]
+    J = len(pqs)
     tb = 4
     row = jax.ShapeDtypeStruct((T + 1, 8, 128), F32)
     return pl.pallas_call(
@@ -253,7 +286,7 @@
         grid=(T // tb,),
         in_specs=[
             pl.BlockSpec((T, 128), lambda t: (0, 0)),
-            pl.BlockSpec((J, 2, T, 128), lambda t: (0, 0, 0, 0)),
+            *[pl.BlockSpec((2, T, 128), lambda t: (0, 0, 0)) for _ in range(J)],
             pl.BlockSpec((2, tb, 8, 128), lambda t: (0, t, 0, 0)),
             pl.BlockSpec((tb, n, 128), lambda t: (t, 0, 0)),
             pl.BlockSpec((5, n, 128), lambda t: (0, 0, 0)),
@@ -275,6 +308,7 @@
             row,
         ],
         scratch_shapes=[
+            pltpu.VMEM((J, 2, T, 128), F32),
             pltpu.VMEM((2, T, 128), F32),
             pltpu.VMEM((n, 128), F32),
             pltpu.VMEM((tb, n // 8, 8, 128), F32),
@@ -282,7 +316,7 @@
         compiler_params=pltpu.CompilerParams(vmem_limit_bytes=24 * MIB),
         cost_estimate=pl.CostEstimate(flops=10 * T * n * 128, bytes_accessed=8 * T * n * 128, transcendentals=0),
         name="heat",
-    )(d, gathered, seg, prior, pk, lo7, hi7)
+    )(d, *pqs, seg, prior, pk, lo7, hi7)
 
 
 def corner_kernel(n, fl_ref, fr_ref, lo_in, hi_in, r_ref, lo_ref, hi_ref):
@@ -331,7 +365,7 @@
 def coefficients(f0, f1, free, heated):
     v = jnp.exp(-0.5 * heated)
     w = RELAX_FACTOR * free
-    a = w / (DRAG_COEFF + 4.0 * v)
+    a = w * reciprocal(DRAG_COEFF + 4.0 * v)
     return 1.0 - w, a * v, a * f0, a * f1
 
 
@@ -392,25 +426,31 @@
             w = [jnp.where(outer, r[c], o_at(c, i)) for c in range(2)]
             return r, w
 
-        prev, here = both(-2), both(-1)
-        for i in range(-1, S + 1):
-            after = both(i + 1)
-            k, g, a0, a1 = coefficients(e_at(2, i), e_at(3, i), e_at(4, i), e_at(5, i))
-            dr = [after[0][c] - prev[0][c] for c in range(2)]
-            qw = [0.25 * (after[1][c] - prev[1][c]) for c in range(2)]
-            for c in range(2):
-                yh1[c, i + 1] = here[0][c] + sign * dr[1 - c]
-                around = (
-                    prev[0][c]
-                    + after[0][c]
-                    + pltpu.roll(here[1][c] + qw[1 - c], 127, 1)
-                    + pltpu.roll(here[1][c] - qw[1 - c], 1, 1)
-                )
-                r1s[c, i + 1] = k * here[0][c] + (a0, a1)[c] + g * around
-            prev, here = here, after
-        for i in range(S):
-            for c in range(2):
-                yh2[c, i] = r1s[c, i + 1] + sign * (r1s[1 - c, i + 2] - r1s[1 - c, i])
+        for rows in batches(-1, S + 1):
+            both_at = {i: both(i) for i in range(rows[0] - 1, rows[-1] + 2)}
+            done = []
+            for i in rows:
+                prev, here, after = both_at[i - 1], both_at[i], both_at[i + 1]
+                k, g, a0, a1 = coefficients(e_at(2, i), e_at(3, i), e_at(4, i), e_at(5, i))
+                dr = [after[0][c] - prev[0][c] for c in range(2)]
+                qw = [0.25 * (after[1][c] - prev[1][c]) for c in range(2)]
+                for c in range(2):
+                    around = (
+                        prev[0][c]
+                        + after[0][c]
+                        + pltpu.roll(here[1][c] + qw[1 - c], 127, 1)
+                        + pltpu.roll(here[1][c] - qw[1 - c], 1, 1)
+                    )
+                    done.append((c, i, here[0][c] + sign * dr[1 - c], k * here[0][c] + (a0, a1)[c] + g * around))
+            for c, i, edge, new in done:
+                yh1[c, i + 1] = edge
+                r1s[c, i + 1] = new
+        for rows in batches(0, S):
+            done = [
+                (c, i, r1s[c, i + 1] + sign * (r1s[1 - c, i + 2] - r1s[1 - c, i])) for i in rows for c in range(2)
+            ]
+            for c, i, edge in done:
+                yh2[c, i] = edge
 
     def layer(u, _):
         t = step * tb + u
@@ -441,34 +481,52 @@
         def edge_of(k, load, i):
             return ext(load, lambda q: lo_ref[t, k : k + 1, :], lambda q: hi_ref[t, k : k + 1, :], i)
 
-        prev, here = at(-2), at(-1)
-        for i in range(-1, S + 1):
-            after = at(i + 1)
-            co = coefficients(
-                edge_of(4, lambda q: f_ref[0, u, pl.ds(q, 8, stride=S), :], i),
-                edge_of(5, lambda q: f_ref[1, u, pl.ds(q, 8, stride=S), :], i),
-                edge_of(6, lambda q: 1.0 - p_ref[u, pl.ds(q, 8, stride=S), :].astype(F32), i),
-                edge_of(7, lambda q: h_ref[u, pl.ds(q, 8, stride=S), :], i),
-            )
-            if 0 <= i < S:
+        for rows in batches(-1, S + 1):
+            done = [
+                (
+                    i,
+                    coefficients(
+                        edge_of(4, lambda q: f_ref[0, u, pl.ds(q, 8, stride=S), :], i),
+                        edge_of(5, lambda q: f_ref[1, u, pl.ds(q, 8, stride=S), :], i),
+                        edge_of(6, lambda q: 1.0 - p_ref[u, pl.ds(q, 8, stride=S), :].astype(F32), i),
+                        edge_of(7, lambda q: h_ref[u, pl.ds(q, 8, stride=S), :], i),
+                    ),
+                )
+                for i in rows
+            ]
+            for i, co in done:
                 for m in range(4):
-                    cos[m, i] = co[m]
-            new = update(prev, here, after, co[0], co[1], co[2:], [yh1[c, i + 1] for c in range(2)])
-            for c in range(2):
-                v1s[c, i + 1] = new[c]
-            prev, here = here, after
-        for i in range(S):
-            new = update(
-                [v1s[c, i] for c in range(2)],
-                [v1s[c, i + 1] for c in range(2)],
-                [v1s[c, i + 2] for c in range(2)],
-                cos[0, i],
-                cos[1, i],
-                [cos[2, i], cos[3, i]],
-                [yh2[c, i] for c in range(2)],
-            )
-            for c in range(2):
-                out_ref[c, u, pl.ds(i, 8, stride=S), :] = new[c]
+                    cos[m, i + 1] = co[m]
+        for rows in batches(-1, S + 1):
+            x = {i: at(i) for i in range(rows[0] - 1, rows[-1] + 2)}
+            done = [
+                (
+                    i,
+                    update(
+                        x[i - 1], x[i], x[i + 1], cos[0, i + 1], cos[1, i + 1],
+                        [cos[2, i + 1], cos[3, i + 1]], [yh1[c, i + 1] for c in range(2)],
+                    ),
+                )
+                for i in rows
+            ]
+            for i, new in done:
+                for c in range(2):
+                    v1s[c, i + 1] = new[c]
+        for rows in batches(0, S):
+            x = {i: [v1s[c, i + 1] for c in range(2)] for i in range(rows[0] - 1, rows[-1] + 2)}
+            done = [
+                (
+                    i,
+                    update(
+                        x[i - 1], x[i], x[i + 1], cos[0, i + 1], cos[1, i + 1],
+                        [cos[2, i + 1], cos[3, i + 1]], [yh2[c, i] for c in range(2)],
+                    ),
+                )
+                for i in rows
+            ]
+            for i, new in done:
+                for c in range(2):
+                    out_ref[c, u, pl.ds(i, 8, stride=S), :] = new[c]
         return 0
 
     lax.fori_loop(0, tb, layer, 0)
@@ -497,7 +555,7 @@
             pltpu.VMEM((2, S + 2, 8, 128), F32),
             pltpu.VMEM((2, S, 8, 128), F32),
             pltpu.VMEM((2, S + 2, 8, 128), F32),
-            pltpu.VMEM((4, S, 8, 128), F32),
+            pltpu.VMEM((4, S + 2, 8, 128), F32),
             pltpu.VMEM((2, S + 2, 8, 128), F32),
         ],
         compiler_params=pltpu.CompilerParams(vmem_limit_bytes=32 * MIB),
@@ -515,9 +573,10 @@
 
 def local(prior, d, v, f, pinned):
     seg, pq = moments(d, prior)
-    gathered = lax.all_gather(pq, "wid")
+    J = lax.axis_size("wid")
+    pqs = [pq] + [lax.ppermute(pq, "wid", [(i, (i + s) % J) for i in range(J)]) for s in range(1, J)]
     pk, lo7, hi7 = pack(v, f, pinned)
-    heated, right, left, lo, hi = heat(d, gathered, seg, prior, pk, lo7, hi7)
+    heated, right, left, lo, hi = heat(d, pqs, seg, prior, pk, lo7, hi7)
     from_left, from_right = shifted(right, left, "len")
     r, lo, hi = corners(from_left, from_right, lo, hi)
     from_below, from_above = shifted(hi, lo, "wid")

time: 278 us -> 275 us (0.989)
  blocking collectives: 13.6 us -> 0 us
  Pallas kernels: 227 us -> 234 us
  starting transfers between devices: 11.5 us -> 16.8 us
    all_gather x1 -> x0, blocking collectives: 13.6 us -> none  [local(): gathered = lax.all_gather(pq, 'wid')]
    ppermute x0 -> x3, starting transfers between devices: none -> 4.67 us  [local(): lax.ppermute(pq, 'wid', [(i, (i + s) % J) for i in range(J)])]
    pallas_call x1, Pallas kernels: 7.35 us -> 11.9 us  [pack(): pl.pallas_call(functools.partial(pack_kernel, tb, n), grid=(T // tb,), in...]
    unnamed x18 -> x22, local copies, waits for them, and re-layouts: 14 us -> 12 us
  transfers between devices with their start and end apart: 4 -> 7, of which waited for: 4 -> 4; matrix products, arithmetic and copies ran while one was open for 0% -> 0% of each run, Pallas kernels for 0% -> 4%
where the time goes in v1:
time: 275 us; the launch traced here: 274 us
  Pallas kernels  234 us (85%)
  starting transfers between devices  16.8 us (6%)
  local copies, waits for them, and re-layouts  12 us (4%)
  waiting for transfers between devices  10.5 us (4%)
    pallas_call x1, Pallas kernels, sweeps(): pl.pallas_call(functools.partial(sweep_kernel, tb, n), grid=(T // tb,), i...  208 us
    unnamed x22, local copies, waits for them, and re-layouts  12 us
    pallas_call x1, Pallas kernels, pack(): pl.pallas_call(functools.partial(pack_kernel, tb, n), grid=(T // tb,), in...  11.9 us
    pallas_call x1, Pallas kernels, heat(): pl.pallas_call(functools.partial(heat_kernel, J, tb, n), grid=(T // tb,),...  8.8 us
    ppermute x2, starting transfers between devices, shifted(): lax.ppermute(up_going, axis, up)  6.3 us
    ppermute x2, waiting for transfers between devices, shifted(): lax.ppermute(down_going, axis, down)  5.88 us
    ppermute x2, starting transfers between devices, shifted(): lax.ppermute(down_going, axis, down)  5.83 us
  transfers between devices with their start and end apart: 7, of which 4 were waited for; matrix products, arithmetic and copies ran while one was open for 0% of the time, Pallas kernels for 4%

profile of v1, /device:TPU:4, one launch (start us, length us, event | category | flops | bytes accessed | tf_op | source)
XLA Modules:
  0.0 274.5 jit_solution(12549303155400201450)
XLA Ops:
  0.6 5.1 %moments.1 = (f32[2,32,8,128]{3,2,1,0:T(8,128)}, f32[2,32,128]{2,1,0:T(8,128)}) custom-call(f32[32,128]{1,0:T(8,128)} %refs_0_.1, f32[32,256,128]{2,1,0:T(8,128)} %refs_6_.1), custom_call_target="tpu_custom_call" | custom-call | flops 4194304 | bytes 4194304 | tf_op jit(solution)/shard_map/moments/pallas_call | solution.py:101
  5.7 0.0 copy-start.6
  5.7 0.0 copy-start.9
  5.7 0.0 copy-start.10
  5.8 3.7 %collective-permute-start.2 = (f32[2,32,128]{2,1,0:T(8,128)}, f32[2,32,128]{2,1,0:T(8,128)S(1)}, u32[]{:S(2)}, u32[]{:S(2)}) collective-permute-start(f32[2,32,128]{2,1,0:T(8,128)} %get-tuple-element.15.refs_1_), channel_id=1, source_target_pairs={{0,3},{1,0},{2,1},{3,2},{4,7},{5,4},{6,5},{7,6},{8,11},{9,8},{10,9... | collective-permute-start | bytes 98312 | tf_op jit(solution)/shard_map/ppermute | solution.py:577
  9.4 0.0 collective-permute-start.1
  9.4 1.0 collective-permute-start
  10.4 11.9 %pack_edges.1 = (f32[5,256,128]{2,1,0:T(8,128)}, f32[32,8,128]{2,1,0:T(8,128)}, f32[32,8,128]{2,1,0:T(8,128)}) custom-call(f32[2,32,256,128]{3,2,1,0:T(8,128)} %v_ref.3, f32[2,32,256,128]{3,2,1,0:T(8,128)} %f_ref.5, s32[32,256,128]{2,1,0:T(8,128)} %p_ref.3), custom_call_target="tpu_custom_call" | custom-call | flops 5242880 | bytes 20971520 | tf_op jit(solution)/shard_map/pack_edges/pallas_call | solution.py:161
  22.3 0.0 copy-start.1
  22.4 0.0 collective-permute-done.2.refs_4_
  22.4 0.0 collective-permute-done.1.refs_3_
  22.4 0.0 collective-permute-done.refs_2_
  22.4 0.0 copy-done.6
  22.4 0.0 copy-done.9
  22.4 0.0 copy-done.10
  22.4 0.0 copy-start.2
  22.4 2.3 copy-done.2
  24.8 0.0 copy-start.4
  24.8 1.2 copy-done.4
  26.0 0.0 copy-start.7
  26.0 0.9 copy-done.7
  26.9 0.0 copy-start.8
  26.9 0.9 copy-done.8
  27.8 8.8 %heat.1 = (f32[32,256,128]{2,1,0:T(8,128)}, f32[2,256,128]{2,1,0:T(8,128)S(1)}, f32[2,256,128]{2,1,0:T(8,128)S(1)}, f32[33,8,128]{2,1,0:T(8,128)S(1)}, f32[33,8,128]{2,1,0:T(8,128)S(1)}) custom-call(f32[32,128]{1,0:T(8,128)S(1)} %copy-done.9, f32[2,32,128]{2,1,0:T(8,128)S(1)} %copy-done.10, f32[2,32,128]{2,1,0:T(8,128)S(1)} %collective-permute-done.refs_2_, ...), custom_call_target="tpu_custom_call" | custom-call | flops 10485760 | bytes 8388608 | tf_op jit(solution)/shard_map/heat/pallas_call | solution.py:284
  36.6 1.9 collective-permute-start.3
  38.5 4.5 %collective-permute-start.4 = (f32[2,256,128]{2,1,0:T(8,128)S(1)}, f32[2,256,128]{2,1,0:T(8,128)S(1)}, u32[]{:S(2)}, u32[]{:S(2)}) collective-permute-start(f32[2,256,128]{2,1,0:T(8,128)S(1)} %get-tuple-element.22), channel_id=1, source_target_pairs={{4,0},{8,4},{12,8},{16,12},{20,16},{24,20},{28,24},{5,1},{9,5},{13... | collective-permute-start | bytes 786440 | tf_op jit(solution)/shard_map/ppermute | solution.py:571
  43.0 2.1 collective-permute-done.3.fl_ref
  45.1 1.8 collective-permute-done.4.fr_ref
  46.9 0.3 corners.1
  47.3 4.4 %collective-permute-start.5 = (f32[33,8,128]{2,1,0:T(8,128)S(1)}, f32[33,8,128]{2,1,0:T(8,128)S(1)}, u32[]{:S(2)}, u32[]{:S(2)}) collective-permute-start(f32[33,8,128]{2,1,0:T(8,128)S(1)} %get-tuple-element.25), channel_id=1, source_target_pairs={{0,1},{1,2},{2,3},{4,5},{5,6},{6,7},{8,9},{9,10},{10,11},{12,13},{... | collective-permute-start | bytes 405512 | tf_op jit(solution)/shard_map/ppermute | solution.py:571
  51.7 1.3 collective-permute-start.6
  53.0 2.6 collective-permute-done.5.lo_ref
  55.5 4.1 %collective-permute-done.6.hi_ref = f32[33,8,128]{2,1,0:T(8,128)S(1)} collective-permute-done((f32[33,8,128]{2,1,0:T(8,128)S(1)}, f32[33,8,128]{2,1,0:T(8,128)S(1)}, u32[]{:S(2)}, u32[]{:S(2)}) %collective-permute-start.6) | collective-permute-done | bytes 135200 | tf_op jit(solution)/shard_map/ppermute | solution.py:571
  59.6 0.0 copy-done.1
  59.6 0.0 copy-start
  59.6 3.4 %copy-done = f32[2,32,256,128]{3,2,1,0:T(8,128)S(1)} copy-done((f32[2,32,256,128]{3,2,1,0:T(8,128)S(1)}, f32[2,32,256,128]{3,2,1,0:T(8,128)}, u32[]{:S(2)}) %copy-start) | copy-done | bytes 8388632
  63.0 0.0 copy-start.3
  63.0 2.2 copy-done.3
  65.2 0.0 copy-start.5
  65.2 1.1 copy-done.5
  66.3 208.2 %sweeps.1 = f32[2,32,256,128]{3,2,1,0:T(8,128)} custom-call(f32[2,32,256,128]{3,2,1,0:T(8,128)S(1)} %copy-done, f32[2,32,256,128]{3,2,1,0:T(8,128)} %f_ref.5, s32[32,256,128]{2,1,0:T(8,128)S(1)} %copy-done.1, f32[32,256,128]{2,1,0:T(8,128)S(1)} %copy-done.3, f32[33,8,128]{2,1,0:T(8,128)S(1)} %collective-permute-done.5.lo_ref, ...), custom_call_target="tpu_custom_call" | custom-call | flops 62914560 | bytes 33554432 | tf_op jit(solution)/shard_map/sweeps/pallas_call | solution.py:539
Async XLA Ops:
  5.7 16.6 %copy-start.6 = (f32[2,32,8,128]{3,2,1,0:T(8,128)S(1)}, f32[2,32,8,128]{3,2,1,0:T(8,128)}, u32[]{:S(2)}) copy-start(f32[2,32,8,128]{3,2,1,0:T(8,128)} %get-tuple-element.16.refs_5_) | copy-start | bytes 786436
  5.7 16.7 %copy-start.9 = (f32[32,128]{1,0:T(8,128)S(1)}, f32[32,128]{1,0:T(8,128)}, u32[]{:S(2)}) copy-start(f32[32,128]{1,0:T(8,128)} %refs_0_.1) | copy-start | bytes 49156
  5.7 16.7 %copy-start.10 = (f32[2,32,128]{2,1,0:T(8,128)S(1)}, f32[2,32,128]{2,1,0:T(8,128)}, u32[]{:S(2)}) copy-start(f32[2,32,128]{2,1,0:T(8,128)} %get-tuple-element.15.refs_1_) | copy-start | bytes 98308
  5.8 16.6 %collective-permute-start.2 = (f32[2,32,128]{2,1,0:T(8,128)}, f32[2,32,128]{2,1,0:T(8,128)S(1)}, u32[]{:S(2)}, u32[]{:S(2)}) collective-permute-start(f32[2,32,128]{2,1,0:T(8,128)} %get-tuple-element.15.refs_1_), channel_id=1, source_target_pairs={{0,3},{1,0},{2,1},{3,2},{4,7},{5,4},{6,5},{7,6},{8,11},{9,8},{10,9... | collective-permute-start | bytes 98312 | tf_op jit(solution)/shard_map/ppermute | solution.py:577
  9.4 13.0 %collective-permute-start.1 = (f32[2,32,128]{2,1,0:T(8,128)}, f32[2,32,128]{2,1,0:T(8,128)S(1)}, u32[]{:S(2)}, u32[]{:S(2)}) collective-permute-start(f32[2,32,128]{2,1,0:T(8,128)} %get-tuple-element.15.refs_1_), channel_id=1, source_target_pairs={{0,2},{1,3},{2,0},{3,1},{4,6},{5,7},{6,4},{7,5},{8,10},{9,11},{10,... | collective-permute-start | bytes 98312 | tf_op jit(solution)/shard_map/ppermute | solution.py:577
  9.4 13.0 %collective-permute-start = (f32[2,32,128]{2,1,0:T(8,128)}, f32[2,32,128]{2,1,0:T(8,128)S(1)}, u32[]{:S(2)}, u32[]{:S(2)}) collective-permute-start(f32[2,32,128]{2,1,0:T(8,128)} %get-tuple-element.15.refs_1_), channel_id=1, source_target_pairs={{0,1},{1,2},{2,3},{3,0},{4,5},{5,6},{6,7},{7,4},{8,9},{9,10},{10,1... | collective-permute-start | bytes 98312 | tf_op jit(solution)/shard_map/ppermute | solution.py:577
  22.3 37.3 %copy-start.1 = (s32[32,256,128]{2,1,0:T(8,128)S(1)}, s32[32,256,128]{2,1,0:T(8,128)}, u32[]{:S(2)}) copy-start(s32[32,256,128]{2,1,0:T(8,128)} %p_ref.3) | copy-start | bytes 12582916
  22.4 2.3 copy-start.2
  24.8 1.2 copy-start.4
  26.0 0.9 copy-start.7
  26.9 0.9 copy-start.8
  36.6 8.6 %collective-permute-start.3 = (f32[2,256,128]{2,1,0:T(8,128)S(1)}, f32[2,256,128]{2,1,0:T(8,128)S(1)}, u32[]{:S(2)}, u32[]{:S(2)}) collective-permute-start(f32[2,256,128]{2,1,0:T(8,128)S(1)} %get-tuple-element.21), channel_id=1, source_target_pairs={{0,4},{4,8},{8,12},{12,16},{16,20},{20,24},{24,28},{1,5},{5,9},{9,... | collective-permute-start | bytes 786440 | tf_op jit(solution)/shard_map/ppermute | solution.py:571
  38.5 8.4 %collective-permute-start.4 = (f32[2,256,128]{2,1,0:T(8,128)S(1)}, f32[2,256,128]{2,1,0:T(8,128)S(1)}, u32[]{:S(2)}, u32[]{:S(2)}) collective-permute-start(f32[2,256,128]{2,1,0:T(8,128)S(1)} %get-tuple-element.22), channel_id=1, source_target_pairs={{4,0},{8,4},{12,8},{16,12},{20,16},{24,20},{28,24},{5,1},{9,5},{13... | collective-permute-start | bytes 786440 | tf_op jit(solution)/shard_map/ppermute | solution.py:571
  47.3 8.2 %collective-permute-start.5 = (f32[33,8,128]{2,1,0:T(8,128)S(1)}, f32[33,8,128]{2,1,0:T(8,128)S(1)}, u32[]{:S(2)}, u32[]{:S(2)}) collective-permute-start(f32[33,8,128]{2,1,0:T(8,128)S(1)} %get-tuple-element.25), channel_id=1, source_target_pairs={{0,1},{1,2},{2,3},{4,5},{5,6},{6,7},{8,9},{9,10},{10,11},{12,13},{... | collective-permute-start | bytes 405512 | tf_op jit(solution)/shard_map/ppermute | solution.py:571
  51.7 8.0 %collective-permute-start.6 = (f32[33,8,128]{2,1,0:T(8,128)S(1)}, f32[33,8,128]{2,1,0:T(8,128)S(1)}, u32[]{:S(2)}, u32[]{:S(2)}) collective-permute-start(f32[33,8,128]{2,1,0:T(8,128)S(1)} %get-tuple-element.26), channel_id=1, source_target_pairs={{1,0},{2,1},{3,2},{5,4},{6,5},{7,6},{9,8},{10,9},{11,10},{13,12},{... | collective-permute-start | bytes 405512 | tf_op jit(solution)/shard_map/ppermute | solution.py:571
  59.6 3.4 %copy-start = (f32[2,32,256,128]{3,2,1,0:T(8,128)S(1)}, f32[2,32,256,128]{3,2,1,0:T(8,128)}, u32[]{:S(2)}) copy-start(f32[2,32,256,128]{3,2,1,0:T(8,128)} %v_ref.3) | copy-start | bytes 25165828
  63.0 2.2 copy-start.3
  65.2 1.1 copy-start.5

commit v2 on v1

--- a/solution.py
+++ b/solution.py
@@ -48,10 +48,16 @@
     return y * (2.0 - x * y)
 
 
-def batches(lo, hi, most=11):
-    parts = -(-(hi - lo) // most)
-    cuts = [lo + (hi - lo) * k // parts for k in range(parts + 1)]
-    return [range(a, b) for a, b in zip(cuts, cuts[1:])]
+def over_rows(count, body, init=0, backward=False, most=8):
+    most = min(most, count)
+    parts = count // most
+
+    def step(k, carry):
+        start = (parts - 1 - k if backward else k) * most
+        rows = [start + i for i in range(most)]
+        return body(rows[::-1] if backward else rows, carry)
+
+    return lax.fori_loop(0, parts, step, init)
 
 
 def iotas():
@@ -69,14 +75,18 @@
         for u in range(G):
             r, _ = decay(d_ref[pl.ds(base + g * G + u, 1), :])
             rs.append(jnp.broadcast_to(r, (8, 128)))
-        fwd = [None] * G
-        bwd = [None] * G
-        for i in range(S):
-            for u in range(G):
-                a = f_ref[g * G + u, pl.ds(i, 8, stride=S), :]
-                b = f_ref[g * G + u, pl.ds(S - 1 - i, 8, stride=S), :]
-                fwd[u] = a if i == 0 else fwd[u] * rs[u] + a
-                bwd[u] = b if i == 0 else bwd[u] * rs[u] + b
+        zero = jnp.zeros((8, 128), F32)
+
+        def body(rows, carry):
+            fwd, bwd = list(carry[:G]), list(carry[G:])
+            for i in rows:
+                for u in range(G):
+                    fwd[u] = fwd[u] * rs[u] + f_ref[g * G + u, pl.ds(i, 8, stride=S), :]
+                    bwd[u] = bwd[u] * rs[u] + f_ref[g * G + u, pl.ds(S - 1 - i, 8, stride=S), :]
+            return (*fwd, *bwd)
+
+        carry = over_rows(S, body, (zero,) * (2 * G))
+        fwd, bwd = carry[:G], carry[G:]
         for u in range(G):
             k = g * G + u
             seg_ref[0, k] = fwd[u]
@@ -121,20 +131,29 @@
 
 def pack_kernel(tb, n, v_ref, f_ref, p_ref, pk_ref, lo_ref, hi_ref):
     base = pl.program_id(0) * tb
-    lane = lax.broadcasted_iota(jnp.int32, (n, 128), 1)
-    group = lane >> 2
-    for k in range(5):
-        acc = pk_ref[k]
-        for u in range(tb):
-            if k < 2:
-                x = v_ref[k, u]
-            elif k < 4:
-                x = f_ref[k - 2, u]
-            else:
-                x = 1.0 - p_ref[u].astype(F32)
-            t = base + u
-            acc = jnp.where(group == t, pltpu.roll(x, (4 * t + 2) & 127, 1), acc)
-        pk_ref[k] = acc
+    chunk = min(64, n)
+    group = lax.broadcasted_iota(jnp.int32, (chunk, 128), 1) >> 2
+
+    def body(m, _):
+        rows = pl.ds(pl.multiple_of(m * chunk, chunk), chunk)
+        packed = []
+        for k in range(5):
+            acc = pk_ref[k, rows, :]
+            for u in range(tb):
+                if k < 2:
+                    x = v_ref[k, u, rows, :]
+                elif k < 4:
+                    x = f_ref[k - 2, u, rows, :]
+                else:
+                    x = 1.0 - p_ref[u, rows, :].astype(F32)
+                t = base + u
+                acc = jnp.where(group == t, pltpu.roll(x, (4 * t + 2) & 127, 1), acc)
+            packed.append(acc)
+        for k in range(5):
+            pk_ref[k, rows, :] = packed[k]
+        return 0
+
+    lax.fori_loop(0, n // chunk, body, 0)
     _, sub = iotas()
 
     def stack(v0, v1, f0, f1, fr):
@@ -231,23 +250,29 @@
         gain.append(a0)
         y.append(c)
         z.append(b)
-    for rows in batches(0, S, 8):
-        done = []
+    def forward(rows, y):
+        y, done = list(y), []
         for i in rows:
             for u in range(tb):
                 y[u] = y[u] * rs[u] + f_ref[u, pl.ds(i, 8, stride=S), :]
                 done.append((u, i, y[u]))
         for u, i, value in done:
             ys[u, i] = value
-    for rows in batches(0, S, 8)[::-1]:
-        done = []
-        for i in rows[::-1]:
+        return tuple(y)
+
+    def backward(rows, z):
+        z, done = list(z), []
+        for i in rows:
             for u in range(tb):
                 zr = z[u] * rs[u]
                 done.append((u, i, gain[u] * (ys[u, i] + zr)))
                 z[u] = zr + f_ref[u, pl.ds(i, 8, stride=S), :]
         for u, i, value in done:
             out_ref[u, pl.ds(i, 8, stride=S), :] = value
+        return tuple(z)
+
+    over_rows(S, forward, tuple(y))
+    over_rows(S, backward, tuple(z), backward=True)
 
     lane_n = lax.broadcasted_iota(jnp.int32, (n, 128), 1)
     group = lane_n >> 2
@@ -371,7 +396,7 @@
 
 def sweep_kernel(
     tb, n, v_ref, f_ref, p_ref, h_ref, lo_ref, hi_ref, r_ref, own_ref,
-    out_ref, yh1, yh2, v1s, cos, r1s,
+    out_ref, yh1, yh2, xs, ws, v1s, cos,
 ):
     S = n // 8
     T = lo_ref.shape[0] - 1
@@ -380,83 +405,102 @@
     slot = lane & 3
     first, last = lane == 0, lane == 127
 
-    def ext(load, lo_row, hi_row, i):
-        if i < 0:
-            return jnp.where(sub == 0, lo_row(i), pltpu.roll(load(S + i), 1, 0))
-        if i >= S:
-            return jnp.where(sub == 7, hi_row(i - S), pltpu.roll(load(i - S), 7, 0))
-        return load(i)
+    def under(row, last_vector):
+        return jnp.where(sub == 0, row, pltpu.roll(last_vector, 1, 0))
+
+    def over(row, first_vector):
+        return jnp.where(sub == 7, row, pltpu.roll(first_vector, 7, 0))
+
+    def put(todo):
+        for ref, c, i, value in todo:
+            ref[c, i] = value
+
+    def halo_rows(ref, low, high):
+        todo = []
+        for c in range(2):
+            for q in range(2):
+                todo.append((ref, c, q, under(low(2 * c + q), ref[c, S + q])))
+                todo.append((ref, c, S + 2 + q, over(high(2 * c + q), ref[c, q + 2])))
+        put(todo)
+
+    def halo_coefficients(low, high, get):
+        below = coefficients(*[under(low(4 + m), get(m, S - 1)) for m in range(4)])
+        above = coefficients(*[over(high(4 + m), get(m, 0)) for m in range(4)])
+        put([(cos, m, 0, below[m]) for m in range(4)] + [(cos, m, S + 1, above[m]) for m in range(4)])
 
     @pl.when(step == 0)
     def _():
-        own_lo = jnp.zeros((8, 128), F32)
-        own_hi = jnp.zeros((8, 128), F32)
-        for t in range(T):
-            own_lo = jnp.where(lane >> 2 == t, pltpu.roll(lo_ref[t], (4 * t + 2) & 127, 1), own_lo)
-            own_hi = jnp.where(lane >> 2 == t, pltpu.roll(hi_ref[t], (4 * t + 2) & 127, 1), own_hi)
         outer = (slot == 0) | (slot == 3)
         sign = jnp.where(slot == 1, -0.25, 0.25)
 
-        def r_at(c, i):
-            return ext(
-                lambda q: r_ref[c, pl.ds(q, 8, stride=S), :],
-                lambda q: lo_ref[T, 2 * c + 2 + q : 2 * c + 3 + q, :],
-                lambda q: hi_ref[T, 2 * c + q : 2 * c + 1 + q, :],
-                i,
+        def get(m, i):
+            return r_ref[2 + m, pl.ds(i, 8, stride=S), :]
+
+        def collect(t, carry):
+            own = lane >> 2 == t
+            return [
+                jnp.where(own, pltpu.roll(ref[t], (4 * t + 2) & 127, 1), acc)
+                for ref, acc in zip((lo_ref, hi_ref), carry)
+            ]
+
+        zero = jnp.zeros((8, 128), F32)
+        own_lo, own_hi = lax.fori_loop(0, T, collect, [zero, zero])
+        both_lo = jnp.where(outer, lo_ref[T], own_lo)
+        both_hi = jnp.where(outer, hi_ref[T], own_hi)
+
+        def load(rows, _):
+            todo = []
+            for i in rows:
+                for c in range(2):
+                    r = r_ref[c, pl.ds(i, 8, stride=S), :]
+                    todo.append((xs, c, i + 2, r))
+                    todo.append((ws, c, i + 2, jnp.where(outer, r, own_ref[c, pl.ds(i, 8, stride=S), :])))
+                co = coefficients(*[get(m, i) for m in range(4)])
+                todo += [(cos, m, i + 1, co[m]) for m in range(4)]
+            put(todo)
+            return 0
+
+        over_rows(S, load, most=4)
+        halo_rows(xs, lambda k: lo_ref[T, k : k + 1, :], lambda k: hi_ref[T, k : k + 1, :])
+        halo_rows(ws, lambda k: both_lo[k : k + 1, :], lambda k: both_hi[k : k + 1, :])
+        halo_coefficients(lambda k: lo_ref[T, k : k + 1, :], lambda k: hi_ref[T, k : k + 1, :], get)
+
+        def relax(rows, _):
+            todo = []
+            for i in rows:
+                r = [[xs[c, i + d] for c in range(2)] for d in (1, 2, 3)]
+                w = [[ws[c, i + d] for c in range(2)] for d in (1, 2, 3)]
+                for c in range(2):
+                    q = 0.25 * (w[2][1 - c] - w[0][1 - c])
+                    around = (
+                        r[0][c] + r[2][c] + pltpu.roll(w[1][c] + q, 127, 1) + pltpu.roll(w[1][c] - q, 1, 1)
+                    )
+                    todo.append((yh1, c, i + 1, r[1][c] + sign * (r[2][1 - c] - r[0][1 - c])))
+                    new = cos[0, i + 1] * r[1][c] + cos[2 + c, i + 1] + cos[1, i + 1] * around
+                    todo.append((v1s, c, i + 1, new))
+            put(todo)
+            return 0
+
+        over_rows(S, relax, most=4)
+        relax([-1, S], 0)
+
+        def edges(rows, _):
+            put(
+                [
+                    (yh2, c, i, v1s[c, i + 1] + sign * (v1s[1 - c, i + 2] - v1s[1 - c, i]))
+                    for i in rows
+                    for c in range(2)
+                ]
             )
-
-        def o_at(c, i):
-            return ext(
-                lambda q: own_ref[c, pl.ds(q, 8, stride=S), :],
-                lambda q: own_lo[2 * c + 2 + q : 2 * c + 3 + q, :],
-                lambda q: own_hi[2 * c + q : 2 * c + 1 + q, :],
-                i,
-            )
-
-        def e_at(k, i):
-            return ext(
-                lambda q: r_ref[k, pl.ds(q, 8, stride=S), :],
-                lambda q: lo_ref[T, 2 + k : 3 + k, :],
-                lambda q: hi_ref[T, 2 + k : 3 + k, :],
-                i,
-            )
-
-        def both(i):
-            r = [r_at(c, i) for c in range(2)]
-            w = [jnp.where(outer, r[c], o_at(c, i)) for c in range(2)]
-            return r, w
-
-        for rows in batches(-1, S + 1):
-            both_at = {i: both(i) for i in range(rows[0] - 1, rows[-1] + 2)}
-            done = []
-            for i in rows:
-                prev, here, after = both_at[i - 1], both_at[i], both_at[i + 1]
-                k, g, a0, a1 = coefficients(e_at(2, i), e_at(3, i), e_at(4, i), e_at(5, i))
-                dr = [after[0][c] - prev[0][c] for c in range(2)]
-                qw = [0.25 * (after[1][c] - prev[1][c]) for c in range(2)]
-                for c in range(2):
-                    around = (
-                        prev[0][c]
-                        + after[0][c]
-                        + pltpu.roll(here[1][c] + qw[1 - c], 127, 1)
-                        + pltpu.roll(here[1][c] - qw[1 - c], 1, 1)
-                    )
-                    done.append((c, i, here[0][c] + sign * dr[1 - c], k * here[0][c] + (a0, a1)[c] + g * around))
-            for c, i, edge, new in done:
-                yh1[c, i + 1] = edge
-                r1s[c, i + 1] = new
-        for rows in batches(0, S):
-            done = [
-                (c, i, r1s[c, i + 1] + sign * (r1s[1 - c, i + 2] - r1s[1 - c, i])) for i in rows for c in range(2)
-            ]
-            for c, i, edge in done:
-                yh2[c, i] = edge
+            return 0
+
+        over_rows(S, edges)
 
     def layer(u, _):
         t = step * tb + u
         shift = (126 - 4 * t) & 127
 
-        def update(prev, here, after, k, g, a, yh):
+        def update(prev, here, after, i, yh):
             q = [0.25 * (after[c] - prev[c]) for c in range(2)]
             new = []
             for c in range(2):
@@ -464,69 +508,51 @@
                 up = jnp.where(first, edge, here[c] + q[1 - c])
                 down = jnp.where(last, edge, here[c] - q[1 - c])
                 around = prev[c] + after[c] + (pltpu.roll(up, 127, 1) + pltpu.roll(down, 1, 1))
-                new.append(k * here[c] + a[c] + g * around)
+                new.append(cos[0, i + 1] * here[c] + cos[2 + c, i + 1] + cos[1, i + 1] * around)
             return new
 
-        def at(i):
-            return [
-                ext(
-                    lambda q: v_ref[c, u, pl.ds(q, 8, stride=S), :],
-                    lambda q: lo_ref[t, 2 * c + 2 + q : 2 * c + 3 + q, :],
-                    lambda q: hi_ref[t, 2 * c + q : 2 * c + 1 + q, :],
-                    i,
-                )
-                for c in range(2)
-            ]
-
-        def edge_of(k, load, i):
-            return ext(load, lambda q: lo_ref[t, k : k + 1, :], lambda q: hi_ref[t, k : k + 1, :], i)
-
-        for rows in batches(-1, S + 1):
-            done = [
-                (
-                    i,
-                    coefficients(
-                        edge_of(4, lambda q: f_ref[0, u, pl.ds(q, 8, stride=S), :], i),
-                        edge_of(5, lambda q: f_ref[1, u, pl.ds(q, 8, stride=S), :], i),
-                        edge_of(6, lambda q: 1.0 - p_ref[u, pl.ds(q, 8, stride=S), :].astype(F32), i),
-                        edge_of(7, lambda q: h_ref[u, pl.ds(q, 8, stride=S), :], i),
-                    ),
-                )
-                for i in rows
-            ]
-            for i, co in done:
-                for m in range(4):
-                    cos[m, i + 1] = co[m]
-        for rows in batches(-1, S + 1):
-            x = {i: at(i) for i in range(rows[0] - 1, rows[-1] + 2)}
-            done = [
-                (
-                    i,
-                    update(
-                        x[i - 1], x[i], x[i + 1], cos[0, i + 1], cos[1, i + 1],
-                        [cos[2, i + 1], cos[3, i + 1]], [yh1[c, i + 1] for c in range(2)],
-                    ),
-                )
-                for i in rows
-            ]
-            for i, new in done:
-                for c in range(2):
-                    v1s[c, i + 1] = new[c]
-        for rows in batches(0, S):
-            x = {i: [v1s[c, i + 1] for c in range(2)] for i in range(rows[0] - 1, rows[-1] + 2)}
-            done = [
-                (
-                    i,
-                    update(
-                        x[i - 1], x[i], x[i + 1], cos[0, i + 1], cos[1, i + 1],
-                        [cos[2, i + 1], cos[3, i + 1]], [yh2[c, i] for c in range(2)],
-                    ),
-                )
-                for i in rows
-            ]
-            for i, new in done:
-                for c in range(2):
-                    out_ref[c, u, pl.ds(i, 8, stride=S), :] = new[c]
+        def get(m, i):
+            rows = pl.ds(i, 8, stride=S)
+            if m < 2:
+                return f_ref[m, u, rows, :]
+            return 1.0 - p_ref[u, rows, :].astype(F32) if m == 2 else h_ref[u, rows, :]
+
+        def load(rows, _):
+            todo = []
+            for i in rows:
+                todo += [(xs, c, i + 2, v_ref[c, u, pl.ds(i, 8, stride=S), :]) for c in range(2)]
+                co = coefficients(*[get(m, i) for m in range(4)])
+                todo += [(cos, m, i + 1, co[m]) for m in range(4)]
+            put(todo)
+            return 0
+
+        over_rows(S, load)
+        halo_rows(xs, lambda k: lo_ref[t, k : k + 1, :], lambda k: hi_ref[t, k : k + 1, :])
+        halo_coefficients(lambda k: lo_ref[t, k : k + 1, :], lambda k: hi_ref[t, k : k + 1, :], get)
+
+        def first_sweep(rows, _):
+            todo = []
+            for i in rows:
+                x = [[xs[c, i + d] for c in range(2)] for d in (1, 2, 3)]
+                new = update(*x, i, [yh1[c, i + 1] for c in range(2)])
+                todo += [(v1s, c, i + 1, new[c]) for c in range(2)]
+            put(todo)
+            return 0
+
+        over_rows(S, first_sweep)
+        first_sweep([-1, S], 0)
+
+        def second_sweep(rows, _):
+            todo = []
+            for i in rows:
+                x = [[v1s[c, i + d] for c in range(2)] for d in (0, 1, 2)]
+                new = update(*x, i, [yh2[c, i] for c in range(2)])
+                todo += [(c, i, new[c]) for c in range(2)]
+            for c, i, value in todo:
+                out_ref[c, u, pl.ds(i, 8, stride=S), :] = value
+            return 0
+
+        over_rows(S, second_sweep)
         return 0
 
     lax.fori_loop(0, tb, layer, 0)
@@ -554,9 +580,10 @@
         scratch_shapes=[
             pltpu.VMEM((2, S + 2, 8, 128), F32),
             pltpu.VMEM((2, S, 8, 128), F32),
+            pltpu.VMEM((2, S + 4, 8, 128), F32),
+            pltpu.VMEM((2, S + 4, 8, 128), F32),
             pltpu.VMEM((2, S + 2, 8, 128), F32),
             pltpu.VMEM((4, S + 2, 8, 128), F32),
-            pltpu.VMEM((2, S + 2, 8, 128), F32),
         ],
         compiler_params=pltpu.CompilerParams(vmem_limit_bytes=32 * MIB),
         cost_estimate=pl.CostEstimate(flops=60 * T * n * 128, bytes_accessed=32 * T * n * 128, transcendentals=T * n * 128),

time: 275 us -> 151 us (0.55)
  Pallas kernels: 234 us -> 110 us
    pallas_call x1, Pallas kernels: 208 us -> 77.8 us  [sweeps(): pl.pallas_call(functools.partial(sweep_kernel, tb, n), grid=(T // tb,), i...]
    pallas_call x1, Pallas kernels: 8.8 us -> 12.3 us  [heat(): pl.pallas_call(functools.partial(heat_kernel, J, tb, n), grid=(T // tb,),...]
  transfers between devices with their start and end apart: 7 -> 7, of which waited for: 4 -> 4; matrix products, arithmetic and copies ran while one was open for 0% -> 0% of each run, Pallas kernels for 4% -> 9%
where the time goes in v2:
time: 151 us
  Pallas kernels  110 us (73%)
  starting transfers between devices  16.8 us (11%)
  local copies, waits for them, and re-layouts  12 us (8%)
  waiting for transfers between devices  10.5 us (7%)
    pallas_call x1, Pallas kernels, sweeps(): pl.pallas_call(functools.partial(sweep_kernel, tb, n), grid=(T // tb,), i...  77.8 us
    pallas_call x1, Pallas kernels, pack(): pl.pallas_call(functools.partial(pack_kernel, tb, n), grid=(T // tb,), in...  12.8 us
    pallas_call x1, Pallas kernels, heat(): pl.pallas_call(functools.partial(heat_kernel, J, tb, n), grid=(T // tb,),...  12.3 us
    unnamed x22, local copies, waits for them, and re-layouts  12 us
    pallas_call x1, Pallas kernels, moments(): pl.pallas_call(functools.partial(moments_kernel, tb, n), grid=(T // tb,),...  7.26 us
    ppermute x2, starting transfers between devices, shifted(): lax.ppermute(up_going, axis, up)  6.3 us
    ppermute x2, waiting for transfers between devices, shifted(): lax.ppermute(down_going, axis, down)  5.88 us
    ppermute x2, starting transfers between devices, shifted(): lax.ppermute(down_going, axis, down)  5.83 us
  transfers between devices with their start and end apart: 7, of which 4 were waited for; matrix products, arithmetic and copies ran while one was open for 0% of the time, Pallas kernels for 9%

profile of v2, /device:TPU:4, one launch (start us, length us, event | category | flops | bytes accessed | tf_op | source)
XLA Modules:
  0.0 150.6 jit_solution(15957155120286127055)
XLA Ops:
  0.6 7.3 %moments.1 = (f32[2,32,8,128]{3,2,1,0:T(8,128)}, f32[2,32,128]{2,1,0:T(8,128)}) custom-call(f32[32,128]{1,0:T(8,128)} %refs_0_.1, f32[32,256,128]{2,1,0:T(8,128)} %refs_6_.1), custom_call_target="tpu_custom_call" | custom-call | flops 4194304 | bytes 4194304 | tf_op jit(solution)/shard_map/moments/pallas_call | solution.py:111
  7.9 0.0 copy-start.6
  7.9 0.0 copy-start.9
  7.9 0.0 copy-start.10
  7.9 3.7 %collective-permute-start.2 = (f32[2,32,128]{2,1,0:T(8,128)}, f32[2,32,128]{2,1,0:T(8,128)S(1)}, u32[]{:S(2)}, u32[]{:S(2)}) collective-permute-start(f32[2,32,128]{2,1,0:T(8,128)} %get-tuple-element.15.refs_1_), channel_id=1, source_target_pairs={{0,3},{1,0},{2,1},{3,2},{4,7},{5,4},{6,5},{7,6},{8,11},{9,8},{10,9... | collective-permute-start | bytes 98312 | tf_op jit(solution)/shard_map/ppermute | solution.py:604
  11.6 0.0 collective-permute-start.1
  11.6 1.0 collective-permute-start
  12.6 12.8 %pack_edges.1 = (f32[5,256,128]{2,1,0:T(8,128)}, f32[32,8,128]{2,1,0:T(8,128)}, f32[32,8,128]{2,1,0:T(8,128)}) custom-call(f32[2,32,256,128]{3,2,1,0:T(8,128)} %v_ref.3, f32[2,32,256,128]{3,2,1,0:T(8,128)} %f_ref.5, s32[32,256,128]{2,1,0:T(8,128)} %p_ref.3), custom_call_target="tpu_custom_call" | custom-call | flops 5242880 | bytes 20971520 | tf_op jit(solution)/shard_map/pack_edges/pallas_call | solution.py:180
  25.4 0.0 copy-start.1
  25.4 0.0 collective-permute-done.2.refs_4_
  25.4 0.0 collective-permute-done.1.refs_3_
  25.4 0.0 collective-permute-done.refs_2_
  25.4 0.0 copy-done.6
  25.4 0.0 copy-done.9
  25.5 0.0 copy-done.10
  25.5 0.0 copy-start.2
  25.5 2.3 %copy-done.2 = f32[32,256,128]{2,1,0:T(8,128)S(1)} copy-done((f32[32,256,128]{2,1,0:T(8,128)S(1)}, f32[32,256,128]{2,1,0:T(8,128)}, u32[]{:S(2)}) %copy-start.2) | copy-done | bytes 4194328
  27.8 0.0 copy-start.4
  27.8 1.2 copy-done.4
  29.0 0.0 copy-start.7
  29.0 0.9 copy-done.7
  29.9 0.0 copy-start.8
  29.9 0.9 copy-done.8
  30.8 12.3 %heat.1 = (f32[32,256,128]{2,1,0:T(8,128)}, f32[2,256,128]{2,1,0:T(8,128)S(1)}, f32[2,256,128]{2,1,0:T(8,128)S(1)}, f32[33,8,128]{2,1,0:T(8,128)S(1)}, f32[33,8,128]{2,1,0:T(8,128)S(1)}) custom-call(f32[32,128]{1,0:T(8,128)S(1)} %copy-done.9, f32[2,32,128]{2,1,0:T(8,128)S(1)} %copy-done.10, f32[2,32,128]{2,1,0:T(8,128)S(1)} %collective-permute-done.refs_2_, ...), custom_call_target="tpu_custom_call" | custom-call | flops 10485760 | bytes 8388608 | tf_op jit(solution)/shard_map/heat/pallas_call | solution.py:309
  43.1 1.9 %collective-permute-start.3 = (f32[2,256,128]{2,1,0:T(8,128)S(1)}, f32[2,256,128]{2,1,0:T(8,128)S(1)}, u32[]{:S(2)}, u32[]{:S(2)}) collective-permute-start(f32[2,256,128]{2,1,0:T(8,128)S(1)} %get-tuple-element.21), channel_id=1, source_target_pairs={{0,4},{4,8},{8,12},{12,16},{16,20},{20,24},{24,28},{1,5},{5,9},{9,... | collective-permute-start | bytes 786440 | tf_op jit(solution)/shard_map/ppermute | solution.py:598
  45.0 4.5 %collective-permute-start.4 = (f32[2,256,128]{2,1,0:T(8,128)S(1)}, f32[2,256,128]{2,1,0:T(8,128)S(1)}, u32[]{:S(2)}, u32[]{:S(2)}) collective-permute-start(f32[2,256,128]{2,1,0:T(8,128)S(1)} %get-tuple-element.22), channel_id=1, source_target_pairs={{4,0},{8,4},{12,8},{16,12},{20,16},{24,20},{28,24},{5,1},{9,5},{13... | collective-permute-start | bytes 786440 | tf_op jit(solution)/shard_map/ppermute | solution.py:598
  49.5 2.1 %collective-permute-done.3.fl_ref = f32[2,256,128]{2,1,0:T(8,128)S(1)} collective-permute-done((f32[2,256,128]{2,1,0:T(8,128)S(1)}, f32[2,256,128]{2,1,0:T(8,128)S(1)}, u32[]{:S(2)}, u32[]{:S(2)}) %collective-permute-start.3) | collective-permute-done | bytes 262176 | tf_op jit(solution)/shard_map/ppermute | solution.py:598
  51.7 1.8 %collective-permute-done.4.fr_ref = f32[2,256,128]{2,1,0:T(8,128)S(1)} collective-permute-done((f32[2,256,128]{2,1,0:T(8,128)S(1)}, f32[2,256,128]{2,1,0:T(8,128)S(1)}, u32[]{:S(2)}, u32[]{:S(2)}) %collective-permute-start.4) | collective-permute-done | bytes 262176 | tf_op jit(solution)/shard_map/ppermute | solution.py:598
  53.4 0.3 corners.1
  53.8 4.4 %collective-permute-start.5 = (f32[33,8,128]{2,1,0:T(8,128)S(1)}, f32[33,8,128]{2,1,0:T(8,128)S(1)}, u32[]{:S(2)}, u32[]{:S(2)}) collective-permute-start(f32[33,8,128]{2,1,0:T(8,128)S(1)} %get-tuple-element.25), channel_id=1, source_target_pairs={{0,1},{1,2},{2,3},{4,5},{5,6},{6,7},{8,9},{9,10},{10,11},{12,13},{... | collective-permute-start | bytes 405512 | tf_op jit(solution)/shard_map/ppermute | solution.py:598
  58.2 1.3 collective-permute-start.6
  59.5 2.6 %collective-permute-done.5.lo_ref = f32[33,8,128]{2,1,0:T(8,128)S(1)} collective-permute-done((f32[33,8,128]{2,1,0:T(8,128)S(1)}, f32[33,8,128]{2,1,0:T(8,128)S(1)}, u32[]{:S(2)}, u32[]{:S(2)}) %collective-permute-start.5) | collective-permute-done | bytes 135200 | tf_op jit(solution)/shard_map/ppermute | solution.py:598
  62.0 4.1 %collective-permute-done.6.hi_ref = f32[33,8,128]{2,1,0:T(8,128)S(1)} collective-permute-done((f32[33,8,128]{2,1,0:T(8,128)S(1)}, f32[33,8,128]{2,1,0:T(8,128)S(1)}, u32[]{:S(2)}, u32[]{:S(2)}) %collective-permute-start.6) | collective-permute-done | bytes 135200 | tf_op jit(solution)/shard_map/ppermute | solution.py:598
  66.1 0.0 copy-done.1
  66.1 0.0 copy-start
  66.1 3.4 %copy-done = f32[2,32,256,128]{3,2,1,0:T(8,128)S(1)} copy-done((f32[2,32,256,128]{3,2,1,0:T(8,128)S(1)}, f32[2,32,256,128]{3,2,1,0:T(8,128)}, u32[]{:S(2)}) %copy-start) | copy-done | bytes 8388632
  69.5 0.0 copy-start.3
  69.5 2.2 %copy-done.3 = f32[32,256,128]{2,1,0:T(8,128)S(1)} copy-done((f32[32,256,128]{2,1,0:T(8,128)S(1)}, f32[32,256,128]{2,1,0:T(8,128)}, u32[]{:S(2)}) %copy-start.3) | copy-done | bytes 4194328
  71.7 0.0 copy-start.5
  71.7 1.1 copy-done.5
  72.8 77.8 %sweeps.1 = f32[2,32,256,128]{3,2,1,0:T(8,128)} custom-call(f32[2,32,256,128]{3,2,1,0:T(8,128)S(1)} %copy-done, f32[2,32,256,128]{3,2,1,0:T(8,128)} %f_ref.5, s32[32,256,128]{2,1,0:T(8,128)S(1)} %copy-done.1, f32[32,256,128]{2,1,0:T(8,128)S(1)} %copy-done.3, f32[33,8,128]{2,1,0:T(8,128)S(1)} %collective-permute-done.5.lo_ref, ...), custom_call_target="tpu_custom_call" | custom-call | flops 62914560 | bytes 33554432 | tf_op jit(solution)/shard_map/sweeps/pallas_call | solution.py:565
Async XLA Ops:
  7.9 17.6 %copy-start.6 = (f32[2,32,8,128]{3,2,1,0:T(8,128)S(1)}, f32[2,32,8,128]{3,2,1,0:T(8,128)}, u32[]{:S(2)}) copy-start(f32[2,32,8,128]{3,2,1,0:T(8,128)} %get-tuple-element.16.refs_5_) | copy-start | bytes 786436
  7.9 17.6 %copy-start.9 = (f32[32,128]{1,0:T(8,128)S(1)}, f32[32,128]{1,0:T(8,128)}, u32[]{:S(2)}) copy-start(f32[32,128]{1,0:T(8,128)} %refs_0_.1) | copy-start | bytes 49156
  7.9 17.6 %copy-start.10 = (f32[2,32,128]{2,1,0:T(8,128)S(1)}, f32[2,32,128]{2,1,0:T(8,128)}, u32[]{:S(2)}) copy-start(f32[2,32,128]{2,1,0:T(8,128)} %get-tuple-element.15.refs_1_) | copy-start | bytes 98308
  7.9 17.5 %collective-permute-start.2 = (f32[2,32,128]{2,1,0:T(8,128)}, f32[2,32,128]{2,1,0:T(8,128)S(1)}, u32[]{:S(2)}, u32[]{:S(2)}) collective-permute-start(f32[2,32,128]{2,1,0:T(8,128)} %get-tuple-element.15.refs_1_), channel_id=1, source_target_pairs={{0,3},{1,0},{2,1},{3,2},{4,7},{5,4},{6,5},{7,6},{8,11},{9,8},{10,9... | collective-permute-start | bytes 98312 | tf_op jit(solution)/shard_map/ppermute | solution.py:604
  11.6 13.9 %collective-permute-start.1 = (f32[2,32,128]{2,1,0:T(8,128)}, f32[2,32,128]{2,1,0:T(8,128)S(1)}, u32[]{:S(2)}, u32[]{:S(2)}) collective-permute-start(f32[2,32,128]{2,1,0:T(8,128)} %get-tuple-element.15.refs_1_), channel_id=1, source_target_pairs={{0,2},{1,3},{2,0},{3,1},{4,6},{5,7},{6,4},{7,5},{8,10},{9,11},{10,... | collective-permute-start | bytes 98312 | tf_op jit(solution)/shard_map/ppermute | solution.py:604
  11.6 13.9 %collective-permute-start = (f32[2,32,128]{2,1,0:T(8,128)}, f32[2,32,128]{2,1,0:T(8,128)S(1)}, u32[]{:S(2)}, u32[]{:S(2)}) collective-permute-start(f32[2,32,128]{2,1,0:T(8,128)} %get-tuple-element.15.refs_1_), channel_id=1, source_target_pairs={{0,1},{1,2},{2,3},{3,0},{4,5},{5,6},{6,7},{7,4},{8,9},{9,10},{10,1... | collective-permute-start | bytes 98312 | tf_op jit(solution)/shard_map/ppermute | solution.py:604
  25.4 40.7 %copy-start.1 = (s32[32,256,128]{2,1,0:T(8,128)S(1)}, s32[32,256,128]{2,1,0:T(8,128)}, u32[]{:S(2)}) copy-start(s32[32,256,128]{2,1,0:T(8,128)} %p_ref.3) | copy-start | bytes 12582916
  25.5 2.3 %copy-start.2 = (f32[32,256,128]{2,1,0:T(8,128)S(1)}, f32[32,256,128]{2,1,0:T(8,128)}, u32[]{:S(2)}) copy-start(f32[32,256,128]{2,1,0:T(8,128)} %refs_6_.1) | copy-start | bytes 12582916
  27.8 1.2 copy-start.4
  29.0 0.9 copy-start.7
  29.9 0.9 copy-start.8
  43.1 8.6 %collective-permute-start.3 = (f32[2,256,128]{2,1,0:T(8,128)S(1)}, f32[2,256,128]{2,1,0:T(8,128)S(1)}, u32[]{:S(2)}, u32[]{:S(2)}) collective-permute-start(f32[2,256,128]{2,1,0:T(8,128)S(1)} %get-tuple-element.21), channel_id=1, source_target_pairs={{0,4},{4,8},{8,12},{12,16},{16,20},{20,24},{24,28},{1,5},{5,9},{9,... | collective-permute-start | bytes 786440 | tf_op jit(solution)/shard_map/ppermute | solution.py:598
  45.0 8.4 %collective-permute-start.4 = (f32[2,256,128]{2,1,0:T(8,128)S(1)}, f32[2,256,128]{2,1,0:T(8,128)S(1)}, u32[]{:S(2)}, u32[]{:S(2)}) collective-permute-start(f32[2,256,128]{2,1,0:T(8,128)S(1)} %get-tuple-element.22), channel_id=1, source_target_pairs={{4,0},{8,4},{12,8},{16,12},{20,16},{24,20},{28,24},{5,1},{9,5},{13... | collective-permute-start | bytes 786440 | tf_op jit(solution)/shard_map/ppermute | solution.py:598
  53.8 8.2 %collective-permute-start.5 = (f32[33,8,128]{2,1,0:T(8,128)S(1)}, f32[33,8,128]{2,1,0:T(8,128)S(1)}, u32[]{:S(2)}, u32[]{:S(2)}) collective-permute-start(f32[33,8,128]{2,1,0:T(8,128)S(1)} %get-tuple-element.25), channel_id=1, source_target_pairs={{0,1},{1,2},{2,3},{4,5},{5,6},{6,7},{8,9},{9,10},{10,11},{12,13},{... | collective-permute-start | bytes 405512 | tf_op jit(solution)/shard_map/ppermute | solution.py:598
  58.2 8.0 %collective-permute-start.6 = (f32[33,8,128]{2,1,0:T(8,128)S(1)}, f32[33,8,128]{2,1,0:T(8,128)S(1)}, u32[]{:S(2)}, u32[]{:S(2)}) collective-permute-start(f32[33,8,128]{2,1,0:T(8,128)S(1)} %get-tuple-element.26), channel_id=1, source_target_pairs={{1,0},{2,1},{3,2},{5,4},{6,5},{7,6},{9,8},{10,9},{11,10},{13,12},{... | collective-permute-start | bytes 405512 | tf_op jit(solution)/shard_map/ppermute | solution.py:598
  66.1 3.4 %copy-start = (f32[2,32,256,128]{3,2,1,0:T(8,128)S(1)}, f32[2,32,256,128]{3,2,1,0:T(8,128)}, u32[]{:S(2)}) copy-start(f32[2,32,256,128]{3,2,1,0:T(8,128)} %v_ref.3) | copy-start | bytes 25165828
  69.5 2.2 %copy-start.3 = (f32[32,256,128]{2,1,0:T(8,128)S(1)}, f32[32,256,128]{2,1,0:T(8,128)}, u32[]{:S(2)}) copy-start(f32[32,256,128]{2,1,0:T(8,128)} %get-tuple-element.13.h_ref) | copy-start | bytes 12582916
  71.7 1.1 copy-start.5

commit v3 on v2

--- a/solution.py
+++ b/solution.py
@@ -48,16 +48,20 @@
     return y * (2.0 - x * y)
 
 
-def over_rows(count, body, init=0, backward=False, most=8):
+def batches(lo, hi, most=11):
+    parts = -(-(hi - lo) // most)
+    cuts = [lo + (hi - lo) * k // parts for k in range(parts + 1)]
+    return [range(a, b) for a, b in zip(cuts, cuts[1:])]
+
+
+def over_rows(count, body, most=8):
     most = min(most, count)
-    parts = count // most
-
-    def step(k, carry):
-        start = (parts - 1 - k if backward else k) * most
-        rows = [start + i for i in range(most)]
-        return body(rows[::-1] if backward else rows, carry)
-
-    return lax.fori_loop(0, parts, step, init)
+
+    def step(k, _):
+        body(k * most, most)
+        return 0
+
+    lax.fori_loop(0, count // most, step, 0)
 
 
 def iotas():
@@ -75,18 +79,14 @@
         for u in range(G):
             r, _ = decay(d_ref[pl.ds(base + g * G + u, 1), :])
             rs.append(jnp.broadcast_to(r, (8, 128)))
-        zero = jnp.zeros((8, 128), F32)
-
-        def body(rows, carry):
-            fwd, bwd = list(carry[:G]), list(carry[G:])
-            for i in rows:
-                for u in range(G):
-                    fwd[u] = fwd[u] * rs[u] + f_ref[g * G + u, pl.ds(i, 8, stride=S), :]
-                    bwd[u] = bwd[u] * rs[u] + f_ref[g * G + u, pl.ds(S - 1 - i, 8, stride=S), :]
-            return (*fwd, *bwd)
-
-        carry = over_rows(S, body, (zero,) * (2 * G))
-        fwd, bwd = carry[:G], carry[G:]
+        fwd = [f_ref[g * G + u, pl.ds(0, 8, stride=S), :] for u in range(G)]
+        bwd, weight = list(fwd), list(rs)
+        for i in range(1, S):
+            for u in range(G):
+                x = f_ref[g * G + u, pl.ds(i, 8, stride=S), :]
+                fwd[u] = fwd[u] * rs[u] + x
+                bwd[u] = bwd[u] + weight[u] * x
+                weight[u] = weight[u] * rs[u]
         for u in range(G):
             k = g * G + u
             seg_ref[0, k] = fwd[u]
@@ -250,29 +250,23 @@
         gain.append(a0)
         y.append(c)
         z.append(b)
-    def forward(rows, y):
-        y, done = list(y), []
+    for rows in batches(0, S, 8):
+        done = []
         for i in rows:
             for u in range(tb):
                 y[u] = y[u] * rs[u] + f_ref[u, pl.ds(i, 8, stride=S), :]
                 done.append((u, i, y[u]))
         for u, i, value in done:
             ys[u, i] = value
-        return tuple(y)
-
-    def backward(rows, z):
-        z, done = list(z), []
-        for i in rows:
+    for rows in batches(0, S, 8)[::-1]:
+        done = []
+        for i in rows[::-1]:
             for u in range(tb):
                 zr = z[u] * rs[u]
                 done.append((u, i, gain[u] * (ys[u, i] + zr)))
                 z[u] = zr + f_ref[u, pl.ds(i, 8, stride=S), :]
         for u, i, value in done:
             out_ref[u, pl.ds(i, 8, stride=S), :] = value
-        return tuple(z)
-
-    over_rows(S, forward, tuple(y))
-    over_rows(S, backward, tuple(z), backward=True)
 
     lane_n = lax.broadcasted_iota(jnp.int32, (n, 128), 1)
     group = lane_n >> 2
@@ -338,7 +332,7 @@
             pltpu.VMEM((n, 128), F32),
             pltpu.VMEM((tb, n // 8, 8, 128), F32),
         ],
-        compiler_params=pltpu.CompilerParams(vmem_limit_bytes=24 * MIB),
+        compiler_params=pltpu.CompilerParams(vmem_limit_bytes=60 * MIB),
         cost_estimate=pl.CostEstimate(flops=10 * T * n * 128, bytes_accessed=8 * T * n * 128, transcendentals=0),
         name="heat",
     )(d, *pqs, seg, prior, pk, lo7, hi7)
@@ -381,7 +375,7 @@
         ],
         out_shape=[jax.ShapeDtypeStruct((6, n, 128), F32), row, row],
         input_output_aliases={2: 1, 3: 2},
-        compiler_params=pltpu.CompilerParams(vmem_limit_bytes=16 * MIB),
+        compiler_params=pltpu.CompilerParams(vmem_limit_bytes=60 * MIB),
         cost_estimate=pl.CostEstimate(flops=0, bytes_accessed=40 * n * 128, transcendentals=0),
         name="corners",
     )(from_left, from_right, lo, hi)
@@ -394,122 +388,154 @@
     return 1.0 - w, a * v, a * f0, a * f1
 
 
-def sweep_kernel(
-    tb, n, v_ref, f_ref, p_ref, h_ref, lo_ref, hi_ref, r_ref, own_ref,
-    out_ref, yh1, yh2, xs, ws, v1s, cos,
-):
+def under(row, last_vector):
+    _, sub = iotas()
+    return jnp.where(sub == 0, row, pltpu.roll(last_vector, 1, 0))
+
+
+def over(row, first_vector):
+    _, sub = iotas()
+    return jnp.where(sub == 7, row, pltpu.roll(first_vector, 7, 0))
+
+
+def put(todo):
+    for ref, c, i, value in todo:
+        ref[c, i] = value
+
+
+def halo_rows(ref, S, low, high):
+    todo = []
+    for c in range(2):
+        for q in range(2):
+            todo.append((ref, c, q, under(low(2 * c + q), ref[c, S + q])))
+            todo.append((ref, c, S + 2 + q, over(high(2 * c + q), ref[c, q + 2])))
+    put(todo)
+
+
+def halo_coefficients(cos, S, low, high, get):
+    below = coefficients(*[under(low(4 + m), get(m, S - 1)) for m in range(4)])
+    above = coefficients(*[over(high(4 + m), get(m, 0)) for m in range(4)])
+    put([(cos, m, 0, below[m]) for m in range(4)] + [(cos, m, S + 1, above[m]) for m in range(4)])
+
+
+def strip_kernel(n, lo_ref, hi_ref, r_ref, own_ref, yh1, yh2, xs, ws, r1s, cos):
     S = n // 8
     T = lo_ref.shape[0] - 1
+    lane, _ = iotas()
+    slot = lane & 3
+    outer = (slot == 0) | (slot == 3)
+    sign = jnp.where(slot == 1, -0.25, 0.25)
+
+    def low(k):
+        return lo_ref[T, k : k + 1, :]
+
+    def high(k):
+        return hi_ref[T, k : k + 1, :]
+
+    def get(m, i):
+        return r_ref[2 + m, pl.ds(i, 8, stride=S), :]
+
+    def collect(t, carry):
+        own = lane >> 2 == t
+        return [
+            jnp.where(own, pltpu.roll(ref[t], (4 * t + 2) & 127, 1), acc)
+            for ref, acc in zip((lo_ref, hi_ref), carry)
+        ]
+
+    zero = jnp.zeros((8, 128), F32)
+    own_lo, own_hi = lax.fori_loop(0, T, collect, [zero, zero])
+    both_lo = jnp.where(outer, lo_ref[T], own_lo)
+    both_hi = jnp.where(outer, hi_ref[T], own_hi)
+
+    def load(start, m):
+        todo = []
+        for i in [start + j for j in range(m)]:
+            for c in range(2):
+                r = r_ref[c, pl.ds(i, 8, stride=S), :]
+                todo.append((xs, c, i + 2, r))
+                todo.append((ws, c, i + 2, jnp.where(outer, r, own_ref[c, pl.ds(i, 8, stride=S), :])))
+            co = coefficients(*[get(q, i) for q in range(4)])
+            todo += [(cos, q, i + 1, co[q]) for q in range(4)]
+        put(todo)
+
+    over_rows(S, load)
+    halo_rows(xs, S, low, high)
+    halo_rows(ws, S, lambda k: both_lo[k : k + 1, :], lambda k: both_hi[k : k + 1, :])
+    halo_coefficients(cos, S, low, high, get)
+
+    def relax(start, m):
+        r = [[xs[c, start + 1 + j] for c in range(2)] for j in range(m + 2)]
+        w = [[ws[c, start + 1 + j] for c in range(2)] for j in range(m + 2)]
+        todo = []
+        for j in range(m):
+            i = start + j
+            for c in range(2):
+                q = 0.25 * (w[j + 2][1 - c] - w[j][1 - c])
+                around = (
+                    r[j][c] + r[j + 2][c] + pltpu.roll(w[j + 1][c] + q, 127, 1) + pltpu.roll(w[j + 1][c] - q, 1, 1)
+                )
+                todo.append((yh1, c, i + 1, r[j + 1][c] + sign * (r[j + 2][1 - c] - r[j][1 - c])))
+                new = cos[0, i + 1] * r[j + 1][c] + cos[2 + c, i + 1] + cos[1, i + 1] * around
+                todo.append((r1s, c, i + 1, new))
+        put(todo)
+
+    over_rows(S, relax)
+    relax(-1, 1)
+    relax(S, 1)
+
+    def edges(start, m):
+        r = [[r1s[c, start + j] for c in range(2)] for j in range(m + 2)]
+        put(
+            [
+                (yh2, c, start + j, r[j + 1][c] + sign * (r[j + 2][1 - c] - r[j][1 - c]))
+                for j in range(m)
+                for c in range(2)
+            ]
+        )
+
+    over_rows(S, edges)
+
+
+def strips(lo, hi, r, pk):
+    n = r.shape[1]
+    S = n // 8
+    whole = lambda shape: pl.BlockSpec(shape, lambda g: (0,) * len(shape))
+    return pl.pallas_call(
+        functools.partial(strip_kernel, n),
+        grid=(1,),
+        in_specs=[whole(lo.shape), whole(hi.shape), whole(r.shape), whole((2, n, 128))],
+        out_specs=[whole((2, S + 2, 8, 128)), whole((2, S, 8, 128))],
+        out_shape=[
+            jax.ShapeDtypeStruct((2, S + 2, 8, 128), F32),
+            jax.ShapeDtypeStruct((2, S, 8, 128), F32),
+        ],
+        scratch_shapes=[
+            pltpu.VMEM((2, S + 4, 8, 128), F32),
+            pltpu.VMEM((2, S + 4, 8, 128), F32),
+            pltpu.VMEM((2, S + 2, 8, 128), F32),
+            pltpu.VMEM((4, S + 2, 8, 128), F32),
+        ],
+        compiler_params=pltpu.CompilerParams(vmem_limit_bytes=60 * MIB),
+        cost_estimate=pl.CostEstimate(flops=60 * n * 128, bytes_accessed=60 * n * 128, transcendentals=n * 128),
+        name="strips",
+    )(lo, hi, r, pk)
+
+
+def sweep_kernel(tb, n, v_ref, f_ref, p_ref, h_ref, lo_ref, hi_ref, yh1, yh2, out_ref, xs, v1s, cos):
+    S = n // 8
     step = pl.program_id(0)
-    lane, sub = iotas()
-    slot = lane & 3
+    lane, _ = iotas()
     first, last = lane == 0, lane == 127
-
-    def under(row, last_vector):
-        return jnp.where(sub == 0, row, pltpu.roll(last_vector, 1, 0))
-
-    def over(row, first_vector):
-        return jnp.where(sub == 7, row, pltpu.roll(first_vector, 7, 0))
-
-    def put(todo):
-        for ref, c, i, value in todo:
-            ref[c, i] = value
-
-    def halo_rows(ref, low, high):
-        todo = []
-        for c in range(2):
-            for q in range(2):
-                todo.append((ref, c, q, under(low(2 * c + q), ref[c, S + q])))
-                todo.append((ref, c, S + 2 + q, over(high(2 * c + q), ref[c, q + 2])))
-        put(todo)
-
-    def halo_coefficients(low, high, get):
-        below = coefficients(*[under(low(4 + m), get(m, S - 1)) for m in range(4)])
-        above = coefficients(*[over(high(4 + m), get(m, 0)) for m in range(4)])
-        put([(cos, m, 0, below[m]) for m in range(4)] + [(cos, m, S + 1, above[m]) for m in range(4)])
-
-    @pl.when(step == 0)
-    def _():
-        outer = (slot == 0) | (slot == 3)
-        sign = jnp.where(slot == 1, -0.25, 0.25)
-
-        def get(m, i):
-            return r_ref[2 + m, pl.ds(i, 8, stride=S), :]
-
-        def collect(t, carry):
-            own = lane >> 2 == t
-            return [
-                jnp.where(own, pltpu.roll(ref[t], (4 * t + 2) & 127, 1), acc)
-                for ref, acc in zip((lo_ref, hi_ref), carry)
-            ]
-
-        zero = jnp.zeros((8, 128), F32)
-        own_lo, own_hi = lax.fori_loop(0, T, collect, [zero, zero])
-        both_lo = jnp.where(outer, lo_ref[T], own_lo)
-        both_hi = jnp.where(outer, hi_ref[T], own_hi)
-
-        def load(rows, _):
-            todo = []
-            for i in rows:
-                for c in range(2):
-                    r = r_ref[c, pl.ds(i, 8, stride=S), :]
-                    todo.append((xs, c, i + 2, r))
-                    todo.append((ws, c, i + 2, jnp.where(outer, r, own_ref[c, pl.ds(i, 8, stride=S), :])))
-                co = coefficients(*[get(m, i) for m in range(4)])
-                todo += [(cos, m, i + 1, co[m]) for m in range(4)]
-            put(todo)
-            return 0
-
-        over_rows(S, load, most=4)
-        halo_rows(xs, lambda k: lo_ref[T, k : k + 1, :], lambda k: hi_ref[T, k : k + 1, :])
-        halo_rows(ws, lambda k: both_lo[k : k + 1, :], lambda k: both_hi[k : k + 1, :])
-        halo_coefficients(lambda k: lo_ref[T, k : k + 1, :], lambda k: hi_ref[T, k : k + 1, :], get)
-
-        def relax(rows, _):
-            todo = []
-            for i in rows:
-                r = [[xs[c, i + d] for c in range(2)] for d in (1, 2, 3)]
-                w = [[ws[c, i + d] for c in range(2)] for d in (1, 2, 3)]
-                for c in range(2):
-                    q = 0.25 * (w[2][1 - c] - w[0][1 - c])
-                    around = (
-                        r[0][c] + r[2][c] + pltpu.roll(w[1][c] + q, 127, 1) + pltpu.roll(w[1][c] - q, 1, 1)
-                    )
-                    todo.append((yh1, c, i + 1, r[1][c] + sign * (r[2][1 - c] - r[0][1 - c])))
-                    new = cos[0, i + 1] * r[1][c] + cos[2 + c, i + 1] + cos[1, i + 1] * around
-                    todo.append((v1s, c, i + 1, new))
-            put(todo)
-            return 0
-
-        over_rows(S, relax, most=4)
-        relax([-1, S], 0)
-
-        def edges(rows, _):
-            put(
-                [
-                    (yh2, c, i, v1s[c, i + 1] + sign * (v1s[1 - c, i + 2] - v1s[1 - c, i]))
-                    for i in rows
-                    for c in range(2)
-                ]
-            )
-            return 0
-
-        over_rows(S, edges)
 
     def layer(u, _):
         t = step * tb + u
         shift = (126 - 4 * t) & 127
 
-        def update(prev, here, after, i, yh):
-            q = [0.25 * (after[c] - prev[c]) for c in range(2)]
-            new = []
-            for c in range(2):
-                edge = pltpu.roll(yh[c], shift, 1)
-                up = jnp.where(first, edge, here[c] + q[1 - c])
-                down = jnp.where(last, edge, here[c] - q[1 - c])
-                around = prev[c] + after[c] + (pltpu.roll(up, 127, 1) + pltpu.roll(down, 1, 1))
-                new.append(cos[0, i + 1] * here[c] + cos[2 + c, i + 1] + cos[1, i + 1] * around)
-            return new
+        def low(k):
+            return lo_ref[t, k : k + 1, :]
+
+        def high(k):
+            return hi_ref[t, k : k + 1, :]
 
         def get(m, i):
             rows = pl.ds(i, 8, stride=S)
@@ -517,51 +543,54 @@
                 return f_ref[m, u, rows, :]
             return 1.0 - p_ref[u, rows, :].astype(F32) if m == 2 else h_ref[u, rows, :]
 
-        def load(rows, _):
+        def load(start, m):
             todo = []
-            for i in rows:
+            for i in [start + j for j in range(m)]:
                 todo += [(xs, c, i + 2, v_ref[c, u, pl.ds(i, 8, stride=S), :]) for c in range(2)]
-                co = coefficients(*[get(m, i) for m in range(4)])
-                todo += [(cos, m, i + 1, co[m]) for m in range(4)]
+                co = coefficients(*[get(q, i) for q in range(4)])
+                todo += [(cos, q, i + 1, co[q]) for q in range(4)]
             put(todo)
-            return 0
-
-        over_rows(S, load)
-        halo_rows(xs, lambda k: lo_ref[t, k : k + 1, :], lambda k: hi_ref[t, k : k + 1, :])
-        halo_coefficients(lambda k: lo_ref[t, k : k + 1, :], lambda k: hi_ref[t, k : k + 1, :], get)
-
-        def first_sweep(rows, _):
-            todo = []
-            for i in rows:
-                x = [[xs[c, i + d] for c in range(2)] for d in (1, 2, 3)]
-                new = update(*x, i, [yh1[c, i + 1] for c in range(2)])
-                todo += [(v1s, c, i + 1, new[c]) for c in range(2)]
-            put(todo)
-            return 0
-
-        over_rows(S, first_sweep)
-        first_sweep([-1, S], 0)
-
-        def second_sweep(rows, _):
-            todo = []
-            for i in rows:
-                x = [[v1s[c, i + d] for c in range(2)] for d in (0, 1, 2)]
-                new = update(*x, i, [yh2[c, i] for c in range(2)])
-                todo += [(c, i, new[c]) for c in range(2)]
-            for c, i, value in todo:
+
+        def sweep(src, off, yh, start, m):
+            x = [[src[c, start + off + j] for c in range(2)] for j in range(m + 2)]
+            done = []
+            for j in range(m):
+                i = start + j
+                prev, here, after = x[j], x[j + 1], x[j + 2]
+                q = [0.25 * (after[c] - prev[c]) for c in range(2)]
+                k, g = cos[0, i + 1], cos[1, i + 1]
+                for c in range(2):
+                    edge = pltpu.roll(yh[c, i + off], shift, 1)
+                    up = jnp.where(first, edge, here[c] + q[1 - c])
+                    down = jnp.where(last, edge, here[c] - q[1 - c])
+                    around = prev[c] + after[c] + (pltpu.roll(up, 127, 1) + pltpu.roll(down, 1, 1))
+                    done.append((c, i, k * here[c] + cos[2 + c, i + 1] + g * around))
+            return done
+
+        def first_sweep(start, m):
+            put([(v1s, c, i + 1, value) for c, i, value in sweep(xs, 1, yh1, start, m)])
+
+        def second_sweep(start, m):
+            for c, i, value in sweep(v1s, 0, yh2, start, m):
                 out_ref[c, u, pl.ds(i, 8, stride=S), :] = value
-            return 0
-
-        over_rows(S, second_sweep)
+
+        over_rows(S, load, 16)
+        halo_rows(xs, S, low, high)
+        halo_coefficients(cos, S, low, high, get)
+        over_rows(S, first_sweep, 16)
+        first_sweep(-1, 1)
+        first_sweep(S, 1)
+        over_rows(S, second_sweep, 16)
         return 0
 
     lax.fori_loop(0, tb, layer, 0)
 
 
-def sweeps(v, f, pinned, heated, lo, hi, r, pk):
+def sweeps(v, f, pinned, heated, lo, hi, yh1, yh2):
     _, T, n, _ = v.shape
     S = n // 8
     tb = 2
+    whole = lambda shape: pl.BlockSpec(shape, lambda t: (0,) * len(shape))
     return pl.pallas_call(
         functools.partial(sweep_kernel, tb, n),
         grid=(T // tb,),
@@ -570,25 +599,24 @@
             pl.BlockSpec((2, tb, n, 128), lambda t: (0, t, 0, 0)),
             pl.BlockSpec((tb, n, 128), lambda t: (t, 0, 0)),
             pl.BlockSpec((tb, n, 128), lambda t: (t, 0, 0)),
-            pl.BlockSpec((T + 1, 8, 128), lambda t: (0, 0, 0)),
-            pl.BlockSpec((T + 1, 8, 128), lambda t: (0, 0, 0)),
-            pl.BlockSpec((6, n, 128), lambda t: (0, 0, 0)),
-            pl.BlockSpec((2, n, 128), lambda t: (0, 0, 0)),
+            whole((T + 1, 8, 128)),
+            whole((T + 1, 8, 128)),
+            whole((2, S + 2, 8, 128)),
+            whole((2, S, 8, 128)),
         ],
         out_specs=pl.BlockSpec((2, tb, n, 128), lambda t: (0, t, 0, 0)),
         out_shape=jax.ShapeDtypeStruct((2, T, n, 128), F32),
         scratch_shapes=[
-            pltpu.VMEM((2, S + 2, 8, 128), F32),
-            pltpu.VMEM((2, S, 8, 128), F32),
-            pltpu.VMEM((2, S + 4, 8, 128), F32),
             pltpu.VMEM((2, S + 4, 8, 128), F32),
             pltpu.VMEM((2, S + 2, 8, 128), F32),
             pltpu.VMEM((4, S + 2, 8, 128), F32),
         ],
-        compiler_params=pltpu.CompilerParams(vmem_limit_bytes=32 * MIB),
-        cost_estimate=pl.CostEstimate(flops=60 * T * n * 128, bytes_accessed=32 * T * n * 128, transcendentals=T * n * 128),
+        compiler_params=pltpu.CompilerParams(vmem_limit_bytes=60 * MIB),
+        cost_estimate=pl.CostEstimate(
+            flops=60 * T * n * 128, bytes_accessed=32 * T * n * 128, transcendentals=T * n * 128
+        ),
         name="sweeps",
-    )(v, f, pinned, heated, lo, hi, r, pk)
+    )(v, f, pinned, heated, lo, hi, yh1, yh2)
 
 
 def shifted(up_going, down_going, axis):
@@ -607,7 +635,8 @@
     from_left, from_right = shifted(right, left, "len")
     r, lo, hi = corners(from_left, from_right, lo, hi)
     from_below, from_above = shifted(hi, lo, "wid")
-    flow = sweeps(v, f, pinned, heated, from_below, from_above, r, pk)
+    yh1, yh2 = strips(from_below, from_above, r, pk)
+    flow = sweeps(v, f, pinned, heated, from_below, from_above, yh1, yh2)
     return heated, flow
 
 

time: 151 us -> 123 us (0.81)
  Pallas kernels: 110 us -> 92.3 us
  local copies, waits for them, and re-layouts: 12 us -> 1.94 us
    pallas_call x1, Pallas kernels: 77.8 us -> 55.1 us  [sweeps(): pl.pallas_call(functools.partial(sweep_kernel, tb, n), grid=(T // tb,), i...]
    unnamed x22 -> x14, local copies, waits for them, and re-layouts: 12 us -> 1.94 us
    pallas_call x0 -> x1, Pallas kernels: none -> 5.79 us  [strips(): pl.pallas_call(functools.partial(strip_kernel, n), grid=(1,), in_specs=[w...]
    pallas_call x1, Pallas kernels: 7.26 us -> 5.02 us  [moments(): pl.pallas_call(functools.partial(moments_kernel, tb, n), grid=(T // tb,),...]
    pallas_call x1, Pallas kernels: 0.35 us -> 2.26 us  [corners(): pl.pallas_call(functools.partial(corner_kernel, n), grid=(1,), in_specs=[...]
  transfers between devices with their start and end apart: 7 -> 7, of which waited for: 4 -> 4; matrix products, arithmetic and copies ran while one was open for 0% -> 0% of each run, Pallas kernels for 9% -> 10%
where the time goes in v3:
time: 123 us
  Pallas kernels  92.3 us (75%)
  starting transfers between devices  16.7 us (14%)
  waiting for transfers between devices  11 us (9%)
  local copies, waits for them, and re-layouts  1.94 us (2%)
    pallas_call x1, Pallas kernels, sweeps(): pl.pallas_call(functools.partial(sweep_kernel, tb, n), grid=(T // tb,), i...  55.1 us
    pallas_call x1, Pallas kernels, pack(): pl.pallas_call(functools.partial(pack_kernel, tb, n), grid=(T // tb,), in...  12.8 us
    pallas_call x1, Pallas kernels, heat(): pl.pallas_call(functools.partial(heat_kernel, J, tb, n), grid=(T // tb,),...  11.3 us
    ppermute x2, starting transfers between devices, shifted(): lax.ppermute(up_going, axis, up)  6.3 us
    ppermute x2, waiting for transfers between devices, shifted(): lax.ppermute(down_going, axis, down)  5.87 us
    ppermute x2, starting transfers between devices, shifted(): lax.ppermute(down_going, axis, down)  5.83 us
    pallas_call x1, Pallas kernels, strips(): pl.pallas_call(functools.partial(strip_kernel, n), grid=(1,), in_specs=[w...  5.79 us
    ppermute x2, waiting for transfers between devices, shifted(): lax.ppermute(up_going, axis, up)  5.09 us
  transfers between devices with their start and end apart: 7, of which 4 were waited for; matrix products, arithmetic and copies ran while one was open for 0% of the time, Pallas kernels for 10%

profile of v3, /device:TPU:4, one launch (start us, length us, event | category | flops | bytes accessed | tf_op | source)
XLA Modules:
  0.0 122.6 jit_solution(16898521052791349168)
XLA Ops:
  0.6 5.0 %moments.1 = (f32[2,32,8,128]{3,2,1,0:T(8,128)}, f32[2,32,128]{2,1,0:T(8,128)}) custom-call(f32[32,128]{1,0:T(8,128)} %refs_0_.1, f32[32,256,128]{2,1,0:T(8,128)} %refs_6_.1), custom_call_target="tpu_custom_call" | custom-call | flops 4194304 | bytes 4194304 | tf_op jit(solution)/shard_map/moments/pallas_call | solution.py:111
  5.6 3.6 %collective-permute-start.2 = (f32[2,32,128]{2,1,0:T(8,128)}, f32[2,32,128]{2,1,0:T(8,128)S(1)}, u32[]{:S(2)}, u32[]{:S(2)}) collective-permute-start(f32[2,32,128]{2,1,0:T(8,128)} %get-tuple-element.17.refs_1_), channel_id=1, source_target_pairs={{0,3},{1,0},{2,1},{3,2},{4,7},{5,4},{6,5},{7,6},{8,11},{9,8},{10,9... | collective-permute-start | bytes 98312 | tf_op jit(solution)/shard_map/ppermute | solution.py:632
  9.2 0.0 collective-permute-start.1
  9.3 1.0 collective-permute-start
  10.3 12.8 %pack_edges.1 = (f32[5,256,128]{2,1,0:T(8,128)}, f32[32,8,128]{2,1,0:T(8,128)}, f32[32,8,128]{2,1,0:T(8,128)}) custom-call(f32[2,32,256,128]{3,2,1,0:T(8,128)} %v_ref.3, f32[2,32,256,128]{3,2,1,0:T(8,128)} %f_ref.5, s32[32,256,128]{2,1,0:T(8,128)} %p_ref.3), custom_call_target="tpu_custom_call" | custom-call | flops 5242880 | bytes 20971520 | tf_op jit(solution)/shard_map/pack_edges/pallas_call | solution.py:180
  23.1 0.0 collective-permute-done.2.refs_4_
  23.1 0.0 copy-start.4
  23.1 0.0 collective-permute-done.1.refs_3_
  23.1 0.0 copy-start.5
  23.1 0.0 collective-permute-done.refs_2_
  23.1 0.0 copy-start.6
  23.1 0.6 copy-done.4
  23.7 0.0 copy-done.5
  23.7 0.0 copy-done.6
  23.7 11.3 %heat.1 = (f32[32,256,128]{2,1,0:T(8,128)}, f32[2,256,128]{2,1,0:T(8,128)}, f32[2,256,128]{2,1,0:T(8,128)}, f32[33,8,128]{2,1,0:T(8,128)}, f32[33,8,128]{2,1,0:T(8,128)}) custom-call(f32[32,128]{1,0:T(8,128)} %refs_0_.1, f32[2,32,128]{2,1,0:T(8,128)} %get-tuple-element.17.refs_1_, f32[2,32,128]{2,1,0:T(8,128)} %copy-done.6, f32[2,32,128]{2,1,0:T(8,128)} %copy-done.5, ...), custom_call_target="tpu_custom_call" | custom-call | flops 10485760 | bytes 8388608 | tf_op jit(solution)/shard_map/heat/pallas_call | solution.py:303
  35.0 1.9 %collective-permute-start.3 = (f32[2,256,128]{2,1,0:T(8,128)}, f32[2,256,128]{2,1,0:T(8,128)S(1)}, u32[]{:S(2)}, u32[]{:S(2)}) collective-permute-start(f32[2,256,128]{2,1,0:T(8,128)} %get-tuple-element.23), channel_id=1, source_target_pairs={{0,4},{4,8},{8,12},{12,16},{16,20},{20,24},{24,28},{1,5},{5,9},{9,... | collective-permute-start | bytes 786440 | tf_op jit(solution)/shard_map/ppermute | solution.py:626
  37.0 4.5 %collective-permute-start.4 = (f32[2,256,128]{2,1,0:T(8,128)}, f32[2,256,128]{2,1,0:T(8,128)S(1)}, u32[]{:S(2)}, u32[]{:S(2)}) collective-permute-start(f32[2,256,128]{2,1,0:T(8,128)} %get-tuple-element.24), channel_id=1, source_target_pairs={{4,0},{8,4},{12,8},{16,12},{20,16},{24,20},{28,24},{5,1},{9,5},{13... | collective-permute-start | bytes 786440 | tf_op jit(solution)/shard_map/ppermute | solution.py:626
  41.5 2.3 %collective-permute-done.3.fl_ref = f32[2,256,128]{2,1,0:T(8,128)S(1)} collective-permute-done((f32[2,256,128]{2,1,0:T(8,128)}, f32[2,256,128]{2,1,0:T(8,128)S(1)}, u32[]{:S(2)}, u32[]{:S(2)}) %collective-permute-start.3) | collective-permute-done | bytes 262176 | tf_op jit(solution)/shard_map/ppermute | solution.py:626
  43.8 0.0 copy-start.2
  43.8 1.9 %collective-permute-done.4.fr_ref = f32[2,256,128]{2,1,0:T(8,128)S(1)} collective-permute-done((f32[2,256,128]{2,1,0:T(8,128)}, f32[2,256,128]{2,1,0:T(8,128)S(1)}, u32[]{:S(2)}, u32[]{:S(2)}) %collective-permute-start.4) | collective-permute-done | bytes 262176 | tf_op jit(solution)/shard_map/ppermute | solution.py:626
  45.7 0.0 copy-start.3
  45.7 0.0 copy-done.2
  45.7 0.7 copy-done.3
  46.4 2.3 %corners.1 = (f32[6,256,128]{2,1,0:T(8,128)}, f32[33,8,128]{2,1,0:T(8,128)}, f32[33,8,128]{2,1,0:T(8,128)}) custom-call(f32[2,256,128]{2,1,0:T(8,128)} %copy-done.2, f32[2,256,128]{2,1,0:T(8,128)} %copy-done.3, f32[33,8,128]{2,1,0:T(8,128)} %get-tuple-element.25.lo_in, ...), custom_call_target="tpu_custom_call", output_to_operand_aliasing={{1}: (2, {}), {2}: (3, {})} | custom-call | bytes 1310720 | tf_op jit(solution)/shard_map/corners/pallas_call | solution.py:362
  48.6 4.4 %collective-permute-start.5 = (f32[33,8,128]{2,1,0:T(8,128)}, f32[33,8,128]{2,1,0:T(8,128)S(1)}, u32[]{:S(2)}, u32[]{:S(2)}) collective-permute-start(f32[33,8,128]{2,1,0:T(8,128)} %get-tuple-element.27), channel_id=1, source_target_pairs={{0,1},{1,2},{2,3},{4,5},{5,6},{6,7},{8,9},{9,10},{10,11},{12,13},{... | collective-permute-start | bytes 405512 | tf_op jit(solution)/shard_map/ppermute | solution.py:626
  53.0 1.3 %collective-permute-start.6 = (f32[33,8,128]{2,1,0:T(8,128)}, f32[33,8,128]{2,1,0:T(8,128)S(1)}, u32[]{:S(2)}, u32[]{:S(2)}) collective-permute-start(f32[33,8,128]{2,1,0:T(8,128)} %get-tuple-element.28), channel_id=1, source_target_pairs={{1,0},{2,1},{3,2},{5,4},{6,5},{7,6},{9,8},{10,9},{11,10},{13,12},{... | collective-permute-start | bytes 405512 | tf_op jit(solution)/shard_map/ppermute | solution.py:626
  54.3 2.8 %collective-permute-done.5.lo_ref = f32[33,8,128]{2,1,0:T(8,128)S(1)} collective-permute-done((f32[33,8,128]{2,1,0:T(8,128)}, f32[33,8,128]{2,1,0:T(8,128)S(1)}, u32[]{:S(2)}, u32[]{:S(2)}) %collective-permute-start.5) | collective-permute-done | bytes 135200 | tf_op jit(solution)/shard_map/ppermute | solution.py:626
  57.1 0.0 copy-start
  57.1 4.0 %collective-permute-done.6.hi_ref = f32[33,8,128]{2,1,0:T(8,128)S(1)} collective-permute-done((f32[33,8,128]{2,1,0:T(8,128)}, f32[33,8,128]{2,1,0:T(8,128)S(1)}, u32[]{:S(2)}, u32[]{:S(2)}) %collective-permute-start.6) | collective-permute-done | bytes 135200 | tf_op jit(solution)/shard_map/ppermute | solution.py:626
  61.1 0.0 copy-start.1
  61.1 0.0 copy-done
  61.1 0.6 copy-done.1
  61.7 5.8 %strips.1 = (f32[2,34,8,128]{3,2,1,0:T(8,128)}, f32[2,32,8,128]{3,2,1,0:T(8,128)}) custom-call(f32[33,8,128]{2,1,0:T(8,128)} %copy-done, f32[33,8,128]{2,1,0:T(8,128)} %copy-done.1, f32[6,256,128]{2,1,0:T(8,128)} %get-tuple-element.29.r_ref, f32[5,256,128]{2,1,0:T(8,128)} %get-tuple-element.19.refs_7_.own_ref), custom_call_target="tpu_custom_call" | custom-call | flops 1966080 | bytes 1966080 | tf_op jit(solution)/shard_map/strips/pallas_call | solution.py:503
  67.5 55.1 %sweeps.1 = f32[2,32,256,128]{3,2,1,0:T(8,128)} custom-call(f32[2,32,256,128]{3,2,1,0:T(8,128)} %v_ref.3, f32[2,32,256,128]{3,2,1,0:T(8,128)} %f_ref.5, s32[32,256,128]{2,1,0:T(8,128)} %p_ref.3, f32[32,256,128]{2,1,0:T(8,128)} %get-tuple-element.15.h_ref, f32[33,8,128]{2,1,0:T(8,128)} %copy-done, f32[33,8,128]{2,1,0:T(8,128)} %copy-done.1, ...), custom_call_target="tpu_custom_call" | custom-call | flops 62914560 | bytes 33554432 | tf_op jit(solution)/shard_map/sweeps/pallas_call | solution.py:594
Async XLA Ops:
  5.6 17.5 %collective-permute-start.2 = (f32[2,32,128]{2,1,0:T(8,128)}, f32[2,32,128]{2,1,0:T(8,128)S(1)}, u32[]{:S(2)}, u32[]{:S(2)}) collective-permute-start(f32[2,32,128]{2,1,0:T(8,128)} %get-tuple-element.17.refs_1_), channel_id=1, source_target_pairs={{0,3},{1,0},{2,1},{3,2},{4,7},{5,4},{6,5},{7,6},{8,11},{9,8},{10,9... | collective-permute-start | bytes 98312 | tf_op jit(solution)/shard_map/ppermute | solution.py:632
  9.2 13.9 %collective-permute-start.1 = (f32[2,32,128]{2,1,0:T(8,128)}, f32[2,32,128]{2,1,0:T(8,128)S(1)}, u32[]{:S(2)}, u32[]{:S(2)}) collective-permute-start(f32[2,32,128]{2,1,0:T(8,128)} %get-tuple-element.17.refs_1_), channel_id=1, source_target_pairs={{0,2},{1,3},{2,0},{3,1},{4,6},{5,7},{6,4},{7,5},{8,10},{9,11},{10,... | collective-permute-start | bytes 98312 | tf_op jit(solution)/shard_map/ppermute | solution.py:632
  9.3 13.9 %collective-permute-start = (f32[2,32,128]{2,1,0:T(8,128)}, f32[2,32,128]{2,1,0:T(8,128)S(1)}, u32[]{:S(2)}, u32[]{:S(2)}) collective-permute-start(f32[2,32,128]{2,1,0:T(8,128)} %get-tuple-element.17.refs_1_), channel_id=1, source_target_pairs={{0,1},{1,2},{2,3},{3,0},{4,5},{5,6},{6,7},{7,4},{8,9},{9,10},{10,1... | collective-permute-start | bytes 98312 | tf_op jit(solution)/shard_map/ppermute | solution.py:632
  23.1 0.6 copy-start.4
  23.1 0.6 copy-start.5
  23.1 0.6 copy-start.6
  35.0 8.8 %collective-permute-start.3 = (f32[2,256,128]{2,1,0:T(8,128)}, f32[2,256,128]{2,1,0:T(8,128)S(1)}, u32[]{:S(2)}, u32[]{:S(2)}) collective-permute-start(f32[2,256,128]{2,1,0:T(8,128)} %get-tuple-element.23), channel_id=1, source_target_pairs={{0,4},{4,8},{8,12},{12,16},{16,20},{20,24},{24,28},{1,5},{5,9},{9,... | collective-permute-start | bytes 786440 | tf_op jit(solution)/shard_map/ppermute | solution.py:626
  37.0 8.7 %collective-permute-start.4 = (f32[2,256,128]{2,1,0:T(8,128)}, f32[2,256,128]{2,1,0:T(8,128)S(1)}, u32[]{:S(2)}, u32[]{:S(2)}) collective-permute-start(f32[2,256,128]{2,1,0:T(8,128)} %get-tuple-element.24), channel_id=1, source_target_pairs={{4,0},{8,4},{12,8},{16,12},{20,16},{24,20},{28,24},{5,1},{9,5},{13... | collective-permute-start | bytes 786440 | tf_op jit(solution)/shard_map/ppermute | solution.py:626
  43.8 1.9 %copy-start.2 = (f32[2,256,128]{2,1,0:T(8,128)}, f32[2,256,128]{2,1,0:T(8,128)S(1)}, u32[]{:S(2)}) copy-start(f32[2,256,128]{2,1,0:T(8,128)S(1)} %collective-permute-done.3.fl_ref) | copy-start | bytes 786436
  45.7 0.7 copy-start.3
  48.6 8.4 %collective-permute-start.5 = (f32[33,8,128]{2,1,0:T(8,128)}, f32[33,8,128]{2,1,0:T(8,128)S(1)}, u32[]{:S(2)}, u32[]{:S(2)}) collective-permute-start(f32[33,8,128]{2,1,0:T(8,128)} %get-tuple-element.27), channel_id=1, source_target_pairs={{0,1},{1,2},{2,3},{4,5},{5,6},{6,7},{8,9},{9,10},{10,11},{12,13},{... | collective-permute-start | bytes 405512 | tf_op jit(solution)/shard_map/ppermute | solution.py:626
  53.0 8.1 %collective-permute-start.6 = (f32[33,8,128]{2,1,0:T(8,128)}, f32[33,8,128]{2,1,0:T(8,128)S(1)}, u32[]{:S(2)}, u32[]{:S(2)}) collective-permute-start(f32[33,8,128]{2,1,0:T(8,128)} %get-tuple-element.28), channel_id=1, source_target_pairs={{1,0},{2,1},{3,2},{5,4},{6,5},{7,6},{9,8},{10,9},{11,10},{13,12},{... | collective-permute-start | bytes 405512 | tf_op jit(solution)/shard_map/ppermute | solution.py:626
  57.1 4.0 %copy-start = (f32[33,8,128]{2,1,0:T(8,128)}, f32[33,8,128]{2,1,0:T(8,128)S(1)}, u32[]{:S(2)}) copy-start(f32[33,8,128]{2,1,0:T(8,128)S(1)} %collective-permute-done.5.lo_ref) | copy-start | bytes 405508
  61.1 0.6 copy-start.1

commit v4 on v3

--- a/solution.py
+++ b/solution.py
@@ -54,14 +54,15 @@
     return [range(a, b) for a, b in zip(cuts, cuts[1:])]
 
 
-def over_rows(count, body, most=8):
-    most = min(most, count)
+def over_rows(first, stop, body, most=8):
+    count = stop - first
+    m = max(k for k in range(1, most + 1) if count % k == 0)
 
     def step(k, _):
-        body(k * most, most)
+        body(first + k * m, m)
         return 0
 
-    lax.fori_loop(0, count // most, step, 0)
+    lax.fori_loop(0, count // m, step, 0)
 
 
 def iotas():
@@ -131,29 +132,20 @@
 
 def pack_kernel(tb, n, v_ref, f_ref, p_ref, pk_ref, lo_ref, hi_ref):
     base = pl.program_id(0) * tb
-    chunk = min(64, n)
-    group = lax.broadcasted_iota(jnp.int32, (chunk, 128), 1) >> 2
-
-    def body(m, _):
-        rows = pl.ds(pl.multiple_of(m * chunk, chunk), chunk)
-        packed = []
-        for k in range(5):
-            acc = pk_ref[k, rows, :]
-            for u in range(tb):
-                if k < 2:
-                    x = v_ref[k, u, rows, :]
-                elif k < 4:
-                    x = f_ref[k - 2, u, rows, :]
-                else:
-                    x = 1.0 - p_ref[u, rows, :].astype(F32)
-                t = base + u
-                acc = jnp.where(group == t, pltpu.roll(x, (4 * t + 2) & 127, 1), acc)
-            packed.append(acc)
-        for k in range(5):
-            pk_ref[k, rows, :] = packed[k]
-        return 0
-
-    lax.fori_loop(0, n // chunk, body, 0)
+    lane = lax.broadcasted_iota(jnp.int32, (n, 128), 1)
+    group = lane >> 2
+    for k in range(5):
+        acc = pk_ref[k]
+        for u in range(tb):
+            if k < 2:
+                x = v_ref[k, u]
+            elif k < 4:
+                x = f_ref[k - 2, u]
+            else:
+                x = 1.0 - p_ref[u].astype(F32)
+            t = base + u
+            acc = jnp.where(group == t, pltpu.roll(x, (4 * t + 2) & 127, 1), acc)
+        pk_ref[k] = acc
     _, sub = iotas()
 
     def stack(v0, v1, f0, f1, fr):
@@ -375,7 +367,7 @@
         ],
         out_shape=[jax.ShapeDtypeStruct((6, n, 128), F32), row, row],
         input_output_aliases={2: 1, 3: 2},
-        compiler_params=pltpu.CompilerParams(vmem_limit_bytes=60 * MIB),
+        compiler_params=pltpu.CompilerParams(vmem_limit_bytes=8 * MIB),
         cost_estimate=pl.CostEstimate(flops=0, bytes_accessed=40 * n * 128, transcendentals=0),
         name="corners",
     )(from_left, from_right, lo, hi)
@@ -403,19 +395,19 @@
         ref[c, i] = value
 
 
-def halo_rows(ref, S, low, high):
+def halo_rows(ref, S, low, high, get):
     todo = []
     for c in range(2):
         for q in range(2):
-            todo.append((ref, c, q, under(low(2 * c + q), ref[c, S + q])))
-            todo.append((ref, c, S + 2 + q, over(high(2 * c + q), ref[c, q + 2])))
-    put(todo)
+            todo.append((ref, c, q, under(low(2 * c + q), get(c, S - 2 + q))))
+            todo.append((ref, c, S + 2 + q, over(high(2 * c + q), get(c, q))))
+    return todo
 
 
 def halo_coefficients(cos, S, low, high, get):
     below = coefficients(*[under(low(4 + m), get(m, S - 1)) for m in range(4)])
     above = coefficients(*[over(high(4 + m), get(m, 0)) for m in range(4)])
-    put([(cos, m, 0, below[m]) for m in range(4)] + [(cos, m, S + 1, above[m]) for m in range(4)])
+    return [(cos, m, 0, below[m]) for m in range(4)] + [(cos, m, S + 1, above[m]) for m in range(4)]
 
 
 def strip_kernel(n, lo_ref, hi_ref, r_ref, own_ref, yh1, yh2, xs, ws, r1s, cos):
@@ -435,15 +427,15 @@
     def get(m, i):
         return r_ref[2 + m, pl.ds(i, 8, stride=S), :]
 
-    def collect(t, carry):
-        own = lane >> 2 == t
-        return [
-            jnp.where(own, pltpu.roll(ref[t], (4 * t + 2) & 127, 1), acc)
-            for ref, acc in zip((lo_ref, hi_ref), carry)
+    def collect(ref):
+        parts = [
+            jnp.where(lane >> 2 == t, pltpu.roll(ref[t], (4 * t + 2) & 127, 1), 0.0) for t in range(T)
         ]
-
-    zero = jnp.zeros((8, 128), F32)
-    own_lo, own_hi = lax.fori_loop(0, T, collect, [zero, zero])
+        while len(parts) > 1:
+            parts = [p + q for p, q in zip(parts[::2], parts[1::2])]
+        return parts[0]
+
+    own_lo, own_hi = collect(lo_ref), collect(hi_ref)
     both_lo = jnp.where(outer, lo_ref[T], own_lo)
     both_hi = jnp.where(outer, hi_ref[T], own_hi)
 
@@ -458,10 +450,24 @@
             todo += [(cos, q, i + 1, co[q]) for q in range(4)]
         put(todo)
 
-    over_rows(S, load)
-    halo_rows(xs, S, low, high)
-    halo_rows(ws, S, lambda k: both_lo[k : k + 1, :], lambda k: both_hi[k : k + 1, :])
-    halo_coefficients(cos, S, low, high, get)
+    over_rows(0, S, load)
+    def row_low(k):
+        return both_lo[k : k + 1, :]
+
+    def row_high(k):
+        return both_hi[k : k + 1, :]
+
+    def get_r(c, i):
+        return r_ref[c, pl.ds(i, 8, stride=S), :]
+
+    def get_w(c, i):
+        return jnp.where(outer, get_r(c, i), own_ref[c, pl.ds(i, 8, stride=S), :])
+
+    put(
+        halo_rows(xs, S, low, high, get_r)
+        + halo_rows(ws, S, row_low, row_high, get_w)
+        + halo_coefficients(cos, S, low, high, get)
+    )
 
     def relax(start, m):
         r = [[xs[c, start + 1 + j] for c in range(2)] for j in range(m + 2)]
@@ -479,9 +485,7 @@
                 todo.append((r1s, c, i + 1, new))
         put(todo)
 
-    over_rows(S, relax)
-    relax(-1, 1)
-    relax(S, 1)
+    over_rows(-1, S + 1, relax, 17)
 
     def edges(start, m):
         r = [[r1s[c, start + j] for c in range(2)] for j in range(m + 2)]
@@ -493,7 +497,7 @@
             ]
         )
 
-    over_rows(S, edges)
+    over_rows(0, S, edges, 16)
 
 
 def strips(lo, hi, r, pk):
@@ -515,7 +519,7 @@
             pltpu.VMEM((2, S + 2, 8, 128), F32),
             pltpu.VMEM((4, S + 2, 8, 128), F32),
         ],
-        compiler_params=pltpu.CompilerParams(vmem_limit_bytes=60 * MIB),
+        compiler_params=pltpu.CompilerParams(vmem_limit_bytes=8 * MIB),
         cost_estimate=pl.CostEstimate(flops=60 * n * 128, bytes_accessed=60 * n * 128, transcendentals=n * 128),
         name="strips",
     )(lo, hi, r, pk)
@@ -574,13 +578,13 @@
             for c, i, value in sweep(v1s, 0, yh2, start, m):
                 out_ref[c, u, pl.ds(i, 8, stride=S), :] = value
 
-        over_rows(S, load, 16)
-        halo_rows(xs, S, low, high)
-        halo_coefficients(cos, S, low, high, get)
-        over_rows(S, first_sweep, 16)
-        first_sweep(-1, 1)
-        first_sweep(S, 1)
-        over_rows(S, second_sweep, 16)
+        put(
+            halo_rows(xs, S, low, high, lambda c, i: v_ref[c, u, pl.ds(i, 8, stride=S), :])
+            + halo_coefficients(cos, S, low, high, get)
+        )
+        over_rows(0, S, load, 16)
+        over_rows(-1, S + 1, first_sweep, 17)
+        over_rows(0, S, second_sweep, 16)
         return 0
 
     lax.fori_loop(0, tb, layer, 0)

time: 123 us -> 116 us (0.943)
  Pallas kernels: 92.3 us -> 81.8 us
  local copies, waits for them, and re-layouts: 1.94 us -> 4.95 us
    pallas_call x1, Pallas kernels: 5.79 us -> 1.29 us  [strips(): pl.pallas_call(functools.partial(strip_kernel, n), grid=(1,), in_specs=[w...]
    pallas_call x1, Pallas kernels: 55.1 us -> 52 us  [sweeps(): pl.pallas_call(functools.partial(sweep_kernel, tb, n), grid=(T // tb,), i...]
    unnamed x14 -> x20, local copies, waits for them, and re-layouts: 1.94 us -> 4.95 us
    pallas_call x1, Pallas kernels: 2.26 us -> 0.35 us  [corners(): pl.pallas_call(functools.partial(corner_kernel, n), grid=(1,), in_specs=[...]
where the time goes in v4:
time: 116 us; the launch traced here: 115 us
  Pallas kernels  81.8 us (71%)
  starting transfers between devices  16.8 us (14%)
  waiting for transfers between devices  10.8 us (9%)
  local copies, waits for them, and re-layouts  4.95 us (4%)
    pallas_call x1, Pallas kernels, sweeps(): pl.pallas_call(functools.partial(sweep_kernel, tb, n), grid=(T // tb,), i...  52 us
    pallas_call x1, Pallas kernels, pack(): pl.pallas_call(functools.partial(pack_kernel, tb, n), grid=(T // tb,), in...  11.9 us
    pallas_call x1, Pallas kernels, heat(): pl.pallas_call(functools.partial(heat_kernel, J, tb, n), grid=(T // tb,),...  11.3 us
    ppermute x2, starting transfers between devices, shifted(): lax.ppermute(up_going, axis, up)  6.31 us
    ppermute x2, waiting for transfers between devices, shifted(): lax.ppermute(down_going, axis, down)  5.98 us
    ppermute x2, starting transfers between devices, shifted(): lax.ppermute(down_going, axis, down)  5.83 us
    pallas_call x1, Pallas kernels, moments(): pl.pallas_call(functools.partial(moments_kernel, tb, n), grid=(T // tb,),...  5 us
    unnamed x20, local copies, waits for them, and re-layouts  4.95 us
  transfers between devices with their start and end apart: 7, of which 4 were waited for; matrix products, arithmetic and copies ran while one was open for 0% of the time, Pallas kernels for 10%

profile of v4, /device:TPU:4, one launch (start us, length us, event | category | flops | bytes accessed | tf_op | source)
XLA Modules:
  0.0 115.0 jit_solution(8402029885270939040)
XLA Ops:
  0.6 5.0 %moments.1 = (f32[2,32,8,128]{3,2,1,0:T(8,128)}, f32[2,32,128]{2,1,0:T(8,128)}) custom-call(f32[32,128]{1,0:T(8,128)} %refs_0_.1, f32[32,256,128]{2,1,0:T(8,128)} %refs_6_.1), custom_call_target="tpu_custom_call" | custom-call | flops 4194304 | bytes 4194304 | tf_op jit(solution)/shard_map/moments/pallas_call | solution.py:112
  5.6 3.6 %collective-permute-start.2 = (f32[2,32,128]{2,1,0:T(8,128)}, f32[2,32,128]{2,1,0:T(8,128)S(1)}, u32[]{:S(2)}, u32[]{:S(2)}) collective-permute-start(f32[2,32,128]{2,1,0:T(8,128)} %get-tuple-element.17.refs_1_), channel_id=1, source_target_pairs={{0,3},{1,0},{2,1},{3,2},{4,7},{5,4},{6,5},{7,6},{8,11},{9,8},{10,9... | collective-permute-start | bytes 98312 | tf_op jit(solution)/shard_map/ppermute | solution.py:636
  9.2 0.0 collective-permute-start.1
  9.2 1.0 collective-permute-start
  10.2 11.9 %pack_edges.1 = (f32[5,256,128]{2,1,0:T(8,128)}, f32[32,8,128]{2,1,0:T(8,128)}, f32[32,8,128]{2,1,0:T(8,128)}) custom-call(f32[2,32,256,128]{3,2,1,0:T(8,128)} %v_ref.3, f32[2,32,256,128]{3,2,1,0:T(8,128)} %f_ref.5, s32[32,256,128]{2,1,0:T(8,128)} %p_ref.3), custom_call_target="tpu_custom_call" | custom-call | flops 5242880 | bytes 20971520 | tf_op jit(solution)/shard_map/pack_edges/pallas_call | solution.py:172
  22.2 0.0 collective-permute-done.2.refs_4_
  22.2 0.0 copy-start.7
  22.2 0.0 collective-permute-done.1.refs_3_
  22.2 0.0 copy-start.8
  22.2 0.0 collective-permute-done.refs_2_
  22.2 0.0 copy-start.9
  22.2 0.6 copy-done.7
  22.8 0.0 copy-done.8
  22.8 0.0 copy-done.9
  22.8 11.3 %heat.1 = (f32[32,256,128]{2,1,0:T(8,128)}, f32[2,256,128]{2,1,0:T(8,128)}, f32[2,256,128]{2,1,0:T(8,128)}, f32[33,8,128]{2,1,0:T(8,128)}, f32[33,8,128]{2,1,0:T(8,128)}) custom-call(f32[32,128]{1,0:T(8,128)} %refs_0_.1, f32[2,32,128]{2,1,0:T(8,128)} %get-tuple-element.17.refs_1_, f32[2,32,128]{2,1,0:T(8,128)} %copy-done.9, f32[2,32,128]{2,1,0:T(8,128)} %copy-done.8, ...), custom_call_target="tpu_custom_call" | custom-call | flops 10485760 | bytes 8388608 | tf_op jit(solution)/shard_map/heat/pallas_call | solution.py:295
  34.1 1.9 %collective-permute-start.3 = (f32[2,256,128]{2,1,0:T(8,128)}, f32[2,256,128]{2,1,0:T(8,128)S(1)}, u32[]{:S(2)}, u32[]{:S(2)}) collective-permute-start(f32[2,256,128]{2,1,0:T(8,128)} %get-tuple-element.23), channel_id=1, source_target_pairs={{0,4},{4,8},{8,12},{12,16},{16,20},{20,24},{24,28},{1,5},{5,9},{9,... | collective-permute-start | bytes 786440 | tf_op jit(solution)/shard_map/ppermute | solution.py:630
  36.0 4.5 %collective-permute-start.4 = (f32[2,256,128]{2,1,0:T(8,128)}, f32[2,256,128]{2,1,0:T(8,128)S(1)}, u32[]{:S(2)}, u32[]{:S(2)}) collective-permute-start(f32[2,256,128]{2,1,0:T(8,128)} %get-tuple-element.24), channel_id=1, source_target_pairs={{4,0},{8,4},{12,8},{16,12},{20,16},{24,20},{28,24},{5,1},{9,5},{13... | collective-permute-start | bytes 786440 | tf_op jit(solution)/shard_map/ppermute | solution.py:630
  40.6 2.3 %collective-permute-done.3.fl_ref = f32[2,256,128]{2,1,0:T(8,128)S(1)} collective-permute-done((f32[2,256,128]{2,1,0:T(8,128)}, f32[2,256,128]{2,1,0:T(8,128)S(1)}, u32[]{:S(2)}, u32[]{:S(2)}) %collective-permute-start.3) | collective-permute-done | bytes 262176 | tf_op jit(solution)/shard_map/ppermute | solution.py:630
  42.9 1.9 %collective-permute-done.4.fr_ref = f32[2,256,128]{2,1,0:T(8,128)S(1)} collective-permute-done((f32[2,256,128]{2,1,0:T(8,128)}, f32[2,256,128]{2,1,0:T(8,128)S(1)}, u32[]{:S(2)}, u32[]{:S(2)}) %collective-permute-start.4) | collective-permute-done | bytes 262176 | tf_op jit(solution)/shard_map/ppermute | solution.py:630
  44.8 0.0 copy-start.5
  44.8 0.9 copy-done.5
  45.7 0.0 copy-start.6
  45.7 0.9 copy-done.6
  46.6 0.3 corners.1
  46.9 4.4 %collective-permute-start.5 = (f32[33,8,128]{2,1,0:T(8,128)S(1)}, f32[33,8,128]{2,1,0:T(8,128)S(1)}, u32[]{:S(2)}, u32[]{:S(2)}) collective-permute-start(f32[33,8,128]{2,1,0:T(8,128)S(1)} %get-tuple-element.27), channel_id=1, source_target_pairs={{0,1},{1,2},{2,3},{4,5},{5,6},{6,7},{8,9},{9,10},{10,11},{12,13},{... | collective-permute-start | bytes 405512 | tf_op jit(solution)/shard_map/ppermute | solution.py:630
  51.3 1.3 %collective-permute-start.6 = (f32[33,8,128]{2,1,0:T(8,128)S(1)}, f32[33,8,128]{2,1,0:T(8,128)S(1)}, u32[]{:S(2)}, u32[]{:S(2)}) collective-permute-start(f32[33,8,128]{2,1,0:T(8,128)S(1)} %get-tuple-element.28), channel_id=1, source_target_pairs={{1,0},{2,1},{3,2},{5,4},{6,5},{7,6},{9,8},{10,9},{11,10},{13,12},{... | collective-permute-start | bytes 405512 | tf_op jit(solution)/shard_map/ppermute | solution.py:630
  52.6 2.4 %collective-permute-done.5.lo_ref = f32[33,8,128]{2,1,0:T(8,128)S(1)} collective-permute-done((f32[33,8,128]{2,1,0:T(8,128)S(1)}, f32[33,8,128]{2,1,0:T(8,128)S(1)}, u32[]{:S(2)}, u32[]{:S(2)}) %collective-permute-start.5) | collective-permute-done | bytes 135200 | tf_op jit(solution)/shard_map/ppermute | solution.py:630
  55.1 0.0 copy-start.1
  55.1 4.1 %collective-permute-done.6.hi_ref = f32[33,8,128]{2,1,0:T(8,128)S(1)} collective-permute-done((f32[33,8,128]{2,1,0:T(8,128)S(1)}, f32[33,8,128]{2,1,0:T(8,128)S(1)}, u32[]{:S(2)}, u32[]{:S(2)}) %collective-permute-start.6) | collective-permute-done | bytes 135200 | tf_op jit(solution)/shard_map/ppermute | solution.py:630
  59.2 0.0 copy-start.2
  59.2 0.0 copy-start
  59.2 1.1 copy-done
  60.3 1.3 %strips.1 = (f32[2,34,8,128]{3,2,1,0:T(8,128)S(1)}, f32[2,32,8,128]{3,2,1,0:T(8,128)S(1)}) custom-call(f32[33,8,128]{2,1,0:T(8,128)S(1)} %collective-permute-done.5.lo_ref, f32[33,8,128]{2,1,0:T(8,128)S(1)} %collective-permute-done.6.hi_ref, f32[6,256,128]{2,1,0:T(8,128)S(1)} %get-tuple-element.29.r_ref, f32[5,256,128]{2,1,0:T(8,128)S(1)} %copy-done), custom_call_target="tpu_custom_call" | custom-call | flops 1966080 | bytes 1966080 | tf_op jit(solution)/shard_map/strips/pallas_call | solution.py:507
  61.6 0.0 copy-start.3
  61.6 0.7 copy-done.3
  62.3 0.0 copy-start.4
  62.3 0.7 copy-done.4
  63.0 0.0 copy-done.1
  63.0 0.0 copy-done.2
  63.0 52.0 %sweeps.1 = f32[2,32,256,128]{3,2,1,0:T(8,128)} custom-call(f32[2,32,256,128]{3,2,1,0:T(8,128)} %v_ref.3, f32[2,32,256,128]{3,2,1,0:T(8,128)} %f_ref.5, s32[32,256,128]{2,1,0:T(8,128)} %p_ref.3, f32[32,256,128]{2,1,0:T(8,128)} %get-tuple-element.15.h_ref, f32[33,8,128]{2,1,0:T(8,128)} %copy-done.1, f32[33,8,128]{2,1,0:T(8,128)} %copy-done.2, ...), custom_call_target="tpu_custom_call" | custom-call | flops 62914560 | bytes 33554432 | tf_op jit(solution)/shard_map/sweeps/pallas_call | solution.py:598
Async XLA Ops:
  5.6 16.5 %collective-permute-start.2 = (f32[2,32,128]{2,1,0:T(8,128)}, f32[2,32,128]{2,1,0:T(8,128)S(1)}, u32[]{:S(2)}, u32[]{:S(2)}) collective-permute-start(f32[2,32,128]{2,1,0:T(8,128)} %get-tuple-element.17.refs_1_), channel_id=1, source_target_pairs={{0,3},{1,0},{2,1},{3,2},{4,7},{5,4},{6,5},{7,6},{8,11},{9,8},{10,9... | collective-permute-start | bytes 98312 | tf_op jit(solution)/shard_map/ppermute | solution.py:636
  9.2 13.0 %collective-permute-start.1 = (f32[2,32,128]{2,1,0:T(8,128)}, f32[2,32,128]{2,1,0:T(8,128)S(1)}, u32[]{:S(2)}, u32[]{:S(2)}) collective-permute-start(f32[2,32,128]{2,1,0:T(8,128)} %get-tuple-element.17.refs_1_), channel_id=1, source_target_pairs={{0,2},{1,3},{2,0},{3,1},{4,6},{5,7},{6,4},{7,5},{8,10},{9,11},{10,... | collective-permute-start | bytes 98312 | tf_op jit(solution)/shard_map/ppermute | solution.py:636
  9.2 13.0 %collective-permute-start = (f32[2,32,128]{2,1,0:T(8,128)}, f32[2,32,128]{2,1,0:T(8,128)S(1)}, u32[]{:S(2)}, u32[]{:S(2)}) collective-permute-start(f32[2,32,128]{2,1,0:T(8,128)} %get-tuple-element.17.refs_1_), channel_id=1, source_target_pairs={{0,1},{1,2},{2,3},{3,0},{4,5},{5,6},{6,7},{7,4},{8,9},{9,10},{10,1... | collective-permute-start | bytes 98312 | tf_op jit(solution)/shard_map/ppermute | solution.py:636
  22.2 0.6 copy-start.7
  22.2 0.6 copy-start.8
  22.2 0.6 copy-start.9
  34.1 8.8 %collective-permute-start.3 = (f32[2,256,128]{2,1,0:T(8,128)}, f32[2,256,128]{2,1,0:T(8,128)S(1)}, u32[]{:S(2)}, u32[]{:S(2)}) collective-permute-start(f32[2,256,128]{2,1,0:T(8,128)} %get-tuple-element.23), channel_id=1, source_target_pairs={{0,4},{4,8},{8,12},{12,16},{16,20},{20,24},{24,28},{1,5},{5,9},{9,... | collective-permute-start | bytes 786440 | tf_op jit(solution)/shard_map/ppermute | solution.py:630
  36.0 8.7 %collective-permute-start.4 = (f32[2,256,128]{2,1,0:T(8,128)}, f32[2,256,128]{2,1,0:T(8,128)S(1)}, u32[]{:S(2)}, u32[]{:S(2)}) collective-permute-start(f32[2,256,128]{2,1,0:T(8,128)} %get-tuple-element.24), channel_id=1, source_target_pairs={{4,0},{8,4},{12,8},{16,12},{20,16},{24,20},{28,24},{5,1},{9,5},{13... | collective-permute-start | bytes 786440 | tf_op jit(solution)/shard_map/ppermute | solution.py:630
  44.8 0.9 copy-start.5
  45.7 0.9 copy-start.6
  46.9 8.1 %collective-permute-start.5 = (f32[33,8,128]{2,1,0:T(8,128)S(1)}, f32[33,8,128]{2,1,0:T(8,128)S(1)}, u32[]{:S(2)}, u32[]{:S(2)}) collective-permute-start(f32[33,8,128]{2,1,0:T(8,128)S(1)} %get-tuple-element.27), channel_id=1, source_target_pairs={{0,1},{1,2},{2,3},{4,5},{5,6},{6,7},{8,9},{9,10},{10,11},{12,13},{... | collective-permute-start | bytes 405512 | tf_op jit(solution)/shard_map/ppermute | solution.py:630
  51.3 7.9 %collective-permute-start.6 = (f32[33,8,128]{2,1,0:T(8,128)S(1)}, f32[33,8,128]{2,1,0:T(8,128)S(1)}, u32[]{:S(2)}, u32[]{:S(2)}) collective-permute-start(f32[33,8,128]{2,1,0:T(8,128)S(1)} %get-tuple-element.28), channel_id=1, source_target_pairs={{1,0},{2,1},{3,2},{5,4},{6,5},{7,6},{9,8},{10,9},{11,10},{13,12},{... | collective-permute-start | bytes 405512 | tf_op jit(solution)/shard_map/ppermute | solution.py:630
  55.1 8.0 %copy-start.1 = (f32[33,8,128]{2,1,0:T(8,128)}, f32[33,8,128]{2,1,0:T(8,128)S(1)}, u32[]{:S(2)}) copy-start(f32[33,8,128]{2,1,0:T(8,128)S(1)} %collective-permute-done.5.lo_ref) | copy-start | bytes 405508
  59.2 3.8 %copy-start.2 = (f32[33,8,128]{2,1,0:T(8,128)}, f32[33,8,128]{2,1,0:T(8,128)S(1)}, u32[]{:S(2)}) copy-start(f32[33,8,128]{2,1,0:T(8,128)S(1)} %collective-permute-done.6.hi_ref) | copy-start | bytes 405508
  59.2 1.1 copy-start
  61.6 0.7 copy-start.3
  62.3 0.7 copy-start.4

commit v5 on v4

--- a/solution.py
+++ b/solution.py
@@ -9,6 +9,7 @@
 
 DRAG_COEFF = 0.5
 RELAX_FACTOR = 0.8
+HALF_LOG2E = -0.7213475204444817
 F32 = jnp.float32
 MIB = 1 << 20
 
@@ -124,7 +125,7 @@
             jax.ShapeDtypeStruct((2, T, 8, 128), F32),
             jax.ShapeDtypeStruct((2, T, 128), F32),
         ],
-        compiler_params=pltpu.CompilerParams(vmem_limit_bytes=60 * MIB),
+        compiler_params=pltpu.CompilerParams(vmem_limit_bytes=57 * MIB),
         cost_estimate=pl.CostEstimate(flops=4 * T * n * 128, bytes_accessed=4 * T * n * 128, transcendentals=0),
         name="moments",
     )(d, prior)
@@ -183,7 +184,7 @@
             pl.BlockSpec((tb, 8, 128), lambda t: (t, 0, 0)),
         ],
         out_shape=[jax.ShapeDtypeStruct((5, n, 128), F32), row, row],
-        compiler_params=pltpu.CompilerParams(vmem_limit_bytes=60 * MIB),
+        compiler_params=pltpu.CompilerParams(vmem_limit_bytes=57 * MIB),
         cost_estimate=pl.CostEstimate(flops=5 * T * n * 128, bytes_accessed=20 * T * n * 128, transcendentals=0),
         name="pack_edges",
     )(v, f, pinned)
@@ -324,7 +325,7 @@
             pltpu.VMEM((n, 128), F32),
             pltpu.VMEM((tb, n // 8, 8, 128), F32),
         ],
-        compiler_params=pltpu.CompilerParams(vmem_limit_bytes=60 * MIB),
+        compiler_params=pltpu.CompilerParams(vmem_limit_bytes=57 * MIB),
         cost_estimate=pl.CostEstimate(flops=10 * T * n * 128, bytes_accessed=8 * T * n * 128, transcendentals=0),
         name="heat",
     )(d, *pqs, seg, prior, pk, lo7, hi7)
@@ -374,7 +375,7 @@
 
 
 def coefficients(f0, f1, free, heated):
-    v = jnp.exp(-0.5 * heated)
+    v = jnp.exp2(HALF_LOG2E * heated)
     w = RELAX_FACTOR * free
     a = w * reciprocal(DRAG_COEFF + 4.0 * v)
     return 1.0 - w, a * v, a * f0, a * f1
@@ -615,7 +616,7 @@
             pltpu.VMEM((2, S + 2, 8, 128), F32),
             pltpu.VMEM((4, S + 2, 8, 128), F32),
         ],
-        compiler_params=pltpu.CompilerParams(vmem_limit_bytes=60 * MIB),
+        compiler_params=pltpu.CompilerParams(vmem_limit_bytes=57 * MIB),
         cost_estimate=pl.CostEstimate(
             flops=60 * T * n * 128, bytes_accessed=32 * T * n * 128, transcendentals=T * n * 128
         ),

time: 116 us -> 116 us (level)
  no operation moved by 1% of the time
where the time goes in v5:
time: 116 us; the launch traced here: 115 us
  Pallas kernels  82 us (71%)
  starting transfers between devices  16.8 us (14%)
  waiting for transfers between devices  10.8 us (9%)
  local copies, waits for them, and re-layouts  4.95 us (4%)
    pallas_call x1, Pallas kernels, sweeps(): pl.pallas_call(functools.partial(sweep_kernel, tb, n), grid=(T // tb,), i...  52.2 us
    pallas_call x1, Pallas kernels, pack(): pl.pallas_call(functools.partial(pack_kernel, tb, n), grid=(T // tb,), in...  11.9 us
    pallas_call x1, Pallas kernels, heat(): pl.pallas_call(functools.partial(heat_kernel, J, tb, n), grid=(T // tb,),...  11.3 us
    ppermute x2, starting transfers between devices, shifted(): lax.ppermute(up_going, axis, up)  6.31 us
    ppermute x2, waiting for transfers between devices, shifted(): lax.ppermute(down_going, axis, down)  5.98 us
    ppermute x2, starting transfers between devices, shifted(): lax.ppermute(down_going, axis, down)  5.83 us
    pallas_call x1, Pallas kernels, moments(): pl.pallas_call(functools.partial(moments_kernel, tb, n), grid=(T // tb,),...  5 us
    unnamed x20, local copies, waits for them, and re-layouts  4.95 us
  transfers between devices with their start and end apart: 7, of which 4 were waited for; matrix products, arithmetic and copies ran while one was open for 0% of the time, Pallas kernels for 10%

profile of v5, /device:TPU:4, one launch (start us, length us, event | category | flops | bytes accessed | tf_op | source)
XLA Modules:
  0.0 115.2 jit_solution(16616516188257180327)
XLA Ops:
  0.6 5.0 %moments.1 = (f32[2,32,8,128]{3,2,1,0:T(8,128)}, f32[2,32,128]{2,1,0:T(8,128)}) custom-call(f32[32,128]{1,0:T(8,128)} %refs_0_.1, f32[32,256,128]{2,1,0:T(8,128)} %refs_6_.1), custom_call_target="tpu_custom_call" | custom-call | flops 4194304 | bytes 4194304 | tf_op jit(solution)/shard_map/moments/pallas_call | solution.py:113
  5.6 3.6 %collective-permute-start.2 = (f32[2,32,128]{2,1,0:T(8,128)}, f32[2,32,128]{2,1,0:T(8,128)S(1)}, u32[]{:S(2)}, u32[]{:S(2)}) collective-permute-start(f32[2,32,128]{2,1,0:T(8,128)} %get-tuple-element.17.refs_1_), channel_id=1, source_target_pairs={{0,3},{1,0},{2,1},{3,2},{4,7},{5,4},{6,5},{7,6},{8,11},{9,8},{10,9... | collective-permute-start | bytes 98312 | tf_op jit(solution)/shard_map/ppermute | solution.py:637
  9.2 0.0 collective-permute-start.1
  9.2 1.0 collective-permute-start
  10.2 11.9 %pack_edges.1 = (f32[5,256,128]{2,1,0:T(8,128)}, f32[32,8,128]{2,1,0:T(8,128)}, f32[32,8,128]{2,1,0:T(8,128)}) custom-call(f32[2,32,256,128]{3,2,1,0:T(8,128)} %v_ref.3, f32[2,32,256,128]{3,2,1,0:T(8,128)} %f_ref.5, s32[32,256,128]{2,1,0:T(8,128)} %p_ref.3), custom_call_target="tpu_custom_call" | custom-call | flops 5242880 | bytes 20971520 | tf_op jit(solution)/shard_map/pack_edges/pallas_call | solution.py:173
  22.2 0.0 collective-permute-done.2.refs_4_
  22.2 0.0 copy-start.7
  22.2 0.0 collective-permute-done.1.refs_3_
  22.2 0.0 copy-start.8
  22.2 0.0 collective-permute-done.refs_2_
  22.2 0.0 copy-start.9
  22.2 0.6 copy-done.7
  22.8 0.0 copy-done.8
  22.8 0.0 copy-done.9
  22.8 11.3 %heat.1 = (f32[32,256,128]{2,1,0:T(8,128)}, f32[2,256,128]{2,1,0:T(8,128)}, f32[2,256,128]{2,1,0:T(8,128)}, f32[33,8,128]{2,1,0:T(8,128)}, f32[33,8,128]{2,1,0:T(8,128)}) custom-call(f32[32,128]{1,0:T(8,128)} %refs_0_.1, f32[2,32,128]{2,1,0:T(8,128)} %get-tuple-element.17.refs_1_, f32[2,32,128]{2,1,0:T(8,128)} %copy-done.9, f32[2,32,128]{2,1,0:T(8,128)} %copy-done.8, ...), custom_call_target="tpu_custom_call" | custom-call | flops 10485760 | bytes 8388608 | tf_op jit(solution)/shard_map/heat/pallas_call | solution.py:296
  34.1 1.9 %collective-permute-start.3 = (f32[2,256,128]{2,1,0:T(8,128)}, f32[2,256,128]{2,1,0:T(8,128)S(1)}, u32[]{:S(2)}, u32[]{:S(2)}) collective-permute-start(f32[2,256,128]{2,1,0:T(8,128)} %get-tuple-element.23), channel_id=1, source_target_pairs={{0,4},{4,8},{8,12},{12,16},{16,20},{20,24},{24,28},{1,5},{5,9},{9,... | collective-permute-start | bytes 786440 | tf_op jit(solution)/shard_map/ppermute | solution.py:631
  36.0 4.5 %collective-permute-start.4 = (f32[2,256,128]{2,1,0:T(8,128)}, f32[2,256,128]{2,1,0:T(8,128)S(1)}, u32[]{:S(2)}, u32[]{:S(2)}) collective-permute-start(f32[2,256,128]{2,1,0:T(8,128)} %get-tuple-element.24), channel_id=1, source_target_pairs={{4,0},{8,4},{12,8},{16,12},{20,16},{24,20},{28,24},{5,1},{9,5},{13... | collective-permute-start | bytes 786440 | tf_op jit(solution)/shard_map/ppermute | solution.py:631
  40.6 2.3 %collective-permute-done.3.fl_ref = f32[2,256,128]{2,1,0:T(8,128)S(1)} collective-permute-done((f32[2,256,128]{2,1,0:T(8,128)}, f32[2,256,128]{2,1,0:T(8,128)S(1)}, u32[]{:S(2)}, u32[]{:S(2)}) %collective-permute-start.3) | collective-permute-done | bytes 262176 | tf_op jit(solution)/shard_map/ppermute | solution.py:631
  42.9 1.9 %collective-permute-done.4.fr_ref = f32[2,256,128]{2,1,0:T(8,128)S(1)} collective-permute-done((f32[2,256,128]{2,1,0:T(8,128)}, f32[2,256,128]{2,1,0:T(8,128)S(1)}, u32[]{:S(2)}, u32[]{:S(2)}) %collective-permute-start.4) | collective-permute-done | bytes 262176 | tf_op jit(solution)/shard_map/ppermute | solution.py:631
  44.8 0.0 copy-start.5
  44.8 0.9 copy-done.5
  45.7 0.0 copy-start.6
  45.7 0.9 copy-done.6
  46.6 0.3 corners.1
  46.9 4.4 %collective-permute-start.5 = (f32[33,8,128]{2,1,0:T(8,128)S(1)}, f32[33,8,128]{2,1,0:T(8,128)S(1)}, u32[]{:S(2)}, u32[]{:S(2)}) collective-permute-start(f32[33,8,128]{2,1,0:T(8,128)S(1)} %get-tuple-element.27), channel_id=1, source_target_pairs={{0,1},{1,2},{2,3},{4,5},{5,6},{6,7},{8,9},{9,10},{10,11},{12,13},{... | collective-permute-start | bytes 405512 | tf_op jit(solution)/shard_map/ppermute | solution.py:631
  51.3 1.3 %collective-permute-start.6 = (f32[33,8,128]{2,1,0:T(8,128)S(1)}, f32[33,8,128]{2,1,0:T(8,128)S(1)}, u32[]{:S(2)}, u32[]{:S(2)}) collective-permute-start(f32[33,8,128]{2,1,0:T(8,128)S(1)} %get-tuple-element.28), channel_id=1, source_target_pairs={{1,0},{2,1},{3,2},{5,4},{6,5},{7,6},{9,8},{10,9},{11,10},{13,12},{... | collective-permute-start | bytes 405512 | tf_op jit(solution)/shard_map/ppermute | solution.py:631
  52.6 2.4 %collective-permute-done.5.lo_ref = f32[33,8,128]{2,1,0:T(8,128)S(1)} collective-permute-done((f32[33,8,128]{2,1,0:T(8,128)S(1)}, f32[33,8,128]{2,1,0:T(8,128)S(1)}, u32[]{:S(2)}, u32[]{:S(2)}) %collective-permute-start.5) | collective-permute-done | bytes 135200 | tf_op jit(solution)/shard_map/ppermute | solution.py:631
  55.1 0.0 copy-start.1
  55.1 4.1 %collective-permute-done.6.hi_ref = f32[33,8,128]{2,1,0:T(8,128)S(1)} collective-permute-done((f32[33,8,128]{2,1,0:T(8,128)S(1)}, f32[33,8,128]{2,1,0:T(8,128)S(1)}, u32[]{:S(2)}, u32[]{:S(2)}) %collective-permute-start.6) | collective-permute-done | bytes 135200 | tf_op jit(solution)/shard_map/ppermute | solution.py:631
  59.2 0.0 copy-start.2
  59.2 0.0 copy-start
  59.2 1.1 copy-done
  60.3 1.3 %strips.1 = (f32[2,34,8,128]{3,2,1,0:T(8,128)S(1)}, f32[2,32,8,128]{3,2,1,0:T(8,128)S(1)}) custom-call(f32[33,8,128]{2,1,0:T(8,128)S(1)} %collective-permute-done.5.lo_ref, f32[33,8,128]{2,1,0:T(8,128)S(1)} %collective-permute-done.6.hi_ref, f32[6,256,128]{2,1,0:T(8,128)S(1)} %get-tuple-element.29.r_ref, f32[5,256,128]{2,1,0:T(8,128)S(1)} %copy-done), custom_call_target="tpu_custom_call" | custom-call | flops 1966080 | bytes 1966080 | tf_op jit(solution)/shard_map/strips/pallas_call | solution.py:508
  61.6 0.0 copy-start.3
  61.6 0.7 copy-done.3
  62.3 0.0 copy-start.4
  62.3 0.7 copy-done.4
  63.0 0.0 copy-done.1
  63.0 0.0 copy-done.2
  63.0 52.2 %sweeps.1 = f32[2,32,256,128]{3,2,1,0:T(8,128)} custom-call(f32[2,32,256,128]{3,2,1,0:T(8,128)} %v_ref.3, f32[2,32,256,128]{3,2,1,0:T(8,128)} %f_ref.5, s32[32,256,128]{2,1,0:T(8,128)} %p_ref.3, f32[32,256,128]{2,1,0:T(8,128)} %get-tuple-element.15.h_ref, f32[33,8,128]{2,1,0:T(8,128)} %copy-done.1, f32[33,8,128]{2,1,0:T(8,128)} %copy-done.2, ...), custom_call_target="tpu_custom_call" | custom-call | flops 62914560 | bytes 33554432 | tf_op jit(solution)/shard_map/sweeps/pallas_call | solution.py:599
Async XLA Ops:
  5.6 16.5 %collective-permute-start.2 = (f32[2,32,128]{2,1,0:T(8,128)}, f32[2,32,128]{2,1,0:T(8,128)S(1)}, u32[]{:S(2)}, u32[]{:S(2)}) collective-permute-start(f32[2,32,128]{2,1,0:T(8,128)} %get-tuple-element.17.refs_1_), channel_id=1, source_target_pairs={{0,3},{1,0},{2,1},{3,2},{4,7},{5,4},{6,5},{7,6},{8,11},{9,8},{10,9... | collective-permute-start | bytes 98312 | tf_op jit(solution)/shard_map/ppermute | solution.py:637
  9.2 13.0 %collective-permute-start.1 = (f32[2,32,128]{2,1,0:T(8,128)}, f32[2,32,128]{2,1,0:T(8,128)S(1)}, u32[]{:S(2)}, u32[]{:S(2)}) collective-permute-start(f32[2,32,128]{2,1,0:T(8,128)} %get-tuple-element.17.refs_1_), channel_id=1, source_target_pairs={{0,2},{1,3},{2,0},{3,1},{4,6},{5,7},{6,4},{7,5},{8,10},{9,11},{10,... | collective-permute-start | bytes 98312 | tf_op jit(solution)/shard_map/ppermute | solution.py:637
  9.2 13.0 %collective-permute-start = (f32[2,32,128]{2,1,0:T(8,128)}, f32[2,32,128]{2,1,0:T(8,128)S(1)}, u32[]{:S(2)}, u32[]{:S(2)}) collective-permute-start(f32[2,32,128]{2,1,0:T(8,128)} %get-tuple-element.17.refs_1_), channel_id=1, source_target_pairs={{0,1},{1,2},{2,3},{3,0},{4,5},{5,6},{6,7},{7,4},{8,9},{9,10},{10,1... | collective-permute-start | bytes 98312 | tf_op jit(solution)/shard_map/ppermute | solution.py:637
  22.2 0.6 copy-start.7
  22.2 0.6 copy-start.8
  22.2 0.6 copy-start.9
  34.1 8.8 %collective-permute-start.3 = (f32[2,256,128]{2,1,0:T(8,128)}, f32[2,256,128]{2,1,0:T(8,128)S(1)}, u32[]{:S(2)}, u32[]{:S(2)}) collective-permute-start(f32[2,256,128]{2,1,0:T(8,128)} %get-tuple-element.23), channel_id=1, source_target_pairs={{0,4},{4,8},{8,12},{12,16},{16,20},{20,24},{24,28},{1,5},{5,9},{9,... | collective-permute-start | bytes 786440 | tf_op jit(solution)/shard_map/ppermute | solution.py:631
  36.0 8.7 %collective-permute-start.4 = (f32[2,256,128]{2,1,0:T(8,128)}, f32[2,256,128]{2,1,0:T(8,128)S(1)}, u32[]{:S(2)}, u32[]{:S(2)}) collective-permute-start(f32[2,256,128]{2,1,0:T(8,128)} %get-tuple-element.24), channel_id=1, source_target_pairs={{4,0},{8,4},{12,8},{16,12},{20,16},{24,20},{28,24},{5,1},{9,5},{13... | collective-permute-start | bytes 786440 | tf_op jit(solution)/shard_map/ppermute | solution.py:631
  44.8 0.9 copy-start.5
  45.7 0.9 copy-start.6
  46.9 8.1 %collective-permute-start.5 = (f32[33,8,128]{2,1,0:T(8,128)S(1)}, f32[33,8,128]{2,1,0:T(8,128)S(1)}, u32[]{:S(2)}, u32[]{:S(2)}) collective-permute-start(f32[33,8,128]{2,1,0:T(8,128)S(1)} %get-tuple-element.27), channel_id=1, source_target_pairs={{0,1},{1,2},{2,3},{4,5},{5,6},{6,7},{8,9},{9,10},{10,11},{12,13},{... | collective-permute-start | bytes 405512 | tf_op jit(solution)/shard_map/ppermute | solution.py:631
  51.3 7.9 %collective-permute-start.6 = (f32[33,8,128]{2,1,0:T(8,128)S(1)}, f32[33,8,128]{2,1,0:T(8,128)S(1)}, u32[]{:S(2)}, u32[]{:S(2)}) collective-permute-start(f32[33,8,128]{2,1,0:T(8,128)S(1)} %get-tuple-element.28), channel_id=1, source_target_pairs={{1,0},{2,1},{3,2},{5,4},{6,5},{7,6},{9,8},{10,9},{11,10},{13,12},{... | collective-permute-start | bytes 405512 | tf_op jit(solution)/shard_map/ppermute | solution.py:631
  55.1 8.0 %copy-start.1 = (f32[33,8,128]{2,1,0:T(8,128)}, f32[33,8,128]{2,1,0:T(8,128)S(1)}, u32[]{:S(2)}) copy-start(f32[33,8,128]{2,1,0:T(8,128)S(1)} %collective-permute-done.5.lo_ref) | copy-start | bytes 405508
  59.2 3.8 %copy-start.2 = (f32[33,8,128]{2,1,0:T(8,128)}, f32[33,8,128]{2,1,0:T(8,128)S(1)}, u32[]{:S(2)}) copy-start(f32[33,8,128]{2,1,0:T(8,128)S(1)} %collective-permute-done.6.hi_ref) | copy-start | bytes 405508
  59.2 1.1 copy-start
  61.6 0.7 copy-start.3
  62.3 0.7 copy-start.4

commit v6 on v5

--- a/solution.py
+++ b/solution.py
@@ -131,12 +131,62 @@
     )(d, prior)
 
 
-def pack_kernel(tb, n, v_ref, f_ref, p_ref, pk_ref, lo_ref, hi_ref):
+def rows_kernel(T, v_lo, v_hi, f_lo, f_hi, p_lo, p_hi, lo_ref, hi_ref):
+    _, sub = iotas()
+
+    def stack(v0, v1, f0, f1, fr):
+        out = jnp.where(sub < 2, v0, v1)
+        out = jnp.where(sub >= 4, f0, out)
+        out = jnp.where(sub >= 5, f1, out)
+        out = jnp.where(sub >= 6, fr, out)
+        return jnp.where(sub >= 7, 0.0, out)
+
+    for v, f, p, out, shifts in (
+        (v_lo, f_lo, p_lo, lo_ref, (0, 2, 4, 5, 6)),
+        (v_hi, f_hi, p_hi, hi_ref, (2, 4, 5, 6, 7)),
+    ):
+        for t in range(T):
+            raw = [v[0, t], v[1, t], f[0, t], f[1, t], 1.0 - p[t].astype(F32)]
+            out[t] = stack(*[pltpu.roll(x, q, 0) if q else x for x, q in zip(raw, shifts)])
+
+
+def whole(shape):
+    return pl.BlockSpec(shape, lambda t: (0,) * len(shape))
+
+
+def edge_rows(v, f, pinned):
+    _, T, n, _ = v.shape
+    row = jax.ShapeDtypeStruct((T, 8, 128), F32)
+    end = n // 8 - 1
+    four = [pl.BlockSpec((2, T, 8, 128), lambda t, k=k: (0, 0, k, 0)) for k in (0, end)]
+    three = [pl.BlockSpec((T, 8, 128), lambda t, k=k: (0, k, 0)) for k in (0, end)]
+    return pl.pallas_call(
+        functools.partial(rows_kernel, T),
+        grid=(1,),
+        in_specs=[*four, *four, *three],
+        out_specs=[whole((T, 8, 128))] * 2,
+        out_shape=[row, row],
+        compiler_params=pltpu.CompilerParams(vmem_limit_bytes=57 * MIB),
+        cost_estimate=pl.CostEstimate(flops=0, bytes_accessed=48 * T * 8 * 128, transcendentals=0),
+        name="edge_rows",
+    )(v, v, f, f, pinned, pinned)
+
+
+def gather_columns(ref, T):
+    lane, _ = iotas()
+    parts = [jnp.where(lane >> 2 == t, pltpu.roll(ref[t], (4 * t + 2) & 127, 1), 0.0) for t in range(T)]
+    while len(parts) > 1:
+        parts = [p + q for p, q in zip(parts[::2], parts[1::2])]
+    return parts[0]
+
+
+def pack_kernel(tb, n, T, v_ref, f_ref, p_ref, lo_ref, hi_ref, pk_ref, right_ref, left_ref, fp_ref):
     base = pl.program_id(0) * tb
     lane = lax.broadcasted_iota(jnp.int32, (n, 128), 1)
     group = lane >> 2
     for k in range(5):
-        acc = pk_ref[k]
+        ref, q = (pk_ref, k) if k < 2 else (fp_ref, k - 2)
+        acc = ref[q, 0:n, :]
         for u in range(tb):
             if k < 2:
                 x = v_ref[k, u]
@@ -146,55 +196,55 @@
                 x = 1.0 - p_ref[u].astype(F32)
             t = base + u
             acc = jnp.where(group == t, pltpu.roll(x, (4 * t + 2) & 127, 1), acc)
-        pk_ref[k] = acc
-    _, sub = iotas()
-
-    def stack(v0, v1, f0, f1, fr):
-        out = jnp.where(sub < 2, v0, v1)
-        out = jnp.where(sub >= 4, f0, out)
-        out = jnp.where(sub >= 5, f1, out)
-        return jnp.where(sub >= 6, fr, out)
-
-    tiles = []
-    for u in range(tb):
-        for top, at, shifts in ((True, 0, (0, 2, 4, 5, 6)), (False, n - 8, (2, 4, 5, 6, 7))):
-            rows = pl.ds(at, 8)
-            raw = [v_ref[0, u, rows, :], v_ref[1, u, rows, :], f_ref[0, u, rows, :], f_ref[1, u, rows, :]]
-            raw.append(1.0 - p_ref[u, rows, :].astype(F32))
-            tiles.append((u, top, stack(*[pltpu.roll(x, q, 0) if q else x for x, q in zip(raw, shifts)])))
-    for u, top, tile in tiles:
-        (lo_ref if top else hi_ref)[u] = tile
-
-
-def pack(v, f, pinned):
+        ref[q, 0:n, :] = acc
+
+    @pl.when(pl.program_id(0) == pl.num_programs(0) - 1)
+    def _():
+        slot = lane & 3
+        v0, v1 = pk_ref[0, 0:n, :], pk_ref[1, 0:n, :]
+        f0, f1, fr = fp_ref[0], fp_ref[1], fp_ref[2]
+
+        def sel(a, b, c):
+            return jnp.where(slot < 1, a, jnp.where(slot == 1, b, c))
+
+        right_ref[0, 0:n, :] = jnp.where(slot < 2, v0, pltpu.roll(v1, 2, 1))
+        left_ref[0, 0:n, :] = jnp.where(slot >= 2, v0, pltpu.roll(v1, 126, 1))
+        right_ref[1, 0:n, :] = sel(pltpu.roll(f0, 127, 1), f1, pltpu.roll(fr, 1, 1))
+        left_ref[1, 0:n, :] = sel(pltpu.roll(f0, 126, 1), pltpu.roll(f1, 127, 1), fr)
+        for k, ref in ((0, lo_ref), (1, hi_ref)):
+            tile = gather_columns(ref, T)
+            for out in (pk_ref, right_ref, left_ref):
+                out[k, n : n + 8, :] = tile
+
+
+def pack(v, f, pinned, lo, hi):
     _, T, n, _ = v.shape
     tb = 4
-    row = jax.ShapeDtypeStruct((T, 8, 128), F32)
+    out = jax.ShapeDtypeStruct((2, n + 8, 128), F32)
     return pl.pallas_call(
-        functools.partial(pack_kernel, tb, n),
+        functools.partial(pack_kernel, tb, n, T),
         grid=(T // tb,),
         in_specs=[
             pl.BlockSpec((2, tb, n, 128), lambda t: (0, t, 0, 0)),
             pl.BlockSpec((2, tb, n, 128), lambda t: (0, t, 0, 0)),
             pl.BlockSpec((tb, n, 128), lambda t: (t, 0, 0)),
-        ],
-        out_specs=[
-            pl.BlockSpec((5, n, 128), lambda t: (0, 0, 0)),
-            pl.BlockSpec((tb, 8, 128), lambda t: (t, 0, 0)),
-            pl.BlockSpec((tb, 8, 128), lambda t: (t, 0, 0)),
-        ],
-        out_shape=[jax.ShapeDtypeStruct((5, n, 128), F32), row, row],
+            whole((T, 8, 128)),
+            whole((T, 8, 128)),
+        ],
+        out_specs=[whole((2, n + 8, 128))] * 3,
+        out_shape=[out, out, out],
+        scratch_shapes=[pltpu.VMEM((3, n, 128), F32)],
         compiler_params=pltpu.CompilerParams(vmem_limit_bytes=57 * MIB),
         cost_estimate=pl.CostEstimate(flops=5 * T * n * 128, bytes_accessed=20 * T * n * 128, transcendentals=0),
         name="pack_edges",
-    )(v, f, pinned)
+    )(v, f, pinned, lo, hi)
 
 
 def heat_kernel(J, tb, n, *refs):
     d_ref, *pq_refs = refs[: J + 1]
     (
-        seg_ref, f_ref, pk_ref, lo7_ref, hi7_ref,
-        out_ref, right_ref, left_ref, lo_ref, hi_ref, alls, sums, pkh, ys,
+        seg_ref, f_ref,
+        out_ref, send_ref, row_ref, alls, sums, ys,
     ) = refs[J + 1 :]
     S = n // 8
     step = pl.program_id(0)
@@ -263,115 +313,57 @@
 
     lane_n = lax.broadcasted_iota(jnp.int32, (n, 128), 1)
     group = lane_n >> 2
-    acc = pkh[...]
+    acc = send_ref[0:n, :]
+    tile = send_ref[n : n + 8, :]
+    lane, _ = iotas()
+    rows = []
     for u in range(tb):
         t = base + u
         acc = jnp.where(group == t, pltpu.roll(out_ref[u], (4 * t + 2) & 127, 1), acc)
-    pkh[...] = acc
-    lows = [jnp.where(sub == 7, out_ref[u, 0:1, :], lo7_ref[u]) for u in range(tb)]
-    highs = [jnp.where(sub == 7, out_ref[u, n - 1 : n, :], hi7_ref[u]) for u in range(tb)]
-    for u in range(tb):
-        lo_ref[u] = lows[u]
-        hi_ref[u] = highs[u]
-
-    @pl.when(step == pl.num_programs(0) - 1)
-    def _():
-        slot = lane_n & 3
-        v0, v1, f0, f1, fr, he = pk_ref[0], pk_ref[1], pk_ref[2], pk_ref[3], pk_ref[4], pkh[...]
-
-        def sel(a, b, c, d):
-            return jnp.where(slot < 2, jnp.where(slot == 0, a, b), jnp.where(slot == 2, c, d))
-
-        right_ref[0] = jnp.where(slot < 2, v0, pltpu.roll(v1, 2, 1))
-        left_ref[0] = jnp.where(slot >= 2, v0, pltpu.roll(v1, 126, 1))
-        right_ref[1] = sel(pltpu.roll(f0, 127, 1), f1, pltpu.roll(fr, 1, 1), pltpu.roll(he, 2, 1))
-        left_ref[1] = sel(pltpu.roll(f0, 126, 1), pltpu.roll(f1, 127, 1), fr, pltpu.roll(he, 1, 1))
-
-
-def heat(d, pqs, seg, prior, pk, lo7, hi7):
+        below = gain[u][0:1] * (sums[0, pl.ds(t, 1), :] + rs[u][0:1] * z[u][0:1])
+        above = gain[u][0:1] * (sums[1, pl.ds(t, 1), :] + rs[u][0:1] * y[u][7:8])
+        both = jnp.where(sub == 0, below, above)
+        rows.append((u, below, above))
+        tile = jnp.where(lane >> 2 == t, pltpu.roll(both, (4 * t + 2) & 127, 1), tile)
+    send_ref[0:n, :] = acc
+    send_ref[n : n + 8, :] = tile
+    for u, below, above in rows:
+        row_ref[0, pl.ds(base + u, 1), :] = below
+        row_ref[1, pl.ds(base + u, 1), :] = above
+
+
+def heat(d, pqs, seg, prior):
     T, n, _ = prior.shape
     J = len(pqs)
     tb = 4
-    row = jax.ShapeDtypeStruct((T + 1, 8, 128), F32)
     return pl.pallas_call(
         functools.partial(heat_kernel, J, tb, n),
         grid=(T // tb,),
         in_specs=[
-            pl.BlockSpec((T, 128), lambda t: (0, 0)),
-            *[pl.BlockSpec((2, T, 128), lambda t: (0, 0, 0)) for _ in range(J)],
+            whole((T, 128)),
+            *[whole((2, T, 128)) for _ in range(J)],
             pl.BlockSpec((2, tb, 8, 128), lambda t: (0, t, 0, 0)),
             pl.BlockSpec((tb, n, 128), lambda t: (t, 0, 0)),
-            pl.BlockSpec((5, n, 128), lambda t: (0, 0, 0)),
-            pl.BlockSpec((tb, 8, 128), lambda t: (t, 0, 0)),
-            pl.BlockSpec((tb, 8, 128), lambda t: (t, 0, 0)),
         ],
         out_specs=[
             pl.BlockSpec((tb, n, 128), lambda t: (t, 0, 0)),
-            pl.BlockSpec((2, n, 128), lambda t: (0, 0, 0)),
-            pl.BlockSpec((2, n, 128), lambda t: (0, 0, 0)),
-            pl.BlockSpec((tb, 8, 128), lambda t: (t, 0, 0)),
-            pl.BlockSpec((tb, 8, 128), lambda t: (t, 0, 0)),
+            whole((n + 8, 128)),
+            whole((2, T, 128)),
         ],
         out_shape=[
             jax.ShapeDtypeStruct((T, n, 128), F32),
-            jax.ShapeDtypeStruct((2, n, 128), F32),
-            jax.ShapeDtypeStruct((2, n, 128), F32),
-            row,
-            row,
+            jax.ShapeDtypeStruct((n + 8, 128), F32),
+            jax.ShapeDtypeStruct((2, T, 128), F32),
         ],
         scratch_shapes=[
             pltpu.VMEM((J, 2, T, 128), F32),
             pltpu.VMEM((2, T, 128), F32),
-            pltpu.VMEM((n, 128), F32),
             pltpu.VMEM((tb, n // 8, 8, 128), F32),
         ],
         compiler_params=pltpu.CompilerParams(vmem_limit_bytes=57 * MIB),
         cost_estimate=pl.CostEstimate(flops=10 * T * n * 128, bytes_accessed=8 * T * n * 128, transcendentals=0),
         name="heat",
-    )(d, *pqs, seg, prior, pk, lo7, hi7)
-
-
-def corner_kernel(n, fl_ref, fr_ref, lo_in, hi_in, r_ref, lo_ref, hi_ref):
-    slot = lax.broadcasted_iota(jnp.int32, (n, 128), 1) & 3
-    al, ar, bl, br = fl_ref[0], fr_ref[0], fl_ref[1], fr_ref[1]
-    low = slot < 2
-    r_ref[0] = jnp.where(low, al, ar)
-    r_ref[1] = jnp.where(low, pltpu.roll(al, 126, 1), pltpu.roll(ar, 2, 1))
-    for k in range(4):
-        a = bl if k == 1 else pltpu.roll(bl, (1 - k) & 127, 1)
-        b = br if k == 2 else pltpu.roll(br, (2 - k) & 127, 1)
-        r_ref[2 + k] = jnp.where(low, a, b)
-    for ref, a, e in ((lo_ref, 0, 0), (hi_ref, n - 2, n - 1)):
-        ref[0, 0:2, :] = r_ref[0, a : a + 2, :]
-        ref[0, 2:4, :] = r_ref[1, a : a + 2, :]
-        for k in range(4):
-            ref[0, 4 + k : 5 + k, :] = r_ref[2 + k, e : e + 1, :]
-
-
-def corners(from_left, from_right, lo, hi):
-    _, n, _ = from_left.shape
-    T = lo.shape[0] - 1
-    row = jax.ShapeDtypeStruct(lo.shape, F32)
-    return pl.pallas_call(
-        functools.partial(corner_kernel, n),
-        grid=(1,),
-        in_specs=[
-            pl.BlockSpec((2, n, 128), lambda g: (0, 0, 0)),
-            pl.BlockSpec((2, n, 128), lambda g: (0, 0, 0)),
-            pl.BlockSpec(memory_space=pl.ANY),
-            pl.BlockSpec(memory_space=pl.ANY),
-        ],
-        out_specs=[
-            pl.BlockSpec((6, n, 128), lambda g: (0, 0, 0)),
-            pl.BlockSpec((1, 8, 128), lambda g: (T, 0, 0)),
-            pl.BlockSpec((1, 8, 128), lambda g: (T, 0, 0)),
-        ],
-        out_shape=[jax.ShapeDtypeStruct((6, n, 128), F32), row, row],
-        input_output_aliases={2: 1, 3: 2},
-        compiler_params=pltpu.CompilerParams(vmem_limit_bytes=8 * MIB),
-        cost_estimate=pl.CostEstimate(flops=0, bytes_accessed=40 * n * 128, transcendentals=0),
-        name="corners",
-    )(from_left, from_right, lo, hi)
+    )(d, *pqs, seg, prior)
 
 
 def coefficients(f0, f1, free, heated):
@@ -411,34 +403,36 @@
     return [(cos, m, 0, below[m]) for m in range(4)] + [(cos, m, S + 1, above[m]) for m in range(4)]
 
 
-def strip_kernel(n, lo_ref, hi_ref, r_ref, own_ref, yh1, yh2, xs, ws, r1s, cos):
+def strip_kernel(n, own_ref, fl_ref, fr_ref, hl_ref, hr_ref, yh1, yh2, r_ref, edge, xs, ws, r1s, cos):
     S = n // 8
-    T = lo_ref.shape[0] - 1
-    lane, _ = iotas()
+    lane, sub = iotas()
     slot = lane & 3
     outer = (slot == 0) | (slot == 3)
     sign = jnp.where(slot == 1, -0.25, 0.25)
 
+    low_n = lax.broadcasted_iota(jnp.int32, (n, 128), 1) & 3 < 2
+    al, ar, bl, br = [ref[k, 0:n, :] for k in range(2) for ref in (fl_ref, fr_ref)]
+    r_ref[0] = jnp.where(low_n, al, ar)
+    r_ref[1] = jnp.where(low_n, pltpu.roll(al, 126, 1), pltpu.roll(ar, 2, 1))
+    for k in range(3):
+        a = bl if k == 1 else pltpu.roll(bl, (1 - k) & 127, 1)
+        b = br if k == 2 else pltpu.roll(br, (2 - k) & 127, 1)
+        r_ref[2 + k] = jnp.where(low_n, a, b)
+    r_ref[5] = jnp.where(low_n, hl_ref[0:n, :], hr_ref[0:n, :])
+    heat_rows = jnp.where(slot < 2, hl_ref[n : n + 8, :], hr_ref[n : n + 8, :])
+    for k in range(2):
+        tile = jnp.where(slot < 2, fl_ref[k, n : n + 8, :], fr_ref[k, n : n + 8, :])
+        edge[k] = jnp.where(sub == 7, heat_rows[k : k + 1, :], tile)
+        edge[2 + k] = jnp.where(outer, tile, own_ref[k, n : n + 8, :])
+
     def low(k):
-        return lo_ref[T, k : k + 1, :]
+        return edge[0, k : k + 1, :]
 
     def high(k):
-        return hi_ref[T, k : k + 1, :]
+        return edge[1, k : k + 1, :]
 
     def get(m, i):
         return r_ref[2 + m, pl.ds(i, 8, stride=S), :]
-
-    def collect(ref):
-        parts = [
-            jnp.where(lane >> 2 == t, pltpu.roll(ref[t], (4 * t + 2) & 127, 1), 0.0) for t in range(T)
-        ]
-        while len(parts) > 1:
-            parts = [p + q for p, q in zip(parts[::2], parts[1::2])]
-        return parts[0]
-
-    own_lo, own_hi = collect(lo_ref), collect(hi_ref)
-    both_lo = jnp.where(outer, lo_ref[T], own_lo)
-    both_hi = jnp.where(outer, hi_ref[T], own_hi)
 
     def load(start, m):
         todo = []
@@ -453,10 +447,10 @@
 
     over_rows(0, S, load)
     def row_low(k):
-        return both_lo[k : k + 1, :]
+        return edge[2, k : k + 1, :]
 
     def row_high(k):
-        return both_hi[k : k + 1, :]
+        return edge[3, k : k + 1, :]
 
     def get_r(c, i):
         return r_ref[c, pl.ds(i, 8, stride=S), :]
@@ -501,32 +495,33 @@
     over_rows(0, S, edges, 16)
 
 
-def strips(lo, hi, r, pk):
-    n = r.shape[1]
+def strips(own, fl, fr, hl, hr):
+    n = own.shape[1] - 8
     S = n // 8
-    whole = lambda shape: pl.BlockSpec(shape, lambda g: (0,) * len(shape))
     return pl.pallas_call(
         functools.partial(strip_kernel, n),
         grid=(1,),
-        in_specs=[whole(lo.shape), whole(hi.shape), whole(r.shape), whole((2, n, 128))],
+        in_specs=[whole(own.shape), whole(fl.shape), whole(fr.shape), whole(hl.shape), whole(hr.shape)],
         out_specs=[whole((2, S + 2, 8, 128)), whole((2, S, 8, 128))],
         out_shape=[
             jax.ShapeDtypeStruct((2, S + 2, 8, 128), F32),
             jax.ShapeDtypeStruct((2, S, 8, 128), F32),
         ],
         scratch_shapes=[
+            pltpu.VMEM((6, n, 128), F32),
+            pltpu.VMEM((4, 8, 128), F32),
             pltpu.VMEM((2, S + 4, 8, 128), F32),
             pltpu.VMEM((2, S + 4, 8, 128), F32),
             pltpu.VMEM((2, S + 2, 8, 128), F32),
             pltpu.VMEM((4, S + 2, 8, 128), F32),
         ],
-        compiler_params=pltpu.CompilerParams(vmem_limit_bytes=8 * MIB),
+        compiler_params=pltpu.CompilerParams(vmem_limit_bytes=12 * MIB),
         cost_estimate=pl.CostEstimate(flops=60 * n * 128, bytes_accessed=60 * n * 128, transcendentals=n * 128),
         name="strips",
-    )(lo, hi, r, pk)
-
-
-def sweep_kernel(tb, n, v_ref, f_ref, p_ref, h_ref, lo_ref, hi_ref, yh1, yh2, out_ref, xs, v1s, cos):
+    )(own, fl, fr, hl, hr)
+
+
+def sweep_kernel(tb, n, v_ref, f_ref, p_ref, h_ref, lo_ref, hi_ref, row_ref, yh1, yh2, out_ref, xs, v1s, cos):
     S = n // 8
     step = pl.program_id(0)
     lane, _ = iotas()
@@ -537,10 +532,10 @@
         shift = (126 - 4 * t) & 127
 
         def low(k):
-            return lo_ref[t, k : k + 1, :]
+            return row_ref[0, pl.ds(t, 1), :] if k == 7 else lo_ref[t, k : k + 1, :]
 
         def high(k):
-            return hi_ref[t, k : k + 1, :]
+            return row_ref[1, pl.ds(t, 1), :] if k == 7 else hi_ref[t, k : k + 1, :]
 
         def get(m, i):
             rows = pl.ds(i, 8, stride=S)
@@ -556,9 +551,8 @@
                 todo += [(cos, q, i + 1, co[q]) for q in range(4)]
             put(todo)
 
-        def sweep(src, off, yh, start, m):
+        def sweep(src, off, yh, start, m, store):
             x = [[src[c, start + off + j] for c in range(2)] for j in range(m + 2)]
-            done = []
             for j in range(m):
                 i = start + j
                 prev, here, after = x[j], x[j + 1], x[j + 2]
@@ -569,15 +563,19 @@
                     up = jnp.where(first, edge, here[c] + q[1 - c])
                     down = jnp.where(last, edge, here[c] - q[1 - c])
                     around = prev[c] + after[c] + (pltpu.roll(up, 127, 1) + pltpu.roll(down, 1, 1))
-                    done.append((c, i, k * here[c] + cos[2 + c, i + 1] + g * around))
-            return done
+                    store(c, i, k * here[c] + cos[2 + c, i + 1] + g * around)
+
+        def keep(c, i, value):
+            v1s[c, i + 1] = value
+
+        def give(c, i, value):
+            out_ref[c, u, pl.ds(i, 8, stride=S), :] = value
 
         def first_sweep(start, m):
-            put([(v1s, c, i + 1, value) for c, i, value in sweep(xs, 1, yh1, start, m)])
+            sweep(xs, 1, yh1, start, m, keep)
 
         def second_sweep(start, m):
-            for c, i, value in sweep(v1s, 0, yh2, start, m):
-                out_ref[c, u, pl.ds(i, 8, stride=S), :] = value
+            sweep(v1s, 0, yh2, start, m, give)
 
         put(
             halo_rows(xs, S, low, high, lambda c, i: v_ref[c, u, pl.ds(i, 8, stride=S), :])
@@ -591,11 +589,10 @@
     lax.fori_loop(0, tb, layer, 0)
 
 
-def sweeps(v, f, pinned, heated, lo, hi, yh1, yh2):
+def sweeps(v, f, pinned, heated, lo, hi, heated_rows, yh1, yh2):
     _, T, n, _ = v.shape
     S = n // 8
     tb = 2
-    whole = lambda shape: pl.BlockSpec(shape, lambda t: (0,) * len(shape))
     return pl.pallas_call(
         functools.partial(sweep_kernel, tb, n),
         grid=(T // tb,),
@@ -604,8 +601,9 @@
             pl.BlockSpec((2, tb, n, 128), lambda t: (0, t, 0, 0)),
             pl.BlockSpec((tb, n, 128), lambda t: (t, 0, 0)),
             pl.BlockSpec((tb, n, 128), lambda t: (t, 0, 0)),
-            whole((T + 1, 8, 128)),
-            whole((T + 1, 8, 128)),
+            whole((T, 8, 128)),
+            whole((T, 8, 128)),
+            whole((2, T, 128)),
             whole((2, S + 2, 8, 128)),
             whole((2, S, 8, 128)),
         ],
@@ -621,7 +619,7 @@
             flops=60 * T * n * 128, bytes_accessed=32 * T * n * 128, transcendentals=T * n * 128
         ),
         name="sweeps",
-    )(v, f, pinned, heated, lo, hi, yh1, yh2)
+    )(v, f, pinned, heated, lo, hi, heated_rows, yh1, yh2)
 
 
 def shifted(up_going, down_going, axis):
@@ -632,16 +630,17 @@
 
 
 def local(prior, d, v, f, pinned):
+    J = lax.axis_size("wid")
+    lo, hi = edge_rows(v, f, pinned)
+    from_below, from_above = shifted(hi, lo, "wid")
     seg, pq = moments(d, prior)
-    J = lax.axis_size("wid")
     pqs = [pq] + [lax.ppermute(pq, "wid", [(i, (i + s) % J) for i in range(J)]) for s in range(1, J)]
-    pk, lo7, hi7 = pack(v, f, pinned)
-    heated, right, left, lo, hi = heat(d, pqs, seg, prior, pk, lo7, hi7)
+    own, right, left = pack(v, f, pinned, from_below, from_above)
     from_left, from_right = shifted(right, left, "len")
-    r, lo, hi = corners(from_left, from_right, lo, hi)
-    from_below, from_above = shifted(hi, lo, "wid")
-    yh1, yh2 = strips(from_below, from_above, r, pk)
-    flow = sweeps(v, f, pinned, heated, from_below, from_above, yh1, yh2)
+    heated, columns, heated_rows = heat(d, pqs, seg, prior)
+    heat_left, heat_right = shifted(columns, columns, "len")
+    yh1, yh2 = strips(own, from_left, from_right, heat_left, heat_right)
+    flow = sweeps(v, f, pinned, heated, from_below, from_above, heated_rows, yh1, yh2)
     return heated, flow
 
 

time: 116 us -> 123 us (1.060)
  waiting for transfers between devices: 10.8 us -> 15.1 us
  starting transfers between devices: 16.8 us -> 20.3 us
  local copies, waits for them, and re-layouts: 4.95 us -> 2.69 us
  Pallas kernels: 82 us -> 83.4 us
    ppermute x3, waiting for transfers between devices: 0.01 us -> 4.34 us  [local(): lax.ppermute(pq, 'wid', [(i, (i + s) % J) for i in range(J)])]
    unnamed x20 -> x16, local copies, waits for them, and re-layouts: 4.95 us -> 2.69 us
    pallas_call x2, Pallas kernels: 12.3 us -> 14.4 us  [the longest x1 12.4 us: pack(): pl.pallas_call(functools.partial(pack_kernel, tb, n, T), grid=(T // tb,),...]
    ppermute x2 -> x3, starting transfers between devices: 5.83 us -> 7.75 us  [shifted(): lax.ppermute(down_going, axis, down)]
    ppermute x2 -> x3, starting transfers between devices: 6.31 us -> 7.92 us  [shifted(): lax.ppermute(up_going, axis, up)]
    ppermute x2 -> x3, waiting for transfers between devices: 4.77 us -> 6.33 us  [shifted(): lax.ppermute(up_going, axis, up)]
    ppermute x2 -> x3, waiting for transfers between devices: 5.98 us -> 4.47 us  [shifted(): lax.ppermute(down_going, axis, down)]
  transfers between devices with their start and end apart: 7 -> 9, of which waited for: 4 -> 6; matrix products, arithmetic and copies ran while one was open for 0% -> 0% of each run, Pallas kernels for 10% -> 13%
where the time goes in v6:
time: 123 us; the launch traced here: 122 us
  Pallas kernels  83.4 us (68%)
  starting transfers between devices  20.3 us (17%)
  waiting for transfers between devices  15.1 us (12%)
  local copies, waits for them, and re-layouts  2.69 us (2%)
    pallas_call x1, Pallas kernels, sweeps(): pl.pallas_call(functools.partial(sweep_kernel, tb, n), grid=(T // tb,), i...  52.2 us
    pallas_call x1, Pallas kernels, pack(): pl.pallas_call(functools.partial(pack_kernel, tb, n, T), grid=(T // tb,),...  12.4 us
    pallas_call x1, Pallas kernels, heat(): pl.pallas_call(functools.partial(heat_kernel, J, tb, n), grid=(T // tb,),...  10.4 us
    ppermute x3, starting transfers between devices, shifted(): lax.ppermute(up_going, axis, up)  7.92 us
    ppermute x3, starting transfers between devices, shifted(): lax.ppermute(down_going, axis, down)  7.75 us
    ppermute x3, waiting for transfers between devices, shifted(): lax.ppermute(up_going, axis, up)  6.33 us
    pallas_call x1, Pallas kernels, moments(): pl.pallas_call(functools.partial(moments_kernel, tb, n), grid=(T // tb,),...  5.02 us
    ppermute x3, starting transfers between devices, local(): lax.ppermute(pq, 'wid', [(i, (i + s) % J) for i in range(J)])  4.61 us
  transfers between devices with their start and end apart: 9, of which 6 were waited for; matrix products, arithmetic and copies ran while one was open for 0% of the time, Pallas kernels for 13%

profile of v6, /device:TPU:4, one launch (start us, length us, event | category | flops | bytes accessed | tf_op | source)
XLA Modules:
  0.0 122.2 jit_solution(7839258483106436389)
XLA Ops:
  0.6 2.0 %edge_rows.1 = (f32[32,8,128]{2,1,0:T(8,128)}, f32[32,8,128]{2,1,0:T(8,128)}) custom-call(f32[2,32,256,128]{3,2,1,0:T(8,128)} %v_ref.3, f32[2,32,256,128]{3,2,1,0:T(8,128)} %v_ref.3, f32[2,32,256,128]{3,2,1,0:T(8,128)} %f_ref.5, f32[2,32,256,128]{3,2,1,0:T(8,128)} %f_ref.5, s32[32,256,128]{2,1,0:T(8,128)} %p_ref.3, s32[32,256,128]{2,1,0:T(8,128)} %p_ref.3), custom_call_target="tpu_custom_call" | custom-call | bytes 1572864 | tf_op jit(solution)/shard_map/edge_rows/pallas_call | solution.py:163
  2.7 3.5 %collective-permute-start.3 = (f32[32,8,128]{2,1,0:T(8,128)}, f32[32,8,128]{2,1,0:T(8,128)S(1)}, u32[]{:S(2)}, u32[]{:S(2)}) collective-permute-start(f32[32,8,128]{2,1,0:T(8,128)} %get-tuple-element.17), channel_id=1, source_target_pairs={{0,1},{1,2},{2,3},{4,5},{5,6},{6,7},{8,9},{9,10},{10,11},{12,13},{... | collective-permute-start | bytes 393224 | tf_op jit(solution)/shard_map/ppermute | solution.py:629
  6.2 1.3 %collective-permute-start.4 = (f32[32,8,128]{2,1,0:T(8,128)}, f32[32,8,128]{2,1,0:T(8,128)S(1)}, u32[]{:S(2)}, u32[]{:S(2)}) collective-permute-start(f32[32,8,128]{2,1,0:T(8,128)} %get-tuple-element.18), channel_id=1, source_target_pairs={{1,0},{2,1},{3,2},{5,4},{6,5},{7,6},{9,8},{10,9},{11,10},{13,12},{... | collective-permute-start | bytes 393224 | tf_op jit(solution)/shard_map/ppermute | solution.py:629
  7.5 1.7 %collective-permute-done.3.lo_ref = f32[32,8,128]{2,1,0:T(8,128)S(1)} collective-permute-done((f32[32,8,128]{2,1,0:T(8,128)}, f32[32,8,128]{2,1,0:T(8,128)S(1)}, u32[]{:S(2)}, u32[]{:S(2)}) %collective-permute-start.3) | collective-permute-done | bytes 131104 | tf_op jit(solution)/shard_map/ppermute | solution.py:629
  9.2 0.0 copy-start.3
  9.2 4.0 %collective-permute-done.4.hi_ref = f32[32,8,128]{2,1,0:T(8,128)S(1)} collective-permute-done((f32[32,8,128]{2,1,0:T(8,128)}, f32[32,8,128]{2,1,0:T(8,128)S(1)}, u32[]{:S(2)}, u32[]{:S(2)}) %collective-permute-start.4) | collective-permute-done | bytes 131104 | tf_op jit(solution)/shard_map/ppermute | solution.py:629
  13.2 0.0 copy-done.3
  13.2 0.0 copy-start.4
  13.2 0.7 copy-done.4
  13.9 12.4 %pack_edges.1 = (f32[2,264,128]{2,1,0:T(8,128)}, f32[2,264,128]{2,1,0:T(8,128)}, f32[2,264,128]{2,1,0:T(8,128)}) custom-call(f32[2,32,256,128]{3,2,1,0:T(8,128)} %v_ref.3, f32[2,32,256,128]{3,2,1,0:T(8,128)} %f_ref.5, s32[32,256,128]{2,1,0:T(8,128)} %p_ref.3, f32[32,8,128]{2,1,0:T(8,128)} %copy-done.3, f32[32,8,128]{2,1,0:T(8,128)} %copy-done.4), custom_call_target="tpu_custom_call" | custom-call | flops 5242880 | bytes 20971520 | tf_op jit(solution)/shard_map/pack_edges/pallas_call | solution.py:224
  26.3 0.0 copy-start.1
  26.3 2.0 %collective-permute-start.5 = (f32[2,264,128]{2,1,0:T(8,128)}, f32[2,264,128]{2,1,0:T(8,128)S(1)}, u32[]{:S(2)}, u32[]{:S(2)}) collective-permute-start(f32[2,264,128]{2,1,0:T(8,128)} %get-tuple-element.21), channel_id=1, source_target_pairs={{0,4},{4,8},{8,12},{12,16},{16,20},{20,24},{24,28},{1,5},{5,9},{9,... | collective-permute-start | bytes 811016 | tf_op jit(solution)/shard_map/ppermute | solution.py:629
  28.3 4.5 %collective-permute-start.6 = (f32[2,264,128]{2,1,0:T(8,128)}, f32[2,264,128]{2,1,0:T(8,128)S(1)}, u32[]{:S(2)}, u32[]{:S(2)}) collective-permute-start(f32[2,264,128]{2,1,0:T(8,128)} %get-tuple-element.22), channel_id=1, source_target_pairs={{4,0},{8,4},{12,8},{16,12},{20,16},{24,20},{28,24},{5,1},{9,5},{13... | collective-permute-start | bytes 811016 | tf_op jit(solution)/shard_map/ppermute | solution.py:629
  32.9 5.0 %moments.1 = (f32[2,32,8,128]{3,2,1,0:T(8,128)}, f32[2,32,128]{2,1,0:T(8,128)}) custom-call(f32[32,128]{1,0:T(8,128)} %refs_0_.1, f32[32,256,128]{2,1,0:T(8,128)} %refs_6_.1), custom_call_target="tpu_custom_call" | custom-call | flops 4194304 | bytes 4194304 | tf_op jit(solution)/shard_map/moments/pallas_call | solution.py:113
  37.9 1.7 %collective-permute-start.2 = (f32[2,32,128]{2,1,0:T(8,128)}, f32[2,32,128]{2,1,0:T(8,128)S(1)}, u32[]{:S(2)}, u32[]{:S(2)}) collective-permute-start(f32[2,32,128]{2,1,0:T(8,128)} %get-tuple-element.14.refs_1_), channel_id=1, source_target_pairs={{0,3},{1,0},{2,1},{3,2},{4,7},{5,4},{6,5},{7,6},{8,11},{9,8},{10,9... | collective-permute-start | bytes 98312 | tf_op jit(solution)/shard_map/ppermute | solution.py:637
  39.6 1.3 %collective-permute-start.1 = (f32[2,32,128]{2,1,0:T(8,128)}, f32[2,32,128]{2,1,0:T(8,128)S(1)}, u32[]{:S(2)}, u32[]{:S(2)}) collective-permute-start(f32[2,32,128]{2,1,0:T(8,128)} %get-tuple-element.14.refs_1_), channel_id=1, source_target_pairs={{0,2},{1,3},{2,0},{3,1},{4,6},{5,7},{6,4},{7,5},{8,10},{9,11},{10,... | collective-permute-start | bytes 98312 | tf_op jit(solution)/shard_map/ppermute | solution.py:637
  40.9 1.6 %collective-permute-start = (f32[2,32,128]{2,1,0:T(8,128)}, f32[2,32,128]{2,1,0:T(8,128)S(1)}, u32[]{:S(2)}, u32[]{:S(2)}) collective-permute-start(f32[2,32,128]{2,1,0:T(8,128)} %get-tuple-element.14.refs_1_), channel_id=1, source_target_pairs={{0,1},{1,2},{2,3},{3,0},{4,5},{5,6},{6,7},{7,4},{8,9},{9,10},{10,1... | collective-permute-start | bytes 98312 | tf_op jit(solution)/shard_map/ppermute | solution.py:637
  42.5 0.0 collective-permute-done.2.refs_4_
  42.5 0.0 copy-start.5
  42.5 2.6 %collective-permute-done.1.refs_3_ = f32[2,32,128]{2,1,0:T(8,128)S(1)} collective-permute-done((f32[2,32,128]{2,1,0:T(8,128)}, f32[2,32,128]{2,1,0:T(8,128)S(1)}, u32[]{:S(2)}, u32[]{:S(2)}) %collective-permute-start.1) | collective-permute-done | bytes 32800 | tf_op jit(solution)/shard_map/ppermute | solution.py:637
  45.1 0.0 copy-start.6
  45.1 1.8 %collective-permute-done.refs_2_ = f32[2,32,128]{2,1,0:T(8,128)S(1)} collective-permute-done((f32[2,32,128]{2,1,0:T(8,128)}, f32[2,32,128]{2,1,0:T(8,128)S(1)}, u32[]{:S(2)}, u32[]{:S(2)}) %collective-permute-start) | collective-permute-done | bytes 32800 | tf_op jit(solution)/shard_map/ppermute | solution.py:637
  46.8 0.0 copy-start.7
  46.8 0.0 copy-done.5
  46.8 0.0 copy-done.6
  46.8 0.6 copy-done.7
  47.5 10.4 %heat.1 = (f32[32,256,128]{2,1,0:T(8,128)}, f32[264,128]{1,0:T(8,128)}, f32[2,32,128]{2,1,0:T(8,128)}) custom-call(f32[32,128]{1,0:T(8,128)} %refs_0_.1, f32[2,32,128]{2,1,0:T(8,128)} %get-tuple-element.14.refs_1_, f32[2,32,128]{2,1,0:T(8,128)} %copy-done.7, f32[2,32,128]{2,1,0:T(8,128)} %copy-done.6, f32[2,32,128]{2,1,0:T(8,128)} %copy-done.5, ...), custom_call_target="tpu_custom_call" | custom-call | flops 10485760 | bytes 8388608 | tf_op jit(solution)/shard_map/heat/pallas_call | solution.py:339
  57.8 1.9 %collective-permute-start.8 = (f32[264,128]{1,0:T(8,128)}, f32[264,128]{1,0:T(8,128)S(1)}, u32[]{:S(2)}, u32[]{:S(2)}) collective-permute-start(f32[264,128]{1,0:T(8,128)} %get-tuple-element.23), channel_id=1, source_target_pairs={{4,0},{8,4},{12,8},{16,12},{20,16},{24,20},{28,24},{5,1},{9,5},{13... | collective-permute-start | bytes 405512 | tf_op jit(solution)/shard_map/ppermute | solution.py:629
  59.8 2.4 %collective-permute-start.7 = (f32[264,128]{1,0:T(8,128)}, f32[264,128]{1,0:T(8,128)S(1)}, u32[]{:S(2)}, u32[]{:S(2)}) collective-permute-start(f32[264,128]{1,0:T(8,128)} %get-tuple-element.23), channel_id=1, source_target_pairs={{0,4},{4,8},{8,12},{12,16},{16,20},{20,24},{24,28},{1,5},{5,9},{9,... | collective-permute-start | bytes 405512 | tf_op jit(solution)/shard_map/ppermute | solution.py:629
  62.2 0.4 collective-permute-done.8.hr_ref
  62.6 4.6 %collective-permute-done.7.hl_ref = f32[264,128]{1,0:T(8,128)S(1)} collective-permute-done((f32[264,128]{1,0:T(8,128)}, f32[264,128]{1,0:T(8,128)S(1)}, u32[]{:S(2)}, u32[]{:S(2)}) %collective-permute-start.7) | collective-permute-done | bytes 135200 | tf_op jit(solution)/shard_map/ppermute | solution.py:629
  67.2 0.0 collective-permute-done.5.fl_ref
  67.2 0.0 collective-permute-done.6.fr_ref
  67.2 0.0 copy-done.1
  67.2 1.4 %strips.1 = (f32[2,34,8,128]{3,2,1,0:T(8,128)S(1)}, f32[2,32,8,128]{3,2,1,0:T(8,128)S(1)}) custom-call(f32[2,264,128]{2,1,0:T(8,128)S(1)} %copy-done.1, f32[2,264,128]{2,1,0:T(8,128)S(1)} %collective-permute-done.5.fl_ref, f32[2,264,128]{2,1,0:T(8,128)S(1)} %collective-permute-done.6.fr_ref, f32[264,128]{1,0:T(8,128)S(1)} %collective-permute-done.7.hl_ref, ...), custom_call_target="tpu_custom_call" | custom-call | flops 1966080 | bytes 1966080 | tf_op jit(solution)/shard_map/strips/pallas_call | solution.py:501
  68.6 0.0 copy-start
  68.6 0.7 copy-done
  69.3 0.0 copy-start.2
  69.3 0.7 copy-done.2
  70.0 52.2 %sweeps.1 = f32[2,32,256,128]{3,2,1,0:T(8,128)} custom-call(f32[2,32,256,128]{3,2,1,0:T(8,128)} %v_ref.3, f32[2,32,256,128]{3,2,1,0:T(8,128)} %f_ref.5, s32[32,256,128]{2,1,0:T(8,128)} %p_ref.3, f32[32,256,128]{2,1,0:T(8,128)} %get-tuple-element.12.h_ref, f32[32,8,128]{2,1,0:T(8,128)} %copy-done.3, f32[32,8,128]{2,1,0:T(8,128)} %copy-done.4, ...), custom_call_target="tpu_custom_call" | custom-call | flops 62914560 | bytes 33554432 | tf_op jit(solution)/shard_map/sweeps/pallas_call | solution.py:596
Async XLA Ops:
  2.7 6.5 %collective-permute-start.3 = (f32[32,8,128]{2,1,0:T(8,128)}, f32[32,8,128]{2,1,0:T(8,128)S(1)}, u32[]{:S(2)}, u32[]{:S(2)}) collective-permute-start(f32[32,8,128]{2,1,0:T(8,128)} %get-tuple-element.17), channel_id=1, source_target_pairs={{0,1},{1,2},{2,3},{4,5},{5,6},{6,7},{8,9},{9,10},{10,11},{12,13},{... | collective-permute-start | bytes 393224 | tf_op jit(solution)/shard_map/ppermute | solution.py:629
  6.2 7.1 %collective-permute-start.4 = (f32[32,8,128]{2,1,0:T(8,128)}, f32[32,8,128]{2,1,0:T(8,128)S(1)}, u32[]{:S(2)}, u32[]{:S(2)}) collective-permute-start(f32[32,8,128]{2,1,0:T(8,128)} %get-tuple-element.18), channel_id=1, source_target_pairs={{1,0},{2,1},{3,2},{5,4},{6,5},{7,6},{9,8},{10,9},{11,10},{13,12},{... | collective-permute-start | bytes 393224 | tf_op jit(solution)/shard_map/ppermute | solution.py:629
  9.2 4.0 %copy-start.3 = (f32[32,8,128]{2,1,0:T(8,128)}, f32[32,8,128]{2,1,0:T(8,128)S(1)}, u32[]{:S(2)}) copy-start(f32[32,8,128]{2,1,0:T(8,128)S(1)} %collective-permute-done.3.lo_ref) | copy-start | bytes 393220
  13.2 0.7 copy-start.4
  26.3 40.9 %copy-start.1 = (f32[2,264,128]{2,1,0:T(8,128)S(1)}, f32[2,264,128]{2,1,0:T(8,128)}, u32[]{:S(2)}) copy-start(f32[2,264,128]{2,1,0:T(8,128)} %get-tuple-element.20.own_ref) | copy-start | bytes 811012
  26.3 40.9 %collective-permute-start.5 = (f32[2,264,128]{2,1,0:T(8,128)}, f32[2,264,128]{2,1,0:T(8,128)S(1)}, u32[]{:S(2)}, u32[]{:S(2)}) collective-permute-start(f32[2,264,128]{2,1,0:T(8,128)} %get-tuple-element.21), channel_id=1, source_target_pairs={{0,4},{4,8},{8,12},{12,16},{16,20},{20,24},{24,28},{1,5},{5,9},{9,... | collective-permute-start | bytes 811016 | tf_op jit(solution)/shard_map/ppermute | solution.py:629
  28.3 38.9 %collective-permute-start.6 = (f32[2,264,128]{2,1,0:T(8,128)}, f32[2,264,128]{2,1,0:T(8,128)S(1)}, u32[]{:S(2)}, u32[]{:S(2)}) collective-permute-start(f32[2,264,128]{2,1,0:T(8,128)} %get-tuple-element.22), channel_id=1, source_target_pairs={{4,0},{8,4},{12,8},{16,12},{20,16},{24,20},{28,24},{5,1},{9,5},{13... | collective-permute-start | bytes 811016 | tf_op jit(solution)/shard_map/ppermute | solution.py:629
  37.9 4.6 %collective-permute-start.2 = (f32[2,32,128]{2,1,0:T(8,128)}, f32[2,32,128]{2,1,0:T(8,128)S(1)}, u32[]{:S(2)}, u32[]{:S(2)}) collective-permute-start(f32[2,32,128]{2,1,0:T(8,128)} %get-tuple-element.14.refs_1_), channel_id=1, source_target_pairs={{0,3},{1,0},{2,1},{3,2},{4,7},{5,4},{6,5},{7,6},{8,11},{9,8},{10,9... | collective-permute-start | bytes 98312 | tf_op jit(solution)/shard_map/ppermute | solution.py:637
  39.6 5.5 %collective-permute-start.1 = (f32[2,32,128]{2,1,0:T(8,128)}, f32[2,32,128]{2,1,0:T(8,128)S(1)}, u32[]{:S(2)}, u32[]{:S(2)}) collective-permute-start(f32[2,32,128]{2,1,0:T(8,128)} %get-tuple-element.14.refs_1_), channel_id=1, source_target_pairs={{0,2},{1,3},{2,0},{3,1},{4,6},{5,7},{6,4},{7,5},{8,10},{9,11},{10,... | collective-permute-start | bytes 98312 | tf_op jit(solution)/shard_map/ppermute | solution.py:637
  40.9 5.9 %collective-permute-start = (f32[2,32,128]{2,1,0:T(8,128)}, f32[2,32,128]{2,1,0:T(8,128)S(1)}, u32[]{:S(2)}, u32[]{:S(2)}) collective-permute-start(f32[2,32,128]{2,1,0:T(8,128)} %get-tuple-element.14.refs_1_), channel_id=1, source_target_pairs={{0,1},{1,2},{2,3},{3,0},{4,5},{5,6},{6,7},{7,4},{8,9},{9,10},{10,1... | collective-permute-start | bytes 98312 | tf_op jit(solution)/shard_map/ppermute | solution.py:637
  42.5 4.3 %copy-start.5 = (f32[2,32,128]{2,1,0:T(8,128)}, f32[2,32,128]{2,1,0:T(8,128)S(1)}, u32[]{:S(2)}) copy-start(f32[2,32,128]{2,1,0:T(8,128)S(1)} %collective-permute-done.2.refs_4_) | copy-start | bytes 98308
  45.1 1.8 %copy-start.6 = (f32[2,32,128]{2,1,0:T(8,128)}, f32[2,32,128]{2,1,0:T(8,128)S(1)}, u32[]{:S(2)}) copy-start(f32[2,32,128]{2,1,0:T(8,128)S(1)} %collective-permute-done.1.refs_3_) | copy-start | bytes 98308
  46.8 0.6 copy-start.7
  57.8 4.8 %collective-permute-start.8 = (f32[264,128]{1,0:T(8,128)}, f32[264,128]{1,0:T(8,128)S(1)}, u32[]{:S(2)}, u32[]{:S(2)}) collective-permute-start(f32[264,128]{1,0:T(8,128)} %get-tuple-element.23), channel_id=1, source_target_pairs={{4,0},{8,4},{12,8},{16,12},{20,16},{24,20},{28,24},{5,1},{9,5},{13... | collective-permute-start | bytes 405512 | tf_op jit(solution)/shard_map/ppermute | solution.py:629
  59.8 7.4 %collective-permute-start.7 = (f32[264,128]{1,0:T(8,128)}, f32[264,128]{1,0:T(8,128)S(1)}, u32[]{:S(2)}, u32[]{:S(2)}) collective-permute-start(f32[264,128]{1,0:T(8,128)} %get-tuple-element.23), channel_id=1, source_target_pairs={{0,4},{4,8},{8,12},{12,16},{16,20},{20,24},{24,28},{1,5},{5,9},{9,... | collective-permute-start | bytes 405512 | tf_op jit(solution)/shard_map/ppermute | solution.py:629
  68.6 0.7 copy-start
  69.3 0.7 copy-start.2

commit v7 on v6

--- a/solution.py
+++ b/solution.py
@@ -180,7 +180,7 @@
     return parts[0]
 
 
-def pack_kernel(tb, n, T, v_ref, f_ref, p_ref, lo_ref, hi_ref, pk_ref, right_ref, left_ref, fp_ref):
+def pack_kernel(tb, n, T, v_ref, f_ref, p_ref, lo_ref, hi_ref, after_ref, pk_ref, right_ref, left_ref, fp_ref):
     base = pl.program_id(0) * tb
     lane = lax.broadcasted_iota(jnp.int32, (n, 128), 1)
     group = lane >> 2
@@ -217,7 +217,7 @@
                 out[k, n : n + 8, :] = tile
 
 
-def pack(v, f, pinned, lo, hi):
+def pack(v, f, pinned, lo, hi, after):
     _, T, n, _ = v.shape
     tb = 4
     out = jax.ShapeDtypeStruct((2, n + 8, 128), F32)
@@ -230,6 +230,7 @@
             pl.BlockSpec((tb, n, 128), lambda t: (t, 0, 0)),
             whole((T, 8, 128)),
             whole((T, 8, 128)),
+            pl.BlockSpec(memory_space=pl.ANY),
         ],
         out_specs=[whole((2, n + 8, 128))] * 3,
         out_shape=[out, out, out],
@@ -237,7 +238,7 @@
         compiler_params=pltpu.CompilerParams(vmem_limit_bytes=57 * MIB),
         cost_estimate=pl.CostEstimate(flops=5 * T * n * 128, bytes_accessed=20 * T * n * 128, transcendentals=0),
         name="pack_edges",
-    )(v, f, pinned, lo, hi)
+    )(v, f, pinned, lo, hi, after)
 
 
 def heat_kernel(J, tb, n, *refs):
@@ -592,7 +593,7 @@
 def sweeps(v, f, pinned, heated, lo, hi, heated_rows, yh1, yh2):
     _, T, n, _ = v.shape
     S = n // 8
-    tb = 2
+    tb = 4
     return pl.pallas_call(
         functools.partial(sweep_kernel, tb, n),
         grid=(T // tb,),
@@ -635,7 +636,8 @@
     from_below, from_above = shifted(hi, lo, "wid")
     seg, pq = moments(d, prior)
     pqs = [pq] + [lax.ppermute(pq, "wid", [(i, (i + s) % J) for i in range(J)]) for s in range(1, J)]
-    own, right, left = pack(v, f, pinned, from_below, from_above)
+    own, right, left = pack(v, f, pinned, from_below, from_above, pq)
+    right, left, *pqs = lax.optimization_barrier((right, left, *pqs))
     from_left, from_right = shifted(right, left, "len")
     heated, columns, heated_rows = heat(d, pqs, seg, prior)
     heat_left, heat_right = shifted(columns, columns, "len")

time: 123 us -> 116 us (0.943)
  waiting for transfers between devices: 15.1 us -> 5.04 us
    ppermute x3, waiting for transfers between devices: 4.34 us -> 0.01 us  [local(): lax.ppermute(pq, 'wid', [(i, (i + s) % J) for i in range(J)])]
    ppermute x3, waiting for transfers between devices: 4.47 us -> 0.45 us  [shifted(): lax.ppermute(down_going, axis, down)]
    ppermute x3, waiting for transfers between devices: 6.33 us -> 4.59 us  [shifted(): lax.ppermute(up_going, axis, up)]
  transfers between devices with their start and end apart: 9 -> 9, of which waited for: 6 -> 2; matrix products, arithmetic and copies ran while one was open for 0% -> 0% of each run, Pallas kernels for 13% -> 24%
where the time goes in v7:
time: 116 us; the launch traced here: 114 us
  Pallas kernels  83.6 us (72%)
  starting transfers between devices  21.2 us (18%)
  waiting for transfers between devices  5.04 us (4%)
  local copies, waits for them, and re-layouts  3.68 us (3%)
    pallas_call x1, Pallas kernels, sweeps(): pl.pallas_call(functools.partial(sweep_kernel, tb, n), grid=(T // tb,), i...  52.4 us
    pallas_call x1, Pallas kernels, pack(): pl.pallas_call(functools.partial(pack_kernel, tb, n, T), grid=(T // tb,),...  12.4 us
    pallas_call x1, Pallas kernels, heat(): pl.pallas_call(functools.partial(heat_kernel, J, tb, n), grid=(T // tb,),...  10.4 us
    ppermute x3, starting transfers between devices, shifted(): lax.ppermute(up_going, axis, up)  7.8 us
    ppermute x3, starting transfers between devices, shifted(): lax.ppermute(down_going, axis, down)  7.75 us
    ppermute x3, starting transfers between devices, local(): lax.ppermute(pq, 'wid', [(i, (i + s) % J) for i in range(J)])  5.68 us
    pallas_call x1, Pallas kernels, moments(): pl.pallas_call(functools.partial(moments_kernel, tb, n), grid=(T // tb,),...  5.02 us
    ppermute x3, waiting for transfers between devices, shifted(): lax.ppermute(up_going, axis, up)  4.59 us
  transfers between devices with their start and end apart: 9, of which 2 were waited for; matrix products, arithmetic and copies ran while one was open for 0% of the time, Pallas kernels for 24%

profile of v7, /device:TPU:4, one launch (start us, length us, event | category | flops | bytes accessed | tf_op | source)
XLA Modules:
  0.0 114.3 jit_solution(16975569592766493205)
XLA Ops:
  0.6 2.0 %edge_rows.1 = (f32[32,8,128]{2,1,0:T(8,128)}, f32[32,8,128]{2,1,0:T(8,128)}) custom-call(f32[2,32,256,128]{3,2,1,0:T(8,128)} %v_ref.3, f32[2,32,256,128]{3,2,1,0:T(8,128)} %v_ref.3, f32[2,32,256,128]{3,2,1,0:T(8,128)} %f_ref.5, f32[2,32,256,128]{3,2,1,0:T(8,128)} %f_ref.5, s32[32,256,128]{2,1,0:T(8,128)} %p_ref.3, s32[32,256,128]{2,1,0:T(8,128)} %p_ref.3), custom_call_target="tpu_custom_call" | custom-call | bytes 1572864 | tf_op jit(solution)/shard_map/edge_rows/pallas_call | solution.py:163
  2.7 3.5 %collective-permute-start = (f32[32,8,128]{2,1,0:T(8,128)}, f32[32,8,128]{2,1,0:T(8,128)S(1)}, u32[]{:S(2)}, u32[]{:S(2)}) collective-permute-start(f32[32,8,128]{2,1,0:T(8,128)} %get-tuple-element.20), channel_id=1, source_target_pairs={{0,1},{1,2},{2,3},{4,5},{5,6},{6,7},{8,9},{9,10},{10,11},{12,13},{... | collective-permute-start | bytes 393224 | tf_op jit(solution)/shard_map/ppermute | solution.py:630
  6.2 1.3 %collective-permute-start.1 = (f32[32,8,128]{2,1,0:T(8,128)}, f32[32,8,128]{2,1,0:T(8,128)S(1)}, u32[]{:S(2)}, u32[]{:S(2)}) collective-permute-start(f32[32,8,128]{2,1,0:T(8,128)} %get-tuple-element.21), channel_id=1, source_target_pairs={{1,0},{2,1},{3,2},{5,4},{6,5},{7,6},{9,8},{10,9},{11,10},{13,12},{... | collective-permute-start | bytes 393224 | tf_op jit(solution)/shard_map/ppermute | solution.py:630
  7.5 5.0 %moments.1 = (f32[2,32,8,128]{3,2,1,0:T(8,128)}, f32[2,32,128]{2,1,0:T(8,128)}) custom-call(f32[32,128]{1,0:T(8,128)} %refs_0_.1, f32[32,256,128]{2,1,0:T(8,128)} %refs_6_.1), custom_call_target="tpu_custom_call" | custom-call | flops 4194304 | bytes 4194304 | tf_op jit(solution)/shard_map/moments/pallas_call | solution.py:113
  12.5 4.7 %collective-permute-start.4 = (f32[2,32,128]{2,1,0:T(8,128)}, f32[2,32,128]{2,1,0:T(8,128)S(1)}, u32[]{:S(2)}, u32[]{:S(2)}) collective-permute-start(f32[2,32,128]{2,1,0:T(8,128)} %get-tuple-element.25.after_ref.refs_1_), channel_id=1, source_target_pairs={{0,3},{1,0},{2,1},{3,2},{4,7},{5,4},{6,5},{7,6},{8,11},{9,8},{10,9... | collective-permute-start | bytes 98312 | tf_op jit(solution)/shard_map/ppermute | solution.py:638
  17.2 0.0 collective-permute-start.3
  17.2 1.0 collective-permute-start.2
  18.2 0.0 collective-permute-done.lo_ref
  18.2 0.0 copy-start.3
  18.2 0.0 collective-permute-done.1.hi_ref
  18.2 0.7 copy-done.3
  18.8 0.0 copy-start.4
  18.8 0.7 copy-done.4
  19.5 12.4 %pack_edges.1 = (f32[2,264,128]{2,1,0:T(8,128)}, f32[2,264,128]{2,1,0:T(8,128)}, f32[2,264,128]{2,1,0:T(8,128)}) custom-call(f32[2,32,256,128]{3,2,1,0:T(8,128)} %v_ref.3, f32[2,32,256,128]{3,2,1,0:T(8,128)} %f_ref.5, s32[32,256,128]{2,1,0:T(8,128)} %p_ref.3, f32[32,8,128]{2,1,0:T(8,128)} %copy-done.3, f32[32,8,128]{2,1,0:T(8,128)} %copy-done.4, ...), custom_call_target="tpu_custom_call" | custom-call | flops 5242880 | bytes 20971520 | tf_op jit(solution)/shard_map/pack_edges/pallas_call | solution.py:224
  31.8 0.0 collective-permute-done.4.refs_4_
  31.9 0.0 copy-start.5
  31.9 0.0 collective-permute-done.3.refs_3_
  31.9 0.0 copy-start.6
  31.9 0.0 collective-permute-done.2.refs_2_
  31.9 0.0 copy-start.7
  31.9 1.9 %collective-permute-start.5 = (f32[2,264,128]{2,1,0:T(8,128)}, f32[2,264,128]{2,1,0:T(8,128)S(1)}, u32[]{:S(2)}, u32[]{:S(2)}) collective-permute-start(f32[2,264,128]{2,1,0:T(8,128)} %get-tuple-element.33), channel_id=1, source_target_pairs={{0,4},{4,8},{8,12},{12,16},{16,20},{20,24},{24,28},{1,5},{5,9},{9,... | collective-permute-start | bytes 811016 | tf_op jit(solution)/shard_map/ppermute | solution.py:630
  33.8 4.5 %collective-permute-start.6 = (f32[2,264,128]{2,1,0:T(8,128)}, f32[2,264,128]{2,1,0:T(8,128)S(1)}, u32[]{:S(2)}, u32[]{:S(2)}) collective-permute-start(f32[2,264,128]{2,1,0:T(8,128)} %get-tuple-element.34), channel_id=1, source_target_pairs={{4,0},{8,4},{12,8},{16,12},{20,16},{24,20},{28,24},{5,1},{9,5},{13... | collective-permute-start | bytes 811016 | tf_op jit(solution)/shard_map/ppermute | solution.py:630
  38.4 0.0 copy-done.5
  38.4 0.0 copy-done.6
  38.4 0.0 copy-done.7
  38.4 10.4 %heat.1 = (f32[32,256,128]{2,1,0:T(8,128)}, f32[264,128]{1,0:T(8,128)}, f32[2,32,128]{2,1,0:T(8,128)}) custom-call(f32[32,128]{1,0:T(8,128)} %refs_0_.1, f32[2,32,128]{2,1,0:T(8,128)} %get-tuple-element.25.after_ref.refs_1_, f32[2,32,128]{2,1,0:T(8,128)} %copy-done.7, f32[2,32,128]{2,1,0:T(8,128)} %copy-done.6, f32[2,32,128]{2,1,0:T(8,128)} %copy-done.5, ...), custom_call_target="tpu_custom_call" | custom-call | flops 10485760 | bytes 8388608 | tf_op jit(solution)/shard_map/heat/pallas_call | solution.py:340
  48.8 1.9 %collective-permute-start.8 = (f32[264,128]{1,0:T(8,128)}, f32[264,128]{1,0:T(8,128)S(1)}, u32[]{:S(2)}, u32[]{:S(2)}) collective-permute-start(f32[264,128]{1,0:T(8,128)} %get-tuple-element.35), channel_id=1, source_target_pairs={{4,0},{8,4},{12,8},{16,12},{20,16},{24,20},{28,24},{5,1},{9,5},{13... | collective-permute-start | bytes 405512 | tf_op jit(solution)/shard_map/ppermute | solution.py:630
  50.7 2.4 %collective-permute-start.7 = (f32[264,128]{1,0:T(8,128)}, f32[264,128]{1,0:T(8,128)S(1)}, u32[]{:S(2)}, u32[]{:S(2)}) collective-permute-start(f32[264,128]{1,0:T(8,128)} %get-tuple-element.35), channel_id=1, source_target_pairs={{0,4},{4,8},{8,12},{12,16},{16,20},{20,24},{24,28},{1,5},{5,9},{9,... | collective-permute-start | bytes 405512 | tf_op jit(solution)/shard_map/ppermute | solution.py:630
  53.1 0.4 collective-permute-done.8.hr_ref
  53.6 4.6 %collective-permute-done.7.hl_ref = f32[264,128]{1,0:T(8,128)S(1)} collective-permute-done((f32[264,128]{1,0:T(8,128)}, f32[264,128]{1,0:T(8,128)S(1)}, u32[]{:S(2)}, u32[]{:S(2)}) %collective-permute-start.7) | collective-permute-done | bytes 135200 | tf_op jit(solution)/shard_map/ppermute | solution.py:630
  58.2 0.0 collective-permute-done.5.fl_ref
  58.2 0.0 collective-permute-done.6.fr_ref
  58.2 0.0 copy-start.1
  58.2 1.0 copy-done.1
  59.1 1.4 %strips.1 = (f32[2,34,8,128]{3,2,1,0:T(8,128)S(1)}, f32[2,32,8,128]{3,2,1,0:T(8,128)S(1)}) custom-call(f32[2,264,128]{2,1,0:T(8,128)S(1)} %copy-done.1, f32[2,264,128]{2,1,0:T(8,128)S(1)} %collective-permute-done.5.fl_ref, f32[2,264,128]{2,1,0:T(8,128)S(1)} %collective-permute-done.6.fr_ref, f32[264,128]{1,0:T(8,128)S(1)} %collective-permute-done.7.hl_ref, ...), custom_call_target="tpu_custom_call" | custom-call | flops 1966080 | bytes 1966080 | tf_op jit(solution)/shard_map/strips/pallas_call | solution.py:502
  60.5 0.0 copy-start
  60.5 0.7 copy-done
  61.2 0.0 copy-start.2
  61.2 0.7 copy-done.2
  61.9 52.4 %sweeps.1 = f32[2,32,256,128]{3,2,1,0:T(8,128)} custom-call(f32[2,32,256,128]{3,2,1,0:T(8,128)} %v_ref.3, f32[2,32,256,128]{3,2,1,0:T(8,128)} %f_ref.5, s32[32,256,128]{2,1,0:T(8,128)} %p_ref.3, f32[32,256,128]{2,1,0:T(8,128)} %get-tuple-element.18.h_ref, f32[32,8,128]{2,1,0:T(8,128)} %copy-done.3, f32[32,8,128]{2,1,0:T(8,128)} %copy-done.4, ...), custom_call_target="tpu_custom_call" | custom-call | flops 62914560 | bytes 33554432 | tf_op jit(solution)/shard_map/sweeps/pallas_call | solution.py:597
Async XLA Ops:
  2.7 15.5 %collective-permute-start = (f32[32,8,128]{2,1,0:T(8,128)}, f32[32,8,128]{2,1,0:T(8,128)S(1)}, u32[]{:S(2)}, u32[]{:S(2)}) collective-permute-start(f32[32,8,128]{2,1,0:T(8,128)} %get-tuple-element.20), channel_id=1, source_target_pairs={{0,1},{1,2},{2,3},{4,5},{5,6},{6,7},{8,9},{9,10},{10,11},{12,13},{... | collective-permute-start | bytes 393224 | tf_op jit(solution)/shard_map/ppermute | solution.py:630
  6.2 12.0 %collective-permute-start.1 = (f32[32,8,128]{2,1,0:T(8,128)}, f32[32,8,128]{2,1,0:T(8,128)S(1)}, u32[]{:S(2)}, u32[]{:S(2)}) collective-permute-start(f32[32,8,128]{2,1,0:T(8,128)} %get-tuple-element.21), channel_id=1, source_target_pairs={{1,0},{2,1},{3,2},{5,4},{6,5},{7,6},{9,8},{10,9},{11,10},{13,12},{... | collective-permute-start | bytes 393224 | tf_op jit(solution)/shard_map/ppermute | solution.py:630
  12.5 19.4 %collective-permute-start.4 = (f32[2,32,128]{2,1,0:T(8,128)}, f32[2,32,128]{2,1,0:T(8,128)S(1)}, u32[]{:S(2)}, u32[]{:S(2)}) collective-permute-start(f32[2,32,128]{2,1,0:T(8,128)} %get-tuple-element.25.after_ref.refs_1_), channel_id=1, source_target_pairs={{0,3},{1,0},{2,1},{3,2},{4,7},{5,4},{6,5},{7,6},{8,11},{9,8},{10,9... | collective-permute-start | bytes 98312 | tf_op jit(solution)/shard_map/ppermute | solution.py:638
  17.2 14.7 %collective-permute-start.3 = (f32[2,32,128]{2,1,0:T(8,128)}, f32[2,32,128]{2,1,0:T(8,128)S(1)}, u32[]{:S(2)}, u32[]{:S(2)}) collective-permute-start(f32[2,32,128]{2,1,0:T(8,128)} %get-tuple-element.25.after_ref.refs_1_), channel_id=1, source_target_pairs={{0,2},{1,3},{2,0},{3,1},{4,6},{5,7},{6,4},{7,5},{8,10},{9,11},{10,... | collective-permute-start | bytes 98312 | tf_op jit(solution)/shard_map/ppermute | solution.py:638
  17.2 14.7 %collective-permute-start.2 = (f32[2,32,128]{2,1,0:T(8,128)}, f32[2,32,128]{2,1,0:T(8,128)S(1)}, u32[]{:S(2)}, u32[]{:S(2)}) collective-permute-start(f32[2,32,128]{2,1,0:T(8,128)} %get-tuple-element.25.after_ref.refs_1_), channel_id=1, source_target_pairs={{0,1},{1,2},{2,3},{3,0},{4,5},{5,6},{6,7},{7,4},{8,9},{9,10},{10,1... | collective-permute-start | bytes 98312 | tf_op jit(solution)/shard_map/ppermute | solution.py:638
  18.2 0.7 copy-start.3
  18.8 0.7 copy-start.4
  31.9 6.5 %copy-start.5 = (f32[2,32,128]{2,1,0:T(8,128)}, f32[2,32,128]{2,1,0:T(8,128)S(1)}, u32[]{:S(2)}) copy-start(f32[2,32,128]{2,1,0:T(8,128)S(1)} %collective-permute-done.4.refs_4_) | copy-start | bytes 98308
  31.9 6.5 %copy-start.6 = (f32[2,32,128]{2,1,0:T(8,128)}, f32[2,32,128]{2,1,0:T(8,128)S(1)}, u32[]{:S(2)}) copy-start(f32[2,32,128]{2,1,0:T(8,128)S(1)} %collective-permute-done.3.refs_3_) | copy-start | bytes 98308
  31.9 6.5 %copy-start.7 = (f32[2,32,128]{2,1,0:T(8,128)}, f32[2,32,128]{2,1,0:T(8,128)S(1)}, u32[]{:S(2)}) copy-start(f32[2,32,128]{2,1,0:T(8,128)S(1)} %collective-permute-done.2.refs_2_) | copy-start | bytes 98308
  31.9 26.3 %collective-permute-start.5 = (f32[2,264,128]{2,1,0:T(8,128)}, f32[2,264,128]{2,1,0:T(8,128)S(1)}, u32[]{:S(2)}, u32[]{:S(2)}) collective-permute-start(f32[2,264,128]{2,1,0:T(8,128)} %get-tuple-element.33), channel_id=1, source_target_pairs={{0,4},{4,8},{8,12},{12,16},{16,20},{20,24},{24,28},{1,5},{5,9},{9,... | collective-permute-start | bytes 811016 | tf_op jit(solution)/shard_map/ppermute | solution.py:630
  33.8 24.4 %collective-permute-start.6 = (f32[2,264,128]{2,1,0:T(8,128)}, f32[2,264,128]{2,1,0:T(8,128)S(1)}, u32[]{:S(2)}, u32[]{:S(2)}) collective-permute-start(f32[2,264,128]{2,1,0:T(8,128)} %get-tuple-element.34), channel_id=1, source_target_pairs={{4,0},{8,4},{12,8},{16,12},{20,16},{24,20},{28,24},{5,1},{9,5},{13... | collective-permute-start | bytes 811016 | tf_op jit(solution)/shard_map/ppermute | solution.py:630
  48.8 4.8 %collective-permute-start.8 = (f32[264,128]{1,0:T(8,128)}, f32[264,128]{1,0:T(8,128)S(1)}, u32[]{:S(2)}, u32[]{:S(2)}) collective-permute-start(f32[264,128]{1,0:T(8,128)} %get-tuple-element.35), channel_id=1, source_target_pairs={{4,0},{8,4},{12,8},{16,12},{20,16},{24,20},{28,24},{5,1},{9,5},{13... | collective-permute-start | bytes 405512 | tf_op jit(solution)/shard_map/ppermute | solution.py:630
  50.7 7.4 %collective-permute-start.7 = (f32[264,128]{1,0:T(8,128)}, f32[264,128]{1,0:T(8,128)S(1)}, u32[]{:S(2)}, u32[]{:S(2)}) collective-permute-start(f32[264,128]{1,0:T(8,128)} %get-tuple-element.35), channel_id=1, source_target_pairs={{0,4},{4,8},{8,12},{12,16},{16,20},{20,24},{24,28},{1,5},{5,9},{9,... | collective-permute-start | bytes 405512 | tf_op jit(solution)/shard_map/ppermute | solution.py:630
  58.2 1.0 copy-start.1
  60.5 0.7 copy-start
  61.2 0.7 copy-start.2

commit v8 on v7

--- a/solution.py
+++ b/solution.py
@@ -516,7 +516,7 @@
             pltpu.VMEM((2, S + 2, 8, 128), F32),
             pltpu.VMEM((4, S + 2, 8, 128), F32),
         ],
-        compiler_params=pltpu.CompilerParams(vmem_limit_bytes=12 * MIB),
+        compiler_params=pltpu.CompilerParams(vmem_limit_bytes=57 * MIB),
         cost_estimate=pl.CostEstimate(flops=60 * n * 128, bytes_accessed=60 * n * 128, transcendentals=n * 128),
         name="strips",
     )(own, fl, fr, hl, hr)
@@ -582,9 +582,9 @@
             halo_rows(xs, S, low, high, lambda c, i: v_ref[c, u, pl.ds(i, 8, stride=S), :])
             + halo_coefficients(cos, S, low, high, get)
         )
-        over_rows(0, S, load, 16)
+        over_rows(0, S, load, 8)
         over_rows(-1, S + 1, first_sweep, 17)
-        over_rows(0, S, second_sweep, 16)
+        over_rows(0, S, second_sweep, 8)
         return 0
 
     lax.fori_loop(0, tb, layer, 0)

time: 116 us -> 126 us (1.086)
  Pallas kernels: 83.6 us -> 95.2 us
  local copies, waits for them, and re-layouts: 3.68 us -> 2.12 us
    pallas_call x1, Pallas kernels: 52.4 us -> 62 us  [sweeps(): pl.pallas_call(functools.partial(sweep_kernel, tb, n), grid=(T // tb,), i...]
    pallas_call x1, Pallas kernels: 1.39 us -> 3.41 us  [strips(): pl.pallas_call(functools.partial(strip_kernel, n), grid=(1,), in_specs=[w...]
    unnamed x16 -> x18, local copies, waits for them, and re-layouts: 3.68 us -> 2.12 us
  transfers between devices with their start and end apart: 9 -> 9, of which waited for: 2 -> 2; matrix products, arithmetic and copies ran while one was open for 0% -> 0% of each run, Pallas kernels for 24% -> 22%
where the time goes in v8:
time: 126 us; the launch traced here: 124 us
  Pallas kernels  95.2 us (76%)
  starting transfers between devices  21.2 us (17%)
  waiting for transfers between devices  5.04 us (4%)
  local copies, waits for them, and re-layouts  2.12 us (2%)
    pallas_call x1, Pallas kernels, sweeps(): pl.pallas_call(functools.partial(sweep_kernel, tb, n), grid=(T // tb,), i...  62 us
    pallas_call x1, Pallas kernels, pack(): pl.pallas_call(functools.partial(pack_kernel, tb, n, T), grid=(T // tb,),...  12.4 us
    pallas_call x1, Pallas kernels, heat(): pl.pallas_call(functools.partial(heat_kernel, J, tb, n), grid=(T // tb,),...  10.4 us
    ppermute x3, starting transfers between devices, shifted(): lax.ppermute(up_going, axis, up)  7.8 us
    ppermute x3, starting transfers between devices, shifted(): lax.ppermute(down_going, axis, down)  7.75 us
    ppermute x3, starting transfers between devices, local(): lax.ppermute(pq, 'wid', [(i, (i + s) % J) for i in range(J)])  5.68 us
    pallas_call x1, Pallas kernels, moments(): pl.pallas_call(functools.partial(moments_kernel, tb, n), grid=(T // tb,),...  5.02 us
    ppermute x3, waiting for transfers between devices, shifted(): lax.ppermute(up_going, axis, up)  4.59 us
  transfers between devices with their start and end apart: 9, of which 2 were waited for; matrix products, arithmetic and copies ran while one was open for 0% of the time, Pallas kernels for 22%

profile of v8, /device:TPU:4, one launch (start us, length us, event | category | flops | bytes accessed | tf_op | source)
XLA Modules:
  0.0 124.4 jit_solution(9664393201263322884)
XLA Ops:
  0.6 2.0 %edge_rows.1 = (f32[32,8,128]{2,1,0:T(8,128)}, f32[32,8,128]{2,1,0:T(8,128)}) custom-call(f32[2,32,256,128]{3,2,1,0:T(8,128)} %v_ref.3, f32[2,32,256,128]{3,2,1,0:T(8,128)} %v_ref.3, f32[2,32,256,128]{3,2,1,0:T(8,128)} %f_ref.5, f32[2,32,256,128]{3,2,1,0:T(8,128)} %f_ref.5, s32[32,256,128]{2,1,0:T(8,128)} %p_ref.3, s32[32,256,128]{2,1,0:T(8,128)} %p_ref.3), custom_call_target="tpu_custom_call" | custom-call | bytes 1572864 | tf_op jit(solution)/shard_map/edge_rows/pallas_call | solution.py:163
  2.7 3.5 %collective-permute-start = (f32[32,8,128]{2,1,0:T(8,128)}, f32[32,8,128]{2,1,0:T(8,128)S(1)}, u32[]{:S(2)}, u32[]{:S(2)}) collective-permute-start(f32[32,8,128]{2,1,0:T(8,128)} %get-tuple-element.20), channel_id=1, source_target_pairs={{0,1},{1,2},{2,3},{4,5},{5,6},{6,7},{8,9},{9,10},{10,11},{12,13},{... | collective-permute-start | bytes 393224 | tf_op jit(solution)/shard_map/ppermute | solution.py:630
  6.2 1.3 %collective-permute-start.1 = (f32[32,8,128]{2,1,0:T(8,128)}, f32[32,8,128]{2,1,0:T(8,128)S(1)}, u32[]{:S(2)}, u32[]{:S(2)}) collective-permute-start(f32[32,8,128]{2,1,0:T(8,128)} %get-tuple-element.21), channel_id=1, source_target_pairs={{1,0},{2,1},{3,2},{5,4},{6,5},{7,6},{9,8},{10,9},{11,10},{13,12},{... | collective-permute-start | bytes 393224 | tf_op jit(solution)/shard_map/ppermute | solution.py:630
  7.5 5.0 %moments.1 = (f32[2,32,8,128]{3,2,1,0:T(8,128)}, f32[2,32,128]{2,1,0:T(8,128)}) custom-call(f32[32,128]{1,0:T(8,128)} %refs_0_.1, f32[32,256,128]{2,1,0:T(8,128)} %refs_6_.1), custom_call_target="tpu_custom_call" | custom-call | flops 4194304 | bytes 4194304 | tf_op jit(solution)/shard_map/moments/pallas_call | solution.py:113
  12.5 4.7 %collective-permute-start.4 = (f32[2,32,128]{2,1,0:T(8,128)}, f32[2,32,128]{2,1,0:T(8,128)S(1)}, u32[]{:S(2)}, u32[]{:S(2)}) collective-permute-start(f32[2,32,128]{2,1,0:T(8,128)} %get-tuple-element.25.after_ref.refs_1_), channel_id=1, source_target_pairs={{0,3},{1,0},{2,1},{3,2},{4,7},{5,4},{6,5},{7,6},{8,11},{9,8},{10,9... | collective-permute-start | bytes 98312 | tf_op jit(solution)/shard_map/ppermute | solution.py:638
  17.1 0.0 collective-permute-start.3
  17.1 1.0 collective-permute-start.2
  18.2 0.0 collective-permute-done.lo_ref
  18.2 0.0 copy-start
  18.2 0.0 collective-permute-done.1.hi_ref
  18.2 0.7 copy-done
  18.8 0.0 copy-start.1
  18.8 0.6 copy-done.1
  19.5 12.4 %pack_edges.1 = (f32[2,264,128]{2,1,0:T(8,128)}, f32[2,264,128]{2,1,0:T(8,128)}, f32[2,264,128]{2,1,0:T(8,128)}) custom-call(f32[2,32,256,128]{3,2,1,0:T(8,128)} %v_ref.3, f32[2,32,256,128]{3,2,1,0:T(8,128)} %f_ref.5, s32[32,256,128]{2,1,0:T(8,128)} %p_ref.3, f32[32,8,128]{2,1,0:T(8,128)} %copy-done, f32[32,8,128]{2,1,0:T(8,128)} %copy-done.1, ...), custom_call_target="tpu_custom_call" | custom-call | flops 5242880 | bytes 20971520 | tf_op jit(solution)/shard_map/pack_edges/pallas_call | solution.py:224
  31.8 0.0 collective-permute-done.4.refs_4_
  31.8 0.0 copy-start.6
  31.8 0.0 collective-permute-done.3.refs_3_
  31.8 0.0 copy-start.7
  31.9 0.0 collective-permute-done.2.refs_2_
  31.9 0.0 copy-start.8
  31.9 1.9 %collective-permute-start.5 = (f32[2,264,128]{2,1,0:T(8,128)}, f32[2,264,128]{2,1,0:T(8,128)S(1)}, u32[]{:S(2)}, u32[]{:S(2)}) collective-permute-start(f32[2,264,128]{2,1,0:T(8,128)} %get-tuple-element.33), channel_id=1, source_target_pairs={{0,4},{4,8},{8,12},{12,16},{16,20},{20,24},{24,28},{1,5},{5,9},{9,... | collective-permute-start | bytes 811016 | tf_op jit(solution)/shard_map/ppermute | solution.py:630
  33.8 4.5 %collective-permute-start.6 = (f32[2,264,128]{2,1,0:T(8,128)}, f32[2,264,128]{2,1,0:T(8,128)S(1)}, u32[]{:S(2)}, u32[]{:S(2)}) collective-permute-start(f32[2,264,128]{2,1,0:T(8,128)} %get-tuple-element.34), channel_id=1, source_target_pairs={{4,0},{8,4},{12,8},{16,12},{20,16},{24,20},{28,24},{5,1},{9,5},{13... | collective-permute-start | bytes 811016 | tf_op jit(solution)/shard_map/ppermute | solution.py:630
  38.4 0.0 copy-done.6
  38.4 0.0 copy-done.7
  38.4 0.0 copy-done.8
  38.4 10.4 %heat.1 = (f32[32,256,128]{2,1,0:T(8,128)}, f32[264,128]{1,0:T(8,128)}, f32[2,32,128]{2,1,0:T(8,128)}) custom-call(f32[32,128]{1,0:T(8,128)} %refs_0_.1, f32[2,32,128]{2,1,0:T(8,128)} %get-tuple-element.25.after_ref.refs_1_, f32[2,32,128]{2,1,0:T(8,128)} %copy-done.8, f32[2,32,128]{2,1,0:T(8,128)} %copy-done.7, f32[2,32,128]{2,1,0:T(8,128)} %copy-done.6, ...), custom_call_target="tpu_custom_call" | custom-call | flops 10485760 | bytes 8388608 | tf_op jit(solution)/shard_map/heat/pallas_call | solution.py:340
  48.8 1.9 %collective-permute-start.8 = (f32[264,128]{1,0:T(8,128)}, f32[264,128]{1,0:T(8,128)S(1)}, u32[]{:S(2)}, u32[]{:S(2)}) collective-permute-start(f32[264,128]{1,0:T(8,128)} %get-tuple-element.35), channel_id=1, source_target_pairs={{4,0},{8,4},{12,8},{16,12},{20,16},{24,20},{28,24},{5,1},{9,5},{13... | collective-permute-start | bytes 405512 | tf_op jit(solution)/shard_map/ppermute | solution.py:630
  50.7 2.4 %collective-permute-start.7 = (f32[264,128]{1,0:T(8,128)}, f32[264,128]{1,0:T(8,128)S(1)}, u32[]{:S(2)}, u32[]{:S(2)}) collective-permute-start(f32[264,128]{1,0:T(8,128)} %get-tuple-element.35), channel_id=1, source_target_pairs={{0,4},{4,8},{8,12},{12,16},{16,20},{20,24},{24,28},{1,5},{5,9},{9,... | collective-permute-start | bytes 405512 | tf_op jit(solution)/shard_map/ppermute | solution.py:630
  53.1 0.4 collective-permute-done.8.hr_ref
  53.6 0.0 copy-start.4
  53.6 4.6 %collective-permute-done.7.hl_ref = f32[264,128]{1,0:T(8,128)S(1)} collective-permute-done((f32[264,128]{1,0:T(8,128)}, f32[264,128]{1,0:T(8,128)S(1)}, u32[]{:S(2)}, u32[]{:S(2)}) %collective-permute-start.7) | collective-permute-done | bytes 135200 | tf_op jit(solution)/shard_map/ppermute | solution.py:630
  58.2 0.0 copy-start.5
  58.2 0.0 collective-permute-done.5.fl_ref
  58.2 0.0 copy-start.2
  58.2 0.0 collective-permute-done.6.fr_ref
  58.2 0.0 copy-start.3
  58.2 0.0 copy-done.4
  58.2 0.6 copy-done.5
  58.8 0.1 copy-done.2
  58.9 0.1 copy-done.3
  59.0 3.4 %strips.1 = (f32[2,34,8,128]{3,2,1,0:T(8,128)}, f32[2,32,8,128]{3,2,1,0:T(8,128)}) custom-call(f32[2,264,128]{2,1,0:T(8,128)} %get-tuple-element.32.own_ref, f32[2,264,128]{2,1,0:T(8,128)} %copy-done.2, f32[2,264,128]{2,1,0:T(8,128)} %copy-done.3, f32[264,128]{1,0:T(8,128)} %copy-done.5, f32[264,128]{1,0:T(8,128)} %copy-done.4), custom_call_target="tpu_custom_call" | custom-call | flops 1966080 | bytes 1966080 | tf_op jit(solution)/shard_map/strips/pallas_call | solution.py:502
  62.4 62.0 %sweeps.1 = f32[2,32,256,128]{3,2,1,0:T(8,128)} custom-call(f32[2,32,256,128]{3,2,1,0:T(8,128)} %v_ref.3, f32[2,32,256,128]{3,2,1,0:T(8,128)} %f_ref.5, s32[32,256,128]{2,1,0:T(8,128)} %p_ref.3, f32[32,256,128]{2,1,0:T(8,128)} %get-tuple-element.18.h_ref, f32[32,8,128]{2,1,0:T(8,128)} %copy-done, f32[32,8,128]{2,1,0:T(8,128)} %copy-done.1, ...), custom_call_target="tpu_custom_call" | custom-call | flops 62914560 | bytes 33554432 | tf_op jit(solution)/shard_map/sweeps/pallas_call | solution.py:597
Async XLA Ops:
  2.7 15.5 %collective-permute-start = (f32[32,8,128]{2,1,0:T(8,128)}, f32[32,8,128]{2,1,0:T(8,128)S(1)}, u32[]{:S(2)}, u32[]{:S(2)}) collective-permute-start(f32[32,8,128]{2,1,0:T(8,128)} %get-tuple-element.20), channel_id=1, source_target_pairs={{0,1},{1,2},{2,3},{4,5},{5,6},{6,7},{8,9},{9,10},{10,11},{12,13},{... | collective-permute-start | bytes 393224 | tf_op jit(solution)/shard_map/ppermute | solution.py:630
  6.2 12.0 %collective-permute-start.1 = (f32[32,8,128]{2,1,0:T(8,128)}, f32[32,8,128]{2,1,0:T(8,128)S(1)}, u32[]{:S(2)}, u32[]{:S(2)}) collective-permute-start(f32[32,8,128]{2,1,0:T(8,128)} %get-tuple-element.21), channel_id=1, source_target_pairs={{1,0},{2,1},{3,2},{5,4},{6,5},{7,6},{9,8},{10,9},{11,10},{13,12},{... | collective-permute-start | bytes 393224 | tf_op jit(solution)/shard_map/ppermute | solution.py:630
  12.5 19.4 %collective-permute-start.4 = (f32[2,32,128]{2,1,0:T(8,128)}, f32[2,32,128]{2,1,0:T(8,128)S(1)}, u32[]{:S(2)}, u32[]{:S(2)}) collective-permute-start(f32[2,32,128]{2,1,0:T(8,128)} %get-tuple-element.25.after_ref.refs_1_), channel_id=1, source_target_pairs={{0,3},{1,0},{2,1},{3,2},{4,7},{5,4},{6,5},{7,6},{8,11},{9,8},{10,9... | collective-permute-start | bytes 98312 | tf_op jit(solution)/shard_map/ppermute | solution.py:638
  17.1 14.7 %collective-permute-start.3 = (f32[2,32,128]{2,1,0:T(8,128)}, f32[2,32,128]{2,1,0:T(8,128)S(1)}, u32[]{:S(2)}, u32[]{:S(2)}) collective-permute-start(f32[2,32,128]{2,1,0:T(8,128)} %get-tuple-element.25.after_ref.refs_1_), channel_id=1, source_target_pairs={{0,2},{1,3},{2,0},{3,1},{4,6},{5,7},{6,4},{7,5},{8,10},{9,11},{10,... | collective-permute-start | bytes 98312 | tf_op jit(solution)/shard_map/ppermute | solution.py:638
  17.1 14.7 %collective-permute-start.2 = (f32[2,32,128]{2,1,0:T(8,128)}, f32[2,32,128]{2,1,0:T(8,128)S(1)}, u32[]{:S(2)}, u32[]{:S(2)}) collective-permute-start(f32[2,32,128]{2,1,0:T(8,128)} %get-tuple-element.25.after_ref.refs_1_), channel_id=1, source_target_pairs={{0,1},{1,2},{2,3},{3,0},{4,5},{5,6},{6,7},{7,4},{8,9},{9,10},{10,1... | collective-permute-start | bytes 98312 | tf_op jit(solution)/shard_map/ppermute | solution.py:638
  18.2 0.7 copy-start
  18.8 0.6 copy-start.1
  31.8 6.5 %copy-start.6 = (f32[2,32,128]{2,1,0:T(8,128)}, f32[2,32,128]{2,1,0:T(8,128)S(1)}, u32[]{:S(2)}) copy-start(f32[2,32,128]{2,1,0:T(8,128)S(1)} %collective-permute-done.4.refs_4_) | copy-start | bytes 98308
  31.8 6.5 %copy-start.7 = (f32[2,32,128]{2,1,0:T(8,128)}, f32[2,32,128]{2,1,0:T(8,128)S(1)}, u32[]{:S(2)}) copy-start(f32[2,32,128]{2,1,0:T(8,128)S(1)} %collective-permute-done.3.refs_3_) | copy-start | bytes 98308
  31.9 6.5 %copy-start.8 = (f32[2,32,128]{2,1,0:T(8,128)}, f32[2,32,128]{2,1,0:T(8,128)S(1)}, u32[]{:S(2)}) copy-start(f32[2,32,128]{2,1,0:T(8,128)S(1)} %collective-permute-done.2.refs_2_) | copy-start | bytes 98308
  31.9 26.3 %collective-permute-start.5 = (f32[2,264,128]{2,1,0:T(8,128)}, f32[2,264,128]{2,1,0:T(8,128)S(1)}, u32[]{:S(2)}, u32[]{:S(2)}) collective-permute-start(f32[2,264,128]{2,1,0:T(8,128)} %get-tuple-element.33), channel_id=1, source_target_pairs={{0,4},{4,8},{8,12},{12,16},{16,20},{20,24},{24,28},{1,5},{5,9},{9,... | collective-permute-start | bytes 811016 | tf_op jit(solution)/shard_map/ppermute | solution.py:630
  33.8 24.4 %collective-permute-start.6 = (f32[2,264,128]{2,1,0:T(8,128)}, f32[2,264,128]{2,1,0:T(8,128)S(1)}, u32[]{:S(2)}, u32[]{:S(2)}) collective-permute-start(f32[2,264,128]{2,1,0:T(8,128)} %get-tuple-element.34), channel_id=1, source_target_pairs={{4,0},{8,4},{12,8},{16,12},{20,16},{24,20},{28,24},{5,1},{9,5},{13... | collective-permute-start | bytes 811016 | tf_op jit(solution)/shard_map/ppermute | solution.py:630
  48.8 4.8 %collective-permute-start.8 = (f32[264,128]{1,0:T(8,128)}, f32[264,128]{1,0:T(8,128)S(1)}, u32[]{:S(2)}, u32[]{:S(2)}) collective-permute-start(f32[264,128]{1,0:T(8,128)} %get-tuple-element.35), channel_id=1, source_target_pairs={{4,0},{8,4},{12,8},{16,12},{20,16},{24,20},{28,24},{5,1},{9,5},{13... | collective-permute-start | bytes 405512 | tf_op jit(solution)/shard_map/ppermute | solution.py:630
  50.7 7.4 %collective-permute-start.7 = (f32[264,128]{1,0:T(8,128)}, f32[264,128]{1,0:T(8,128)S(1)}, u32[]{:S(2)}, u32[]{:S(2)}) collective-permute-start(f32[264,128]{1,0:T(8,128)} %get-tuple-element.35), channel_id=1, source_target_pairs={{0,4},{4,8},{8,12},{12,16},{16,20},{20,24},{24,28},{1,5},{5,9},{9,... | collective-permute-start | bytes 405512 | tf_op jit(solution)/shard_map/ppermute | solution.py:630
  53.6 4.6 %copy-start.4 = (f32[264,128]{1,0:T(8,128)}, f32[264,128]{1,0:T(8,128)S(1)}, u32[]{:S(2)}) copy-start(f32[264,128]{1,0:T(8,128)S(1)} %collective-permute-done.8.hr_ref) | copy-start | bytes 405508
  58.2 0.7 copy-start.5
  58.2 0.7 copy-start.2
  58.2 0.8 copy-start.3

commit v9 on v7

--- a/solution.py
+++ b/solution.py
@@ -582,9 +582,9 @@
             halo_rows(xs, S, low, high, lambda c, i: v_ref[c, u, pl.ds(i, 8, stride=S), :])
             + halo_coefficients(cos, S, low, high, get)
         )
-        over_rows(0, S, load, 16)
+        over_rows(0, S, load, 32)
         over_rows(-1, S + 1, first_sweep, 17)
-        over_rows(0, S, second_sweep, 16)
+        over_rows(0, S, second_sweep, 32)
         return 0
 
     lax.fori_loop(0, tb, layer, 0)

time: 116 us -> 152 us (1.31)
  Pallas kernels: 83.6 us -> 119 us
    pallas_call x1, Pallas kernels: 52.4 us -> 88 us  [sweeps(): pl.pallas_call(functools.partial(sweep_kernel, tb, n), grid=(T // tb,), i...]
  transfers between devices with their start and end apart: 9 -> 9, of which waited for: 2 -> 2; matrix products, arithmetic and copies ran while one was open for 0% -> 0% of each run, Pallas kernels for 24% -> 19%
where the time goes in v9:
time: 152 us; the launch traced here: 150 us
  Pallas kernels  119 us (78%)
  starting transfers between devices  21.2 us (14%)
  waiting for transfers between devices  5.04 us (3%)
  local copies, waits for them, and re-layouts  3.68 us (2%)
    pallas_call x1, Pallas kernels, sweeps(): pl.pallas_call(functools.partial(sweep_kernel, tb, n), grid=(T // tb,), i...  88 us
    pallas_call x1, Pallas kernels, pack(): pl.pallas_call(functools.partial(pack_kernel, tb, n, T), grid=(T // tb,),...  12.4 us
    pallas_call x1, Pallas kernels, heat(): pl.pallas_call(functools.partial(heat_kernel, J, tb, n), grid=(T // tb,),...  10.4 us
    ppermute x3, starting transfers between devices, shifted(): lax.ppermute(up_going, axis, up)  7.8 us
    ppermute x3, starting transfers between devices, shifted(): lax.ppermute(down_going, axis, down)  7.75 us
    ppermute x3, starting transfers between devices, local(): lax.ppermute(pq, 'wid', [(i, (i + s) % J) for i in range(J)])  5.68 us
    pallas_call x1, Pallas kernels, moments(): pl.pallas_call(functools.partial(moments_kernel, tb, n), grid=(T // tb,),...  5.02 us
    ppermute x3, waiting for transfers between devices, shifted(): lax.ppermute(up_going, axis, up)  4.59 us
  transfers between devices with their start and end apart: 9, of which 2 were waited for; matrix products, arithmetic and copies ran while one was open for 0% of the time, Pallas kernels for 19%

profile of v9, /device:TPU:4, one launch (start us, length us, event | category | flops | bytes accessed | tf_op | source)
XLA Modules:
  0.0 150.0 jit_solution(16811208468945449424)
XLA Ops:
  0.6 2.0 %edge_rows.1 = (f32[32,8,128]{2,1,0:T(8,128)}, f32[32,8,128]{2,1,0:T(8,128)}) custom-call(f32[2,32,256,128]{3,2,1,0:T(8,128)} %v_ref.3, f32[2,32,256,128]{3,2,1,0:T(8,128)} %v_ref.3, f32[2,32,256,128]{3,2,1,0:T(8,128)} %f_ref.5, f32[2,32,256,128]{3,2,1,0:T(8,128)} %f_ref.5, s32[32,256,128]{2,1,0:T(8,128)} %p_ref.3, s32[32,256,128]{2,1,0:T(8,128)} %p_ref.3), custom_call_target="tpu_custom_call" | custom-call | bytes 1572864 | tf_op jit(solution)/shard_map/edge_rows/pallas_call | solution.py:163
  2.7 3.5 %collective-permute-start = (f32[32,8,128]{2,1,0:T(8,128)}, f32[32,8,128]{2,1,0:T(8,128)S(1)}, u32[]{:S(2)}, u32[]{:S(2)}) collective-permute-start(f32[32,8,128]{2,1,0:T(8,128)} %get-tuple-element.20), channel_id=1, source_target_pairs={{0,1},{1,2},{2,3},{4,5},{5,6},{6,7},{8,9},{9,10},{10,11},{12,13},{... | collective-permute-start | bytes 393224 | tf_op jit(solution)/shard_map/ppermute | solution.py:630
  6.2 1.3 collective-permute-start.1
  7.5 5.0 %moments.1 = (f32[2,32,8,128]{3,2,1,0:T(8,128)}, f32[2,32,128]{2,1,0:T(8,128)}) custom-call(f32[32,128]{1,0:T(8,128)} %refs_0_.1, f32[32,256,128]{2,1,0:T(8,128)} %refs_6_.1), custom_call_target="tpu_custom_call" | custom-call | flops 4194304 | bytes 4194304 | tf_op jit(solution)/shard_map/moments/pallas_call | solution.py:113
  12.5 4.7 %collective-permute-start.4 = (f32[2,32,128]{2,1,0:T(8,128)}, f32[2,32,128]{2,1,0:T(8,128)S(1)}, u32[]{:S(2)}, u32[]{:S(2)}) collective-permute-start(f32[2,32,128]{2,1,0:T(8,128)} %get-tuple-element.25.after_ref.refs_1_), channel_id=1, source_target_pairs={{0,3},{1,0},{2,1},{3,2},{4,7},{5,4},{6,5},{7,6},{8,11},{9,8},{10,9... | collective-permute-start | bytes 98312 | tf_op jit(solution)/shard_map/ppermute | solution.py:638
  17.2 0.0 collective-permute-start.3
  17.2 1.0 collective-permute-start.2
  18.2 0.0 collective-permute-done.lo_ref
  18.2 0.0 copy-start.3
  18.2 0.0 collective-permute-done.1.hi_ref
  18.2 0.7 copy-done.3
  18.8 0.0 copy-start.4
  18.8 0.7 copy-done.4
  19.5 12.4 %pack_edges.1 = (f32[2,264,128]{2,1,0:T(8,128)}, f32[2,264,128]{2,1,0:T(8,128)}, f32[2,264,128]{2,1,0:T(8,128)}) custom-call(f32[2,32,256,128]{3,2,1,0:T(8,128)} %v_ref.3, f32[2,32,256,128]{3,2,1,0:T(8,128)} %f_ref.5, s32[32,256,128]{2,1,0:T(8,128)} %p_ref.3, f32[32,8,128]{2,1,0:T(8,128)} %copy-done.3, f32[32,8,128]{2,1,0:T(8,128)} %copy-done.4, ...), custom_call_target="tpu_custom_call" | custom-call | flops 5242880 | bytes 20971520 | tf_op jit(solution)/shard_map/pack_edges/pallas_call | solution.py:224
  31.8 0.0 collective-permute-done.4.refs_4_
  31.9 0.0 copy-start.5
  31.9 0.0 collective-permute-done.3.refs_3_
  31.9 0.0 copy-start.6
  31.9 0.0 collective-permute-done.2.refs_2_
  31.9 0.0 copy-start.7
  31.9 1.9 %collective-permute-start.5 = (f32[2,264,128]{2,1,0:T(8,128)}, f32[2,264,128]{2,1,0:T(8,128)S(1)}, u32[]{:S(2)}, u32[]{:S(2)}) collective-permute-start(f32[2,264,128]{2,1,0:T(8,128)} %get-tuple-element.33), channel_id=1, source_target_pairs={{0,4},{4,8},{8,12},{12,16},{16,20},{20,24},{24,28},{1,5},{5,9},{9,... | collective-permute-start | bytes 811016 | tf_op jit(solution)/shard_map/ppermute | solution.py:630
  33.8 4.5 %collective-permute-start.6 = (f32[2,264,128]{2,1,0:T(8,128)}, f32[2,264,128]{2,1,0:T(8,128)S(1)}, u32[]{:S(2)}, u32[]{:S(2)}) collective-permute-start(f32[2,264,128]{2,1,0:T(8,128)} %get-tuple-element.34), channel_id=1, source_target_pairs={{4,0},{8,4},{12,8},{16,12},{20,16},{24,20},{28,24},{5,1},{9,5},{13... | collective-permute-start | bytes 811016 | tf_op jit(solution)/shard_map/ppermute | solution.py:630
  38.4 0.0 copy-done.5
  38.4 0.0 copy-done.6
  38.4 0.0 copy-done.7
  38.4 10.4 %heat.1 = (f32[32,256,128]{2,1,0:T(8,128)}, f32[264,128]{1,0:T(8,128)}, f32[2,32,128]{2,1,0:T(8,128)}) custom-call(f32[32,128]{1,0:T(8,128)} %refs_0_.1, f32[2,32,128]{2,1,0:T(8,128)} %get-tuple-element.25.after_ref.refs_1_, f32[2,32,128]{2,1,0:T(8,128)} %copy-done.7, f32[2,32,128]{2,1,0:T(8,128)} %copy-done.6, f32[2,32,128]{2,1,0:T(8,128)} %copy-done.5, ...), custom_call_target="tpu_custom_call" | custom-call | flops 10485760 | bytes 8388608 | tf_op jit(solution)/shard_map/heat/pallas_call | solution.py:340
  48.8 1.9 %collective-permute-start.8 = (f32[264,128]{1,0:T(8,128)}, f32[264,128]{1,0:T(8,128)S(1)}, u32[]{:S(2)}, u32[]{:S(2)}) collective-permute-start(f32[264,128]{1,0:T(8,128)} %get-tuple-element.35), channel_id=1, source_target_pairs={{4,0},{8,4},{12,8},{16,12},{20,16},{24,20},{28,24},{5,1},{9,5},{13... | collective-permute-start | bytes 405512 | tf_op jit(solution)/shard_map/ppermute | solution.py:630
  50.7 2.4 %collective-permute-start.7 = (f32[264,128]{1,0:T(8,128)}, f32[264,128]{1,0:T(8,128)S(1)}, u32[]{:S(2)}, u32[]{:S(2)}) collective-permute-start(f32[264,128]{1,0:T(8,128)} %get-tuple-element.35), channel_id=1, source_target_pairs={{0,4},{4,8},{8,12},{12,16},{16,20},{20,24},{24,28},{1,5},{5,9},{9,... | collective-permute-start | bytes 405512 | tf_op jit(solution)/shard_map/ppermute | solution.py:630
  53.1 0.4 collective-permute-done.8.hr_ref
  53.6 4.6 %collective-permute-done.7.hl_ref = f32[264,128]{1,0:T(8,128)S(1)} collective-permute-done((f32[264,128]{1,0:T(8,128)}, f32[264,128]{1,0:T(8,128)S(1)}, u32[]{:S(2)}, u32[]{:S(2)}) %collective-permute-start.7) | collective-permute-done | bytes 135200 | tf_op jit(solution)/shard_map/ppermute | solution.py:630
  58.2 0.0 collective-permute-done.5.fl_ref
  58.2 0.0 collective-permute-done.6.fr_ref
  58.2 0.0 copy-start.1
  58.2 1.0 copy-done.1
  59.1 1.4 strips.1
  60.5 0.0 copy-start
  60.5 0.7 copy-done
  61.2 0.0 copy-start.2
  61.2 0.7 copy-done.2
  61.9 88.0 %sweeps.1 = f32[2,32,256,128]{3,2,1,0:T(8,128)} custom-call(f32[2,32,256,128]{3,2,1,0:T(8,128)} %v_ref.3, f32[2,32,256,128]{3,2,1,0:T(8,128)} %f_ref.5, s32[32,256,128]{2,1,0:T(8,128)} %p_ref.3, f32[32,256,128]{2,1,0:T(8,128)} %get-tuple-element.18.h_ref, f32[32,8,128]{2,1,0:T(8,128)} %copy-done.3, f32[32,8,128]{2,1,0:T(8,128)} %copy-done.4, ...), custom_call_target="tpu_custom_call" | custom-call | flops 62914560 | bytes 33554432 | tf_op jit(solution)/shard_map/sweeps/pallas_call | solution.py:597
Async XLA Ops:
  2.7 15.5 %collective-permute-start = (f32[32,8,128]{2,1,0:T(8,128)}, f32[32,8,128]{2,1,0:T(8,128)S(1)}, u32[]{:S(2)}, u32[]{:S(2)}) collective-permute-start(f32[32,8,128]{2,1,0:T(8,128)} %get-tuple-element.20), channel_id=1, source_target_pairs={{0,1},{1,2},{2,3},{4,5},{5,6},{6,7},{8,9},{9,10},{10,11},{12,13},{... | collective-permute-start | bytes 393224 | tf_op jit(solution)/shard_map/ppermute | solution.py:630
  6.2 12.0 %collective-permute-start.1 = (f32[32,8,128]{2,1,0:T(8,128)}, f32[32,8,128]{2,1,0:T(8,128)S(1)}, u32[]{:S(2)}, u32[]{:S(2)}) collective-permute-start(f32[32,8,128]{2,1,0:T(8,128)} %get-tuple-element.21), channel_id=1, source_target_pairs={{1,0},{2,1},{3,2},{5,4},{6,5},{7,6},{9,8},{10,9},{11,10},{13,12},{... | collective-permute-start | bytes 393224 | tf_op jit(solution)/shard_map/ppermute | solution.py:630
  12.5 19.4 %collective-permute-start.4 = (f32[2,32,128]{2,1,0:T(8,128)}, f32[2,32,128]{2,1,0:T(8,128)S(1)}, u32[]{:S(2)}, u32[]{:S(2)}) collective-permute-start(f32[2,32,128]{2,1,0:T(8,128)} %get-tuple-element.25.after_ref.refs_1_), channel_id=1, source_target_pairs={{0,3},{1,0},{2,1},{3,2},{4,7},{5,4},{6,5},{7,6},{8,11},{9,8},{10,9... | collective-permute-start | bytes 98312 | tf_op jit(solution)/shard_map/ppermute | solution.py:638
  17.2 14.7 %collective-permute-start.3 = (f32[2,32,128]{2,1,0:T(8,128)}, f32[2,32,128]{2,1,0:T(8,128)S(1)}, u32[]{:S(2)}, u32[]{:S(2)}) collective-permute-start(f32[2,32,128]{2,1,0:T(8,128)} %get-tuple-element.25.after_ref.refs_1_), channel_id=1, source_target_pairs={{0,2},{1,3},{2,0},{3,1},{4,6},{5,7},{6,4},{7,5},{8,10},{9,11},{10,... | collective-permute-start | bytes 98312 | tf_op jit(solution)/shard_map/ppermute | solution.py:638
  17.2 14.7 %collective-permute-start.2 = (f32[2,32,128]{2,1,0:T(8,128)}, f32[2,32,128]{2,1,0:T(8,128)S(1)}, u32[]{:S(2)}, u32[]{:S(2)}) collective-permute-start(f32[2,32,128]{2,1,0:T(8,128)} %get-tuple-element.25.after_ref.refs_1_), channel_id=1, source_target_pairs={{0,1},{1,2},{2,3},{3,0},{4,5},{5,6},{6,7},{7,4},{8,9},{9,10},{10,1... | collective-permute-start | bytes 98312 | tf_op jit(solution)/shard_map/ppermute | solution.py:638
  18.2 0.7 copy-start.3
  18.8 0.7 copy-start.4
  31.9 6.5 %copy-start.5 = (f32[2,32,128]{2,1,0:T(8,128)}, f32[2,32,128]{2,1,0:T(8,128)S(1)}, u32[]{:S(2)}) copy-start(f32[2,32,128]{2,1,0:T(8,128)S(1)} %collective-permute-done.4.refs_4_) | copy-start | bytes 98308
  31.9 6.5 %copy-start.6 = (f32[2,32,128]{2,1,0:T(8,128)}, f32[2,32,128]{2,1,0:T(8,128)S(1)}, u32[]{:S(2)}) copy-start(f32[2,32,128]{2,1,0:T(8,128)S(1)} %collective-permute-done.3.refs_3_) | copy-start | bytes 98308
  31.9 6.5 %copy-start.7 = (f32[2,32,128]{2,1,0:T(8,128)}, f32[2,32,128]{2,1,0:T(8,128)S(1)}, u32[]{:S(2)}) copy-start(f32[2,32,128]{2,1,0:T(8,128)S(1)} %collective-permute-done.2.refs_2_) | copy-start | bytes 98308
  31.9 26.3 %collective-permute-start.5 = (f32[2,264,128]{2,1,0:T(8,128)}, f32[2,264,128]{2,1,0:T(8,128)S(1)}, u32[]{:S(2)}, u32[]{:S(2)}) collective-permute-start(f32[2,264,128]{2,1,0:T(8,128)} %get-tuple-element.33), channel_id=1, source_target_pairs={{0,4},{4,8},{8,12},{12,16},{16,20},{20,24},{24,28},{1,5},{5,9},{9,... | collective-permute-start | bytes 811016 | tf_op jit(solution)/shard_map/ppermute | solution.py:630
  33.8 24.4 %collective-permute-start.6 = (f32[2,264,128]{2,1,0:T(8,128)}, f32[2,264,128]{2,1,0:T(8,128)S(1)}, u32[]{:S(2)}, u32[]{:S(2)}) collective-permute-start(f32[2,264,128]{2,1,0:T(8,128)} %get-tuple-element.34), channel_id=1, source_target_pairs={{4,0},{8,4},{12,8},{16,12},{20,16},{24,20},{28,24},{5,1},{9,5},{13... | collective-permute-start | bytes 811016 | tf_op jit(solution)/shard_map/ppermute | solution.py:630
  48.8 4.8 %collective-permute-start.8 = (f32[264,128]{1,0:T(8,128)}, f32[264,128]{1,0:T(8,128)S(1)}, u32[]{:S(2)}, u32[]{:S(2)}) collective-permute-start(f32[264,128]{1,0:T(8,128)} %get-tuple-element.35), channel_id=1, source_target_pairs={{4,0},{8,4},{12,8},{16,12},{20,16},{24,20},{28,24},{5,1},{9,5},{13... | collective-permute-start | bytes 405512 | tf_op jit(solution)/shard_map/ppermute | solution.py:630
  50.7 7.4 %collective-permute-start.7 = (f32[264,128]{1,0:T(8,128)}, f32[264,128]{1,0:T(8,128)S(1)}, u32[]{:S(2)}, u32[]{:S(2)}) collective-permute-start(f32[264,128]{1,0:T(8,128)} %get-tuple-element.35), channel_id=1, source_target_pairs={{0,4},{4,8},{8,12},{12,16},{16,20},{20,24},{24,28},{1,5},{5,9},{9,... | collective-permute-start | bytes 405512 | tf_op jit(solution)/shard_map/ppermute | solution.py:630
  58.2 1.0 copy-start.1
  60.5 0.7 copy-start
  61.2 0.7 copy-start.2
